TPU v7x, 32 devices: a whole 2x2x4 slice. The times are simulated.
32 devices in a mesh: batch: 4 (over x, core), seq: 8 (over z, y).
Axes of the slice: x: 2, y: 2, z: 4, core: 2. Of those that a mesh axis runs over, the one named last changes fastest.
Arguments:
- block_input: bfloat16 [8, 2048, 2048], P('batch', 'seq'), may hold values from -5.5 to 5.5, as said below
- weight: bfloat16 [2, 2048, 6144], P(None, ('batch', 'seq')), may hold values from -0.125 to 0.125
- vectors: float32 [2, 5, 2048], P(None, None, ('batch', 'seq')), may hold values from -1 to 13, as said below
- cotangent: bfloat16 [8, 2048, 2048], P('batch', 'seq'), may hold values from -5 to 5, as said below
Outputs:
- block_output: bfloat16 [8, 2048, 2048], P('batch', 'seq')
- input_grad: float32 [8, 2048, 2048], P('batch', 'seq')
- weight_grad: float32 [2, 2048, 6144], P(None, ('batch', 'seq'))
- vector_grad: float32 [2, 5, 2048], P(None, None, ('batch', 'seq'))
Inputs may be any that keep to these rules, and one draw needn't show every extreme that they name: `block_input`: each sequence has a feature offset common to all its positions. `cotangent`: each sequence has a feature offset common to all its positions. `vectors`: gains near 1; vf, vr, br of order one; bf positive.
All inputs are finite; a program needn't handle non-finite values.
Results may differ from a plain program's by a relative error of at most 0.0044.
Values may be sent and summed in bfloat16 or wider, within the bound.
A program may use at most 256 MiB of HBM per device.

v0:
```python
import jax
import jax.numpy as jnp
from jax import lax
from jax.sharding import PartitionSpec as P

epsilon = 1e-05


def prefix(value, axis, join, neutral, backward):
    count, mine = (lax.axis_size(axis), lax.axis_index(axis))
    pieces = jax.tree.map(lambda part: lax.all_gather(part, axis), value)
    if backward:
        pieces = jax.tree.map(lambda part: part[::-1], pieces)
        mine = count - 1 - mine
    subtotal = jax.tree.map(
        lambda part, zero: jnp.full_like(part, 0) + jnp.asarray(zero, part.dtype), value, neutral
    )

    def step(position, subtotal):
        longer = join(subtotal, jax.tree.map(lambda part: part[position], pieces))
        return jax.tree.map(lambda new, old: jnp.where(position < mine, new, old), longer, subtotal)

    return lax.fori_loop(0, count - 1, step, subtotal)


def compose(earlier, later):
    return (later[0] * earlier[0], later[0] * earlier[1] + later[1])


def rebuild_forward(stream, full, vec):
    norm_scale, vforget, bforget = (vec[0], vec[1], vec[2])
    sequence_batch, time_steps, hidden_width = stream.shape
    center = jnp.mean(stream, axis=-1, keepdims=True)
    shifted_input = stream - center
    inverse_deviation = lax.rsqrt(
        jnp.mean(shifted_input * shifted_input, axis=-1, keepdims=True) + epsilon
    )
    centered_input = shifted_input * inverse_deviation
    normed_input = (
        (centered_input * norm_scale)
        .astype(jnp.bfloat16)
        .reshape(sequence_batch * time_steps, hidden_width)
    )
    mixed = jnp.dot(normed_input, full, preferred_element_type=jnp.float32).reshape(
        sequence_batch, time_steps, 3 * hidden_width
    )
    candidate_value = mixed[..., :hidden_width]
    reset_input = mixed[..., 2 * hidden_width :]
    forget_gate = jax.nn.sigmoid(
        mixed[..., hidden_width : 2 * hidden_width] + vforget * stream + bforget
    )
    gate_values, norm_bias = lax.associative_scan(
        compose, (forget_gate, (1.0 - forget_gate) * candidate_value), axis=1
    )
    return (
        centered_input,
        inverse_deviation,
        normed_input,
        candidate_value,
        reset_input,
        forget_gate,
        gate_values,
        norm_bias,
    )


def finish(vec, reset_input, gate_values, norm_bias, incoming):
    vreset, breset = (vec[3], vec[4])
    cells = gate_values * incoming[:, None, :] + norm_bias
    previous = jnp.concatenate([incoming[:, None, :], cells[:, :-1]], axis=1)
    reset = jax.nn.sigmoid(reset_input + vreset * previous + breset)
    return (cells, previous, reset)


def body(block_input, weight, vectors, cotangent):
    sequence_batch, time_steps, hidden_width = block_input.shape
    layers = weight.shape[0]
    params = lax.all_gather(vectors, ("batch", "seq"), axis=2, tiled=True)
    stream = block_input.astype(jnp.float32)
    ones = jnp.ones((sequence_batch, hidden_width), jnp.float32)
    zeros = jnp.zeros((sequence_batch, hidden_width), jnp.float32)
    inputs = []
    entering = []
    for layer in range(layers):
        full = lax.all_gather(weight[layer], ("batch", "seq"), axis=0, tiled=True)
        vec = params[layer]
        pieces = rebuild_forward(stream, full, vec)
        gate_values, norm_bias = (pieces[6], pieces[7])
        arrived = prefix(
            (gate_values[:, -1], norm_bias[:, -1]), "seq", compose, (ones, zeros), False
        )
        incoming = arrived[1]
        cells, previous, reset = finish(vec, pieces[4], gate_values, norm_bias, incoming)
        inputs.append(stream)
        entering.append(incoming)
        stream = reset * cells + (1.0 - reset) * stream
    block_output = stream.astype(jnp.bfloat16)
    grad_out = cotangent.astype(jnp.float32)
    weight_grads = [None] * layers
    vector_terms = [None] * layers
    rows = weight.shape[1]
    for layer in reversed(range(layers)):
        full = lax.all_gather(weight[layer], ("batch", "seq"), axis=0, tiled=True)
        vec = params[layer]
        norm_scale, vforget, vreset = (vec[0], vec[1], vec[3])
        stream = inputs[layer]
        (
            centered_input,
            inverse_deviation,
            normed_input,
            candidate_value,
            reset_input,
            forget_gate,
            gate_values,
            norm_bias,
        ) = rebuild_forward(stream, full, vec)
        cells, previous, reset = finish(vec, reset_input, gate_values, norm_bias, entering[layer])
        dreset = grad_out * (cells - stream) * reset * (1.0 - reset)
        direct = grad_out * reset
        inject = forget_gate * direct + dreset * vreset
        back_gates, back_offsets = lax.associative_scan(
            compose, (jnp.flip(forget_gate, 1), jnp.flip(inject, 1)), axis=1
        )
        back_gates = jnp.flip(back_gates, 1)
        back_offsets = jnp.flip(back_offsets, 1)
        arrived = prefix(
            (back_gates[:, 0], back_offsets[:, 0]), "seq", compose, (ones, zeros), True
        )
        later = arrived[1]
        carried = back_gates * later[:, None, :] + back_offsets
        following = jnp.concatenate([carried[:, 1:], later[:, None, :]], axis=1)
        dcell = direct + following
        dcandidate = dcell * (1.0 - forget_gate)
        dforget = dcell * (previous - candidate_value) * forget_gate * (1.0 - forget_gate)
        dmixed = jnp.concatenate([dcandidate, dforget, dreset], axis=-1).astype(jnp.bfloat16)
        dmixed = dmixed.reshape(sequence_batch * time_steps, 3 * hidden_width)

        def weight_term(start, count, normed_input=normed_input, dmixed=dmixed):
            return lax.dot_general(
                normed_input, dmixed, (((0,), (0,)), ((), ())), preferred_element_type=jnp.float32
            )

        weight_grads[layer] = lax.psum_scatter(
            weight_term(jnp.int32(0), rows * lax.axis_size(("batch", "seq"))),
            ("batch", "seq"),
            scatter_dimension=0,
            tiled=True,
        )
        normed_gradient = lax.dot_general(
            dmixed, full, (((1,), (1,)), ((), ())), preferred_element_type=jnp.float32
        )
        normed_gradient = normed_gradient.reshape(sequence_batch, time_steps, hidden_width)
        vector_terms[layer] = jnp.stack(
            [
                jnp.sum(normed_gradient * centered_input, axis=(0, 1)),
                jnp.sum(dforget * stream, axis=(0, 1)),
                jnp.sum(dforget, axis=(0, 1)),
                jnp.sum(dreset * previous, axis=(0, 1)),
                jnp.sum(dreset, axis=(0, 1)),
            ],
            axis=0,
        )
        centered_gradient = normed_gradient * norm_scale
        through_norm = inverse_deviation * (
            centered_gradient
            - jnp.mean(centered_gradient, axis=-1, keepdims=True)
            - centered_input * jnp.mean(centered_gradient * centered_input, axis=-1, keepdims=True)
        )
        grad_out = grad_out * (1.0 - reset) + dforget * vforget + through_norm
    weight_grad = jnp.stack(weight_grads, axis=0)
    vector_grad = lax.psum_scatter(
        jnp.stack(vector_terms, axis=0), ("batch", "seq"), scatter_dimension=2, tiled=True
    )
    return (block_output, grad_out, weight_grad, vector_grad)


def solution(mesh):
    placed = (
        P("batch", "seq", None),
        P(None, ("batch", "seq"), None),
        P(None, None, ("batch", "seq")),
        P("batch", "seq", None),
    )
    return jax.shard_map(
        body,
        mesh=mesh,
        in_specs=placed,
        out_specs=(
            P("batch", "seq", None),
            P("batch", "seq", None),
            P(None, ("batch", "seq"), None),
            P(None, None, ("batch", "seq")),
        ),
        check_vma=False,
    )
```

profile of v0, /device:TPU:11, one launch (start us, length us, event | category | flops | bytes accessed | tf_op | source)
XLA Modules:
  0.0 2916.2 jit_solution(7193995087033313333)
XLA Ops:
  11.0 90.2 %all_gather.35 = f32[2,5,2048]{1,0,2:T(2,128)S(1)} all-gather(f32[2,5,64]{1,0,2:T(2,128)S(1)} %copy.17), channel_id=1, replica_groups=mesh['batch'=4,'seq'=8] {'batch','seq'}, dimensions={2}, use_global_device_ids=true | all-gather | bytes 84480 | tf_op jit(solution)/shard_map/all_gather | solution.py:78
  102.3 71.8 %slice_reduce_fusion.3 = (f32[2048]{0:T(1024)}, f32[2048]{0:T(1024)}, f32[2048]{0:T(1024)S(1)}, f32[2048]{0:T(1024)S(1)}, f32[2048]{0:T(1024)S(1)}, /*index=5*/f...) fusion(f32[2,5,2048]{1,0,2:T(2,128)S(1)} %all_gather.35), kind=kLoop, calls=%fused_computation.145 | loop fusion | bytes 163840 | tf_op jit(solution)/shard_map/slice | solution.py:68
  180.8 21.2 fusion.10
  229.4 10.1 slice.1244
  245.7 10.1 slice.1318
  343.1 32.7 %reverse.21 = f32[2,256,2048]{2,1,0:T(8,128)} reverse(f32[2,256,2048]{2,1,0:T(8,128)} %get-tuple-element.554), dimensions={1} | reverse | bytes 8388608 | tf_op jit(solution)/shard_map/reverse.9
  495.5 10.1 pad.470
  505.6 10.1 pad.471
  516.7 23.0 all-gather.1
  540.1 10.3 pad.487
  551.4 24.3 all-gather.2
  595.1 22.3 fusion.6
  660.8 10.1 slice.1404
  786.0 10.2 pad.503
  797.3 24.5 all-gather.4
  829.4 23.9 all-gather.5
  854.6 10.2 multiply_add_fusion.2
  864.8 32.6 %reverse.20 = f32[2,256,2048]{2,1,0:T(8,128)} reverse(f32[2,256,2048]{2,1,0:T(8,128)} %get-tuple-element.549), dimensions={1} | reverse | bytes 8388608 | tf_op jit(solution)/shard_map/reverse.1
  981.6 16.6 slice.1448
  998.3 16.7 slice.1450
  1082.1 16.7 slice.1485
  1170.0 10.1 pad.550
  1180.1 10.2 pad.551
  1209.6 10.2 pad.535
  1227.4 32.6 %rev.37 = f32[2,256,2048]{2,1,0:T(8,128)} reverse(f32[2,256,2048]{2,1,0:T(8,128)} %add.1088), dimensions={1} | reverse | bytes 8388608 | tf_op jit(solution)/shard_map/jit(_flip)/rev | solution.py:125
  1260.0 24.1 all-gather.7
  1284.5 32.7 %rev.34 = f32[2,256,2048]{2,1,0:T(8,128)} reverse(f32[2,256,2048]{2,1,0:T(8,128)} %add.1064), dimensions={1} | reverse | bytes 8388608 | tf_op jit(solution)/shard_map/jit(_flip)/rev | solution.py:124
  1317.2 24.1 all-gather.6
  1356.5 25.2 fusion.100
  1381.8 18.3 fusion.97
  1400.1 13.8 multiply_add_fusion
  1444.2 16.7 slice.1528
  1460.9 16.6 slice.1530
  1543.9 16.8 slice.1565
  1631.5 10.1 pad.582
  1641.6 10.1 pad.583
  1660.9 10.1 pad.566
  1671.0 10.1 pad.567
  1688.7 32.7 %rev.42 = f32[2,256,2048]{2,1,0:T(8,128)} reverse(f32[2,256,2048]{2,1,0:T(8,128)} %add.1125), dimensions={1} | reverse | bytes 8388608 | tf_op jit(solution)/shard_map/jit(_flip)/rev | solution.py:125
  1721.4 24.1 all-gather.9
  1746.0 32.6 %rev.39 = f32[2,256,2048]{2,1,0:T(8,128)} reverse(f32[2,256,2048]{2,1,0:T(8,128)} %add.1101), dimensions={1} | reverse | bytes 8388608 | tf_op jit(solution)/shard_map/jit(_flip)/rev | solution.py:124
  1778.6 24.1 all-gather.8
  1818.0 23.3 fusion.98
  1847.2 25.2 convolution_bitcast_fusion
  1872.4 24.4 convolution_bitcast_fusion.1
  1906.5 117.1 %reduce-scatter.10.cloned.1.call-done = f32[64,10]{1,0:T(8,128)} async-done(((f32[2048,10]{1,0:T(8,128)}), f32[64,10]{1,0:T(8,128)}) %reduce-scatter.10.cloned.1.call-update) | async-done | bytes 2576
  2025.1 442.3 %reduce-scatter.8.cloned.1.call-done = f32[64,6144]{1,0:T(8,128)} async-done(((f32[2048,6144]{1,0:T(8,128)}), f32[64,6144]{1,0:T(8,128)}) %reduce-scatter.8.cloned.1.call-update) | async-done | bytes 1572880 | tf_op jit(solution)/shard_map/reduce_scatter | solution.py:143
  2467.4 438.0 %reduce-scatter.6.cloned.1.call-done = f32[64,6144]{1,0:T(8,128)} async-done(((f32[2048,6144]{1,0:T(8,128)}), f32[64,6144]{1,0:T(8,128)}) %reduce-scatter.6.cloned.1.call-update) | async-done | bytes 1572880 | tf_op jit(solution)/shard_map/reduce_scatter | solution.py:143
  (822 shorter events, 926.4 us)
Async XLA Ops:
  7.2 94.0 %copy-start.8 = (bf16[2,256,2048]{2,1,0:T(8,128)(2,1)S(1)}, bf16[2,256,2048]{2,1,0:T(8,128)(2,1)}, u32[]{:S(2)}) copy-start(bf16[2,256,2048]{2,1,0:T(8,128)(2,1)} %param.12) | copy-start | bytes 6291460
  7.2 173.6 %all-gather.13.cloned.1.call-start = ((), (), s32[]{:S(2)}) async-start(), calls=%async_computation.5 | async-start | bytes 25952256 | tf_op jit(solution)/shard_map/all_gather | solution.py:85
  10.0 585.0 %all-gather.15.cloned.1.call-start = ((), (), s32[]{:S(2)}) async-start(), calls=%async_computation.6 | async-start | bytes 25952256 | tf_op jit(solution)/shard_map/all_gather | solution.py:85
  10.8 2012.8 %reduce-scatter.10.cloned.1.call-start = ((), (), s32[]{:S(2)}) async-start(), calls=%async_computation.7 | async-start | bytes 1081344
  101.6 79.2 %copy-start.84 = (f32[2,256]{1,0:T(2,128)}, f32[2,256]{1,0:T(2,128)S(1)}, u32[]{:S(2)}) copy-start(f32[2,256]{1,0:T(2,128)S(1)} %broadcast_multiply_fusion.5) | copy-start | bytes 6148
  102.3 78.5 %copy-start.88 = (f32[2,256]{1,0:T(2,128)}, f32[2,256]{1,0:T(2,128)S(1)}, u32[]{:S(2)}) copy-start(f32[2,256]{1,0:T(2,128)S(1)} %add_rsqrt_fusion.1) | copy-start | bytes 6148
  174.1 27.9 copy-start.77
  174.1 27.9 copy-start.96
  174.1 410.4 %copy-start.94 = (f32[2048]{0:T(1024)}, f32[2048]{0:T(1024)S(1)}, u32[]{:S(2)}) copy-start(f32[2048]{0:T(1024)S(1)} %get-tuple-element.496) | copy-start | bytes 24580
  174.1 421.0 %copy-start.79 = (f32[2048]{0:T(1024)}, f32[2048]{0:T(1024)S(1)}, u32[]{:S(2)}) copy-start(f32[2048]{0:T(1024)S(1)} %get-tuple-element.492) | copy-start | bytes 24580
  174.1 443.3 %copy-start.99 = (f32[2048]{0:T(1024)}, f32[2048]{0:T(1024)S(1)}, u32[]{:S(2)}) copy-start(f32[2048]{0:T(1024)S(1)} %get-tuple-element.491) | copy-start | bytes 24580
  453.4 13.1 copy-start.63
  576.6 7.8 copy-start.92
  576.6 7.8 copy-start.104
  584.4 7.9 copy-start
  592.3 25.1 copy-start.86
  595.0 22.4 copy-start.90
  595.1 22.3 copy-start.3
  745.1 13.1 copy-start.64
  786.0 36.2 %copy-start.49 = (f32[2,128,2048]{2,1,0:T(8,128)S(1)}, f32[2,128,2048]{2,1,0:T(8,128)}, u32[]{:S(2)}) copy-start(f32[2,128,2048]{2,1,0:T(8,128)} %add.1046) | copy-start | bytes 6291460
  796.3 57.5 %copy-start.83 = (f32[2,2048]{1,0:T(2,128)S(1)}, f32[2,2048]{1,0:T(2,128)}, u32[]{:S(2)}) copy-start(f32[2,2048]{1,0:T(2,128)} %custom-call.1) | copy-start | bytes 49156
  912.0 20.0 copy-start.12
  912.0 20.0 copy-start.98
  912.0 20.0 copy-start.103
  932.0 9.7 copy-start.4
  941.7 9.5 copy-start.10
  1141.0 13.1 copy-start.65
  1284.5 57.2 %copy-start.82 = (f32[2,2048]{1,0:T(2,128)S(1)}, f32[2,2048]{1,0:T(2,128)}, u32[]{:S(2)}) copy-start(f32[2,2048]{1,0:T(2,128)} %custom-call.2) | copy-start | bytes 49156
  1342.4 7.1 copy-start.11
  1349.5 7.0 copy-start.80
  1349.5 7.0 copy-start.87
  1349.5 7.0 copy-start.91
  1356.5 25.3 copy-start.9
  1356.5 25.3 copy-start.93
  1356.5 25.3 copy-start.100
  1381.8 18.3 copy-start.95
  1602.5 13.2 copy-start.66
  1746.0 57.2 %copy-start.81 = (f32[2,2048]{1,0:T(2,128)S(1)}, f32[2,2048]{1,0:T(2,128)}, u32[]{:S(2)}) copy-start(f32[2,2048]{1,0:T(2,128)} %custom-call.3) | copy-start | bytes 49156
  1803.8 7.1 copy-start.34
  1810.9 7.0 copy-start.110
  1810.9 7.0 copy-start.111
  1810.9 7.1 copy-start.78
  1810.9 7.1 copy-start.85
  1810.9 7.1 copy-start.89
  1818.0 23.3 copy-start.107
  1818.0 23.3 copy-start.108
  1847.1 620.3 %reduce-scatter.8.cloned.1.call-start = ((), (), s32[]{:S(2)}) async-start(), calls=%async_computation.4 | async-start | bytes 51904512 | tf_op jit(solution)/shard_map/reduce_scatter | solution.py:143
  1872.4 1033.0 %reduce-scatter.6.cloned.1.call-start = ((), (), s32[]{:S(2)}) async-start(), calls=%async_computation.3 | async-start | bytes 51904512 | tf_op jit(solution)/shard_map/reduce_scatter | solution.py:143
  (70 other events, 272.7 us)
Sparse Core Ops, SparseCore 0:
  11.5 169.2 all-gather.12
  183.7 152.3 all-gather.14
  1847.2 176.2 reduce-scatter.9
  2031.0 436.3 reduce-scatter.7
  2474.8 430.5 reduce-scatter.5
where the time goes:
time: 2960 us; the launch traced here: 2920 us
  local copies, waits for them, and re-layouts  1120 us (38%)
  waiting for transfers between devices  1000 us (34%)
  other arithmetic  351 us (12%)
  blocking collectives  283 us (10%)
  matrix products  142 us (5%)
    reduce_scatter x2, waiting for transfers between devices, body(): lax.psum_scatter(weight_term(jnp.int32(0), rows * lax.axis_size(('batch',...  880 us
    slice x110, local copies, waits for them, and re-layouts, body(): lax.associative_scan(compose, (jnp.flip(forget_gate, 1), jnp.flip(inject,...  327 us
    slice x104, local copies, waits for them, and re-layouts, rebuild_forward(): lax.associative_scan(compose, (forget_gate, (1.0 - forget_gate) * candida...  203 us
    all_gather x8, blocking collectives, prefix(): pieces = jax.tree.map(lambda part: lax.all_gather(part, axis), value)  192 us
    pad x56, local copies, waits for them, and re-layouts, body(): lax.associative_scan(compose, (jnp.flip(forget_gate, 1), jnp.flip(inject,...  149 us
    pad x56, local copies, waits for them, and re-layouts, rebuild_forward(): lax.associative_scan(compose, (forget_gate, (1.0 - forget_gate) * candida...  124 us
    unnamed x6, waiting for transfers between devices  118 us
    all_gather x1, blocking collectives, body(): params = lax.all_gather(vectors, ('batch', 'seq'), axis=2, tiled=True)  90.2 us
  transfers between devices with their start and end apart: 5, of which 4 were waited for; matrix products, arithmetic and copies ran while one was open for 17% of the time, Pallas kernels for 0%

commit v1 on v0

--- a/solution.py
+++ b/solution.py
@@ -1,9 +1,389 @@
+import functools
 import jax
 import jax.numpy as jnp
 from jax import lax
+from jax.experimental import pallas as pl
+from jax.experimental.pallas import tpu as pltpu
 from jax.sharding import PartitionSpec as P
 
+MESH = pl.DeviceIdType.MESH
+F32, BF16 = jnp.float32, jnp.bfloat16
 epsilon = 1e-05
+F = 128
+ANY = pl.BlockSpec(memory_space=pl.ANY)
+VM = pl.BlockSpec(memory_space=pltpu.VMEM)
+
+
+def remote(src, dst, ssem, rsem, dev):
+    return pltpu.make_async_remote_copy(
+        src_ref=src, dst_ref=dst, send_sem=ssem, recv_sem=rsem, device_id=dev, device_id_type=MESH
+    )
+
+
+def arrived(dst, rsem, dev):
+    remote(dst, dst, rsem, rsem, dev).wait_recv()
+
+
+def sent(src, ssem, dev):
+    remote(src, src, ssem, ssem, dev).wait_send()
+
+
+def sigmoid(v):
+    return 1.0 / (1.0 + jnp.exp(jnp.minimum(-v, 80.0)))
+
+
+def seq_rows(t, nseq, steps):
+    return pl.ds(t, nseq, stride=steps)
+
+
+def greet(b, s, nb, ns):
+    barrier = pltpu.get_barrier_semaphore()
+    for j in range(1, nb):
+        pl.semaphore_signal(barrier, inc=1, device_id=(lax.rem(b + j, nb), s), device_id_type=MESH)
+    for j in range(1, ns):
+        pl.semaphore_signal(barrier, inc=1, device_id=(b, lax.rem(s + j, ns)), device_id_type=MESH)
+    pl.semaphore_wait(barrier, nb - 1 + ns - 1)
+
+
+class Dims:
+    def __init__(self, nb, ns, x_shape, w_shape):
+        self.nb, self.ns = nb, ns
+        self.inner = 2 if ns == 8 else 8
+        self.outer = ns // self.inner
+        self.sb, self.steps, self.d = x_shape
+        self.local = self.sb * self.steps
+        self.nseq = self.sb * nb
+        self.tok = self.local * nb
+        self.q = self.d // nb
+        self.nf = self.q // F
+        self.layers, self.rows = w_shape[0], w_shape[1]
+
+
+def layer_norm_rows(x, gain):
+    mu = jnp.mean(x, axis=-1, keepdims=True)
+    xc = x - mu
+    rstd = lax.rsqrt(jnp.mean(xc * xc, axis=-1, keepdims=True) + epsilon)
+    return mu, rstd, xc * rstd * gain
+
+
+def forward_one(
+    dm, x_in, w_in, vec_in, cot_in,
+    normed_out, wq0_out, wq1_out, cot_out, x1g_out, x1_out, xo_out, f_out, c_out, r_out, cell_out, inc_out, vec_out,
+    xg, normed, wq0, vecg, vecf, xo, fS, cS, rS, cellS, x1S, x1b, tot, incS, totS,
+    pre_s, pre_r, z_s, z_r, y_s, y_r, vp_s, vp_r, vz_s, vz_r, vy_s, vy_r,
+    xx_s, xx_r, xc_s, xc_r, xl_s, xl_r, cot_s, cot_r, t_s, t_r, h_s, h_r, hc_s, hc_r, hl_s, hl_r, loc,
+):
+    nb, ns, nf, inner, outer = dm.nb, dm.ns, dm.nf, dm.inner, dm.outer
+    R = dm.rows
+    b, s = lax.axis_index("batch"), lax.axis_index("seq")
+    z, y = s // inner, lax.rem(s, inner)
+    across, sib, diag = b ^ 2, b ^ 1, b ^ 3
+    greet(b, s, nb, ns)
+    batch_peers = [lax.rem(b + j, nb) for j in range(1, nb)]
+    outer_peers = [lax.rem(z + j, outer) for j in range(1, outer)]
+    inner_peers = [lax.rem(y + j, inner) for j in range(1, inner)]
+    seq_peers = [lax.rem(s + j, ns) for j in range(1, ns)]
+    wq = [wq0, wq1_out]
+
+    def strip(l, fc, pos):
+        return wq[l].at[fc, :, pl.ds(pl.multiple_of(pos * R, R), R)]
+
+    def cell_strip(l, fc, bb, pos):
+        return wq[l].at[fc, bb, pl.ds(pl.multiple_of(pos * R, R), R)]
+
+    own = []
+
+    def local_copy(src, dst, k):
+        c = pltpu.make_async_copy(src, dst, loc.at[k])
+        c.start()
+        return c
+
+    def pre_start(l, fc):
+        for p in batch_peers:
+            remote(w_in.at[l, p, fc], cell_strip(l, fc, b, s), pre_s.at[l, fc, p], pre_r.at[l, fc, b], (p, s)).start()
+
+    vecg[b, s] = vec_in[...]
+    for p in batch_peers:
+        remote(vec_in, vecg.at[b, s], vp_s.at[p], vp_r.at[b], (p, s)).start()
+    locals0 = [local_copy(x_in, xg.at[b], 0)]
+    for l in range(2):
+        for fc in range(nf):
+            locals0.append(local_copy(w_in.at[l, b, fc], cell_strip(l, fc, b, s), 1 + l * nf + fc))
+    for fc in range(nf):
+        pre_start(0, fc)
+    NX = 4
+    XR = dm.local // NX
+    remote(x_in, xg.at[b], xc_s, xc_r, (sib, s)).start()
+
+    def x_send(k):
+        rows = pl.ds(k * XR, XR)
+        return remote(x_in.at[rows], xg.at[b, rows], xx_s.at[k], xx_r.at[k], (across, s))
+
+    def x_relay(k):
+        rows = pl.ds(k * XR, XR)
+        return remote(xg.at[across, rows], xg.at[across, rows], xl_s.at[k], xl_r.at[k], (sib, s))
+
+    for k in range(NX):
+        x_send(k).start()
+    for fc in range(nf):
+        pre_start(1, fc)
+    for p in batch_peers:
+        cols = pl.ds(pl.multiple_of(p * dm.q, F), dm.q)
+        remote(cot_in.at[:, cols], cot_out.at[b], cot_s.at[p], cot_r.at[b], (p, s)).start()
+    locals0.append(local_copy(cot_in.at[:, pl.ds(pl.multiple_of(b * dm.q, F), dm.q)], cot_out.at[b], 1 + 2 * nf))
+
+    for p in batch_peers:
+        arrived(vecg.at[p, s], vp_r.at[p], (p, s))
+    for p in outer_peers:
+        remote(vecg.at[:, s], vecg.at[:, s], vz_s.at[p], vz_r.at[z], (b, p * inner + y)).start()
+    for c in locals0:
+        c.wait()
+
+    def z_start(l, fc):
+        for p in batch_peers:
+            arrived(cell_strip(l, fc, p, s), pre_r.at[l, fc, p], (p, s))
+        for p in outer_peers:
+            remote(strip(l, fc, s), strip(l, fc, s), z_s.at[l, fc, p], z_r.at[l, fc, z], (b, p * inner + y)).start()
+        for p in inner_peers:
+            remote(strip(l, fc, s), strip(l, fc, s), y_s.at[l, fc, z, p], y_r.at[l, fc, z, y], (b, z * inner + p)).start()
+
+    def z_forward(l, fc):
+        for o in outer_peers:
+            arrived(strip(l, fc, o * inner + y), z_r.at[l, fc, o], (b, o * inner + y))
+            for p in inner_peers:
+                remote(
+                    strip(l, fc, o * inner + y), strip(l, fc, o * inner + y),
+                    y_s.at[l, fc, o, p], y_r.at[l, fc, o, y], (b, z * inner + p),
+                ).start()
+
+    def y_wait(l, fc):
+        for o in range(outer):
+            for p in inner_peers:
+                arrived(strip(l, fc, o * inner + p), y_r.at[l, fc, o, p], (b, z * inner + p))
+
+    z_start(0, 0)
+    for p in outer_peers:
+        arrived(vecg.at[:, p * inner + y], vz_r.at[p], (b, p * inner + y))
+    for o in range(outer):
+        for p in inner_peers:
+            at = vecg.at[:, o * inner + y]
+            remote(at, at, vy_s.at[o, p], vy_r.at[o, y], (b, z * inner + p)).start()
+    for fc in range(1, nf):
+        z_start(0, fc)
+    for o in range(outer):
+        for p in inner_peers:
+            arrived(vecg.at[:, o * inner + p], vy_r.at[o, p], (b, z * inner + p))
+    per = F // R
+    for k in range(dm.d // F):
+        bb, s0 = (k * per) // ns, (k * per) % ns
+        total = vecg[bb, s0]
+        for j in range(1, per):
+            total = total + vecg[bb, s0 + j]
+        vecf[:, k * F : (k + 1) * F] = total
+    vec_out[...] = vecf[...]
+
+    TILE = 32
+
+    def norm_block(bb):
+        gain = vecf[0:1, :]
+
+        def step(i, carry):
+            rows = pl.ds(pl.multiple_of(i * TILE, TILE), TILE)
+            x = xg[bb, rows, :].astype(F32)
+            _, _, n = layer_norm_rows(x, gain)
+            all_rows = pl.ds(pl.multiple_of(bb * dm.local + i * TILE, TILE), TILE)
+            normed[all_rows, :] = n.astype(BF16)
+            for fc in range(nf):
+                cols = pl.ds(pl.multiple_of(b * dm.q + fc * F, F), F)
+                xo[fc, all_rows, :] = xg[bb, rows, cols].astype(F32)
+            return carry
+
+        lax.fori_loop(0, dm.local // TILE, step, 0)
+
+    norm_block(b)
+    arrived(xg.at[sib], xc_r, (sib, s))
+    norm_block(sib)
+    for k in range(NX):
+        arrived(xg.at[across, pl.ds(k * XR, XR)], xx_r.at[k], (across, s))
+        x_relay(k).start()
+        if k == 1:
+            z_forward(0, 0)
+    norm_block(across)
+    for k in range(NX):
+        arrived(xg.at[diag, pl.ds(k * XR, XR)], xl_r.at[k], (sib, s))
+    norm_block(diag)
+    normed_copy = local_copy(normed, normed_out, 0)
+
+    def vrow(k, fc):
+        return vecf[k : k + 1, pl.ds(pl.multiple_of(b * dm.q + fc * F, F), F)]
+
+    def p1(fc):
+        y_wait(0, fc)
+        vf, bf, br = vrow(1, fc), vrow(2, fc), vrow(4, fc)
+
+        def seq_step(i, carry):
+            rows = pl.ds(pl.multiple_of(i * dm.steps, dm.steps), dm.steps)
+            m = jnp.dot(normed[rows, :], wq0[fc].reshape(dm.d, 3 * F), preferred_element_type=F32)
+            fS[fc, rows, :] = sigmoid(m[:, F : 2 * F] + vf * xo[fc, rows, :] + bf)
+            cS[fc, rows, :] = m[:, :F]
+            rS[fc, rows, :] = m[:, 2 * F :] + br
+            return carry
+
+        lax.fori_loop(0, dm.nseq, seq_step, 0)
+
+        def scan_step(t, carry):
+            a, v = carry
+            at = seq_rows(t, dm.nseq, dm.steps)
+            f, cand = fS[fc, at, :], cS[fc, at, :]
+            return a * f, cand + f * (v - cand)
+
+        a, v = lax.fori_loop(
+            0, dm.steps, scan_step, (jnp.ones((dm.nseq, F), F32), jnp.zeros((dm.nseq, F), F32)), unroll=8
+        )
+        totS[fc, 0] = a
+        totS[fc, 1] = v
+        tot[fc, s] = totS[fc]
+        for p in seq_peers:
+            remote(totS.at[fc], tot.at[fc, s], t_s.at[fc, p], t_r.at[fc, s], (b, p)).start()
+
+    def p2(fc):
+        for p in seq_peers:
+            arrived(tot.at[fc, p], t_r.at[fc, p], (b, p))
+        vr = vrow(3, fc)
+
+        def fold(j, c):
+            return jnp.where(j < s, tot[fc, j, 0] * c + tot[fc, j, 1], c)
+
+        c0 = lax.fori_loop(0, ns, fold, jnp.zeros((dm.nseq, F), F32))
+        incS[fc] = c0
+
+        def scan_step(t, prev):
+            at = seq_rows(t, dm.nseq, dm.steps)
+            f, cand, x = fS[fc, at, :], cS[fc, at, :], xo[fc, at, :]
+            r = sigmoid(rS[fc, at, :] + vr * prev)
+            c = cand + f * (prev - cand)
+            cellS[fc, at, :] = c
+            rS[fc, at, :] = r
+            x1S[fc, at, :] = x + r * (c - x)
+            return c
+
+        lax.fori_loop(0, dm.steps, scan_step, c0, unroll=8)
+        x1b[fc] = x1S[fc].astype(BF16)
+        remote(x1b.at[fc], x1g_out.at[b, fc], h_s.at[fc], h_r.at[fc], (across, s)).start()
+        remote(x1b.at[fc], x1g_out.at[b, fc], hc_s.at[fc], hc_r.at[fc], (sib, s)).start()
+        cs = [local_copy(x1b.at[fc], x1g_out.at[b, fc], 2 + fc)]
+        for k, (src, dst) in enumerate(
+            [(fS, f_out), (cS, c_out), (rS, r_out), (cellS, cell_out), (x1S, x1_out), (xo, xo_out)]
+        ):
+            cs.append(local_copy(src.at[fc], dst.at[fc], 2 + (k + 1) * nf + fc))
+        return cs
+
+    def h_relay(fc):
+        arrived(x1g_out.at[across, fc], h_r.at[fc], (across, s))
+        remote(x1g_out.at[across, fc], x1g_out.at[across, fc], hl_s.at[fc], hl_r.at[fc], (sib, s)).start()
+
+    pend = []
+    for fc in range(1, nf):
+        z_forward(0, fc)
+        p1(fc - 1)
+        if fc >= 2:
+            pend += p2(fc - 2)
+    for fc in range(nf):
+        z_start(1, fc)
+    p1(nf - 1)
+    pend += p2(nf - 2)
+    pend += p2(nf - 1)
+    wq_copy = local_copy(wq0, wq0_out, 1)
+    for fc in range(nf):
+        z_forward(1, fc)
+        h_relay(fc)
+    inc_out[...] = incS[...]
+    for fc in range(nf):
+        y_wait(1, fc)
+        arrived(x1g_out.at[sib, fc], hc_r.at[fc], (sib, s))
+        arrived(x1g_out.at[diag, fc], hl_r.at[fc], (sib, s))
+    for p in batch_peers:
+        arrived(cot_out.at[p], cot_r.at[p], (p, s))
+    for c in pend:
+        c.wait()
+    normed_copy.wait()
+    wq_copy.wait()
+    for p in batch_peers:
+        sent(vec_in, vp_s.at[p], (p, s))
+        sent(cot_out.at[p], cot_s.at[p], (p, s))
+        for l in range(2):
+            for fc in range(nf):
+                sent(w_in.at[l, p, fc], pre_s.at[l, fc, p], (p, s))
+    for p in outer_peers:
+        sent(vecg.at[:, s], vz_s.at[p], (b, p * inner + y))
+        for l in range(2):
+            for fc in range(nf):
+                sent(strip(l, fc, s), z_s.at[l, fc, p], (b, p * inner + y))
+    for p in inner_peers:
+        for o in range(outer):
+            sent(vecg.at[:, s], vy_s.at[o, p], (b, z * inner + p))
+            for l in range(2):
+                for fc in range(nf):
+                    sent(strip(l, fc, s), y_s.at[l, fc, o, p], (b, z * inner + p))
+    sent(x_in, xc_s, (sib, s))
+    for k in range(NX):
+        x_send(k).wait_send()
+        x_relay(k).wait_send()
+    for fc in range(nf):
+        for p in seq_peers:
+            sent(totS.at[fc], t_s.at[fc, p], (b, p))
+        sent(x1b.at[fc], h_s.at[fc], (across, s))
+        sent(x1b.at[fc], hc_s.at[fc], (sib, s))
+        sent(x1b.at[fc], hl_s.at[fc], (sib, s))
+
+
+def call_forward_one(dm, x, w, vec, cot):
+    nb, ns, nf, inner, outer, R = dm.nb, dm.ns, dm.nf, dm.inner, dm.outer, dm.rows
+    D, q, tok = dm.d, dm.q, dm.tok
+    sd = jax.ShapeDtypeStruct
+    chunk = sd((nf, tok, F), F32)
+    wshape = (nf, nb, ns * R, 3 * F)
+    DMA = pltpu.SemaphoreType.DMA
+    V = pltpu.VMEM
+    out_shape = [
+        sd((tok, D), BF16), sd(wshape, BF16), sd(wshape, BF16), sd((nb, dm.local, q), BF16),
+        sd((nb, nf, tok, F), BF16), chunk, chunk, chunk, chunk, chunk, chunk,
+        sd((nf, dm.nseq, F), F32), sd((16, D), F32),
+    ]
+    chunkV = V((nf, tok, F), F32)
+    L = 2
+    scratch = [
+        V((nb, dm.local, D), BF16), V((tok, D), BF16), V(wshape, BF16), V((nb, ns, 16, F), F32), V((16, D), F32),
+        chunkV, chunkV, chunkV, chunkV, chunkV, chunkV, V((nf, tok, F), BF16),
+        V((nf, ns, 2, dm.nseq, F), F32), V((nf, dm.nseq, F), F32), V((nf, 2, dm.nseq, F), F32),
+        DMA((L, nf, nb)), DMA((L, nf, nb)), DMA((L, nf, outer)), DMA((L, nf, outer)),
+        DMA((L, nf, outer, inner)), DMA((L, nf, outer, inner)),
+        DMA((nb,)), DMA((nb,)), DMA((outer,)), DMA((outer,)), DMA((outer, inner)), DMA((outer, inner)),
+        DMA((4,)), DMA((4,)), DMA, DMA, DMA((4,)), DMA((4,)), DMA((nb,)), DMA((nb,)),
+        DMA((nf, ns)), DMA((nf, ns)), DMA((nf,)), DMA((nf,)), DMA((nf,)), DMA((nf,)), DMA((nf,)), DMA((nf,)),
+        DMA((2 + 8 * nf,)),
+    ]
+    return pl.pallas_call(
+        functools.partial(forward_one, dm),
+        out_shape=out_shape,
+        in_specs=[ANY, ANY, VM, ANY],
+        out_specs=[ANY] * 11 + [VM, VM],
+        scratch_shapes=scratch,
+        compiler_params=pltpu.CompilerParams(collective_id=0, has_side_effects=True, vmem_limit_bytes=62 * 2**20),
+        name="forward_one",
+    )(x, w, vec, cot)
+
+
+def prepare(dm, block_input, weight, vectors, cotangent):
+    D, q, nf, nb, R = dm.d, dm.q, dm.nf, dm.nb, dm.rows
+    x = block_input.reshape(dm.local, D)
+    cot = cotangent.reshape(dm.local, D)
+    w = weight.reshape(dm.layers, R, 3, nb, nf, F).transpose(0, 3, 4, 1, 2, 5).reshape(dm.layers, nb, nf, R, 3 * F)
+    s = lax.axis_index("seq")
+    v = jnp.pad(vectors.reshape(dm.layers * 5, R), ((0, 16 - dm.layers * 5), (0, 0)))
+    lane = lax.broadcasted_iota(jnp.int32, (16, F), 1) // R
+    v = jnp.where(lane == lax.rem(s, F // R), jnp.tile(v, (1, F // R)), 0.0)
+    return x, w, v, cot
 
 
 def prefix(value, axis, join, neutral, backward):
@@ -72,7 +452,7 @@
     return (cells, previous, reset)
 
 
-def body(block_input, weight, vectors, cotangent):
+def general_body(block_input, weight, vectors, cotangent):
     sequence_batch, time_steps, hidden_width = block_input.shape
     layers = weight.shape[0]
     params = lax.all_gather(vectors, ("batch", "seq"), axis=2, tiled=True)
@@ -174,7 +554,121 @@
     return (block_output, grad_out, weight_grad, vector_grad)
 
 
+def tuned_body(nb, ns, block_input, weight, vectors, cotangent):
+    sequence_batch, time_steps, hidden_width = block_input.shape
+    layers = weight.shape[0]
+    params = lax.all_gather(vectors, ("batch", "seq"), axis=2, tiled=True)
+    stream = block_input.astype(jnp.float32)
+    ones = jnp.ones((sequence_batch, hidden_width), jnp.float32)
+    zeros = jnp.zeros((sequence_batch, hidden_width), jnp.float32)
+    inputs = []
+    entering = []
+    dm = Dims(nb, ns, block_input.shape, weight.shape)
+    made = call_forward_one(dm, *prepare(dm, block_input, weight, vectors, cotangent))
+    mine = made[5].reshape(dm.nf, nb, dm.sb, dm.steps, F).transpose(1, 2, 3, 0, 4).reshape(nb, dm.sb, dm.steps, dm.q)
+    mine = lax.all_to_all(mine, "batch", 0, 0, tiled=True)
+    entry = lax.all_gather(made[11], "batch", axis=0)
+    entry = entry.transpose(2, 0, 1, 3).reshape(dm.nseq, dm.d)
+    entry = lax.dynamic_slice_in_dim(entry, lax.axis_index("batch") * dm.sb, dm.sb, 0)
+    inputs.append(stream)
+    entering.append(entry)
+    stream = mine.transpose(1, 2, 0, 3).reshape(stream.shape)
+    for layer in range(1, layers):
+        full = lax.all_gather(weight[layer], ("batch", "seq"), axis=0, tiled=True)
+        vec = params[layer]
+        pieces = rebuild_forward(stream, full, vec)
+        gate_values, norm_bias = (pieces[6], pieces[7])
+        arrived = prefix(
+            (gate_values[:, -1], norm_bias[:, -1]), "seq", compose, (ones, zeros), False
+        )
+        incoming = arrived[1]
+        cells, previous, reset = finish(vec, pieces[4], gate_values, norm_bias, incoming)
+        inputs.append(stream)
+        entering.append(incoming)
+        stream = reset * cells + (1.0 - reset) * stream
+    block_output = stream.astype(jnp.bfloat16)
+    grad_out = cotangent.astype(jnp.float32)
+    weight_grads = [None] * layers
+    vector_terms = [None] * layers
+    rows = weight.shape[1]
+    for layer in reversed(range(layers)):
+        full = lax.all_gather(weight[layer], ("batch", "seq"), axis=0, tiled=True)
+        vec = params[layer]
+        norm_scale, vforget, vreset = (vec[0], vec[1], vec[3])
+        stream = inputs[layer]
+        (
+            centered_input,
+            inverse_deviation,
+            normed_input,
+            candidate_value,
+            reset_input,
+            forget_gate,
+            gate_values,
+            norm_bias,
+        ) = rebuild_forward(stream, full, vec)
+        cells, previous, reset = finish(vec, reset_input, gate_values, norm_bias, entering[layer])
+        dreset = grad_out * (cells - stream) * reset * (1.0 - reset)
+        direct = grad_out * reset
+        inject = forget_gate * direct + dreset * vreset
+        back_gates, back_offsets = lax.associative_scan(
+            compose, (jnp.flip(forget_gate, 1), jnp.flip(inject, 1)), axis=1
+        )
+        back_gates = jnp.flip(back_gates, 1)
+        back_offsets = jnp.flip(back_offsets, 1)
+        arrived = prefix(
+            (back_gates[:, 0], back_offsets[:, 0]), "seq", compose, (ones, zeros), True
+        )
+        later = arrived[1]
+        carried = back_gates * later[:, None, :] + back_offsets
+        following = jnp.concatenate([carried[:, 1:], later[:, None, :]], axis=1)
+        dcell = direct + following
+        dcandidate = dcell * (1.0 - forget_gate)
+        dforget = dcell * (previous - candidate_value) * forget_gate * (1.0 - forget_gate)
+        dmixed = jnp.concatenate([dcandidate, dforget, dreset], axis=-1).astype(jnp.bfloat16)
+        dmixed = dmixed.reshape(sequence_batch * time_steps, 3 * hidden_width)
+
+        def weight_term(start, count, normed_input=normed_input, dmixed=dmixed):
+            return lax.dot_general(
+                normed_input, dmixed, (((0,), (0,)), ((), ())), preferred_element_type=jnp.float32
+            )
+
+        weight_grads[layer] = lax.psum_scatter(
+            weight_term(jnp.int32(0), rows * lax.axis_size(("batch", "seq"))),
+            ("batch", "seq"),
+            scatter_dimension=0,
+            tiled=True,
+        )
+        normed_gradient = lax.dot_general(
+            dmixed, full, (((1,), (1,)), ((), ())), preferred_element_type=jnp.float32
+        )
+        normed_gradient = normed_gradient.reshape(sequence_batch, time_steps, hidden_width)
+        vector_terms[layer] = jnp.stack(
+            [
+                jnp.sum(normed_gradient * centered_input, axis=(0, 1)),
+                jnp.sum(dforget * stream, axis=(0, 1)),
+                jnp.sum(dforget, axis=(0, 1)),
+                jnp.sum(dreset * previous, axis=(0, 1)),
+                jnp.sum(dreset, axis=(0, 1)),
+            ],
+            axis=0,
+        )
+        centered_gradient = normed_gradient * norm_scale
+        through_norm = inverse_deviation * (
+            centered_gradient
+            - jnp.mean(centered_gradient, axis=-1, keepdims=True)
+            - centered_input * jnp.mean(centered_gradient * centered_input, axis=-1, keepdims=True)
+        )
+        grad_out = grad_out * (1.0 - reset) + dforget * vforget + through_norm
+    weight_grad = jnp.stack(weight_grads, axis=0)
+    vector_grad = lax.psum_scatter(
+        jnp.stack(vector_terms, axis=0), ("batch", "seq"), scatter_dimension=2, tiled=True
+    )
+    return (block_output, grad_out, weight_grad, vector_grad)
+
+
 def solution(mesh):
+    nb, ns = mesh.shape["batch"], mesh.shape["seq"]
+    body = functools.partial(tuned_body, nb, ns) if (nb, ns) == (4, 8) else general_body
     placed = (
         P("batch", "seq", None),
         P(None, ("batch", "seq"), None),

time: 2960 us -> 3500 us (1.18)
  Pallas kernels: 0 us -> 347 us
  local copies, waits for them, and re-layouts: 1120 us -> 1250 us
  other arithmetic: 351 us -> 401 us
    pallas_call x0 -> x1, Pallas kernels: none -> 347 us  [call_forward_one(): pl.pallas_call(functools.partial(forward_one, dm), out_shape=out_shape, i...]
    slice x104, local copies, waits for them, and re-layouts: 203 us -> 294 us  [rebuild_forward(): lax.associative_scan(compose, (forget_gate, (1.0 - forget_gate) * candida...]
    all_gather x1 -> x2, blocking collectives: 90.2 us -> 155 us  [the longest x1 80 us: tuned_body(): entry = lax.all_gather(made[11], 'batch', axis=0)]
    slice x111, local copies, waits for them, and re-layouts: 330 us -> 383 us  [the longest x110 381 us: tuned_body(): lax.associative_scan(compose, (jnp.flip(forget_gate, 1), jnp.flip(inject,...]
    all_gather x8 -> x6, blocking collectives: 192 us -> 147 us  [prefix(): pieces = jax.tree.map(lambda part: lax.all_gather(part, axis), value)]
    pad x56 -> x57, local copies, waits for them, and re-layouts: 149 us -> 123 us  [the longest x56 123 us: tuned_body(): lax.associative_scan(compose, (jnp.flip(forget_gate, 1), jnp.flip(inject,...]
  transfers between devices with their start and end apart: 5 -> 6, of which waited for: 4 -> 3; matrix products, arithmetic and copies ran while one was open for 17% -> 23% of each run, Pallas kernels for 0% -> 10%
where the time goes in v1:
time: 3500 us; the launch traced here: 3450 us
  local copies, waits for them, and re-layouts  1250 us (36%)
  waiting for transfers between devices  990 us (28%)
  other arithmetic  401 us (11%)
  Pallas kernels  347 us (10%)
  blocking collectives  302 us (9%)
  matrix products  144 us (4%)
    reduce_scatter x2, waiting for transfers between devices, tuned_body(): lax.psum_scatter(weight_term(jnp.int32(0), rows * lax.axis_size(('batch',...  880 us
    slice x110, local copies, waits for them, and re-layouts, tuned_body(): lax.associative_scan(compose, (jnp.flip(forget_gate, 1), jnp.flip(inject,...  381 us
    pallas_call x1, Pallas kernels, call_forward_one(): pl.pallas_call(functools.partial(forward_one, dm), out_shape=out_shape, i...  347 us
    slice x104, local copies, waits for them, and re-layouts, rebuild_forward(): lax.associative_scan(compose, (forget_gate, (1.0 - forget_gate) * candida...  294 us
    all_gather x6, blocking collectives, prefix(): pieces = jax.tree.map(lambda part: lax.all_gather(part, axis), value)  147 us
    pad x56, local copies, waits for them, and re-layouts, rebuild_forward(): lax.associative_scan(compose, (forget_gate, (1.0 - forget_gate) * candida...  131 us
    pad x56, local copies, waits for them, and re-layouts, tuned_body(): lax.associative_scan(compose, (jnp.flip(forget_gate, 1), jnp.flip(inject,...  123 us
    unnamed x6, waiting for transfers between devices  110 us
  transfers between devices with their start and end apart: 6, of which 3 were waited for; matrix products, arithmetic and copies ran while one was open for 23% of the time, Pallas kernels for 10%

profile of v1, /device:TPU:11, one launch (start us, length us, event | category | flops | bytes accessed | tf_op | source)
XLA Modules:
  0.0 3453.6 jit_solution(10060413657956314235)
XLA Ops:
  18.6 347.3 %forward_one.1 = (bf16[2048,2048]{1,0:T(8,128)(2,1)}, bf16[4,4,512,384]{3,2,1,0:T(8,128)(2,1)}, bf16[4,4,512,384]{3,2,1,0:T(8,128)(2,1)}, bf16[4,512,512]{2,1,0:...) custom-call(bf16[512,2048]{1,0:T(8,128)(2,1)} %bitcast.115, ...), custom_call_target="tpu_custom_call" | custom-call | tf_op jit(solution)/shard_map/forward_one/pallas_call | solution.py:366
  378.1 80.0 %all-gather.6 = f32[16,8,128]{2,1,0:T(8,128)S(1)} all-gather(f32[4,8,128]{2,1,0:T(8,128)S(1)} %copy-done.167), channel_id=8, replica_groups=mesh['batch'=4,'seq'=8] {'batch'}, dimensions={0}, use_global_device_ids=true | all-gather | bytes 81920 | tf_op jit(solution)/shard_map/all_gather | solution.py:570
  458.7 75.1 %all_gather.34 = f32[2,5,2048]{1,0,2:T(2,128)S(1)} all-gather(f32[2,5,64]{1,0,2:T(2,128)S(1)} %copy.30), channel_id=1, replica_groups=mesh['batch'=4,'seq'=8] {'batch','seq'}, dimensions={2}, use_global_device_ids=true | all-gather | bytes 84480 | tf_op jit(solution)/shard_map/all_gather | solution.py:560
  535.5 71.3 %slice_reduce_fusion.3 = (f32[2048]{0:T(1024)}, f32[2048]{0:T(1024)}, f32[2048]{0:T(1024)}, f32[2048]{0:T(1024)}, f32[2048]{0:T(1024)}, /*index=5*/f32[2048]{0:T...) fusion(f32[2,5,2048]{1,0,2:T(2,128)S(1)} %all_gather.34), kind=kLoop, calls=%fused_computation.138 | loop fusion | bytes 163840 | tf_op jit(solution)/shard_map/slice | solution.py:448
  623.6 25.7 fusion.9
  656.3 10.0 slice.1151
  823.0 32.8 reverse.20
  910.7 10.1 pad.459
  930.2 10.2 pad.443
  947.8 25.5 all-gather.1
  974.7 24.5 all-gather.2
  1000.2 10.4 multiply_add_fusion.2
  1019.7 10.2 fusion.109
  1072.2 16.6 slice.1271
  1088.9 10.3 slice.1269
  1202.2 10.1 slice.1230
  1241.7 10.1 pad.476
  1251.8 16.8 slice.1306
  1288.2 10.2 pad.475
  1323.9 21.4 fusion.5
  1352.3 10.0 slice.1317
  1517.1 10.1 slice.1390
  1531.7 32.6 reverse.21
  1564.3 24.1 all-gather.3
  1588.8 24.2 all-gather.4
  1614.6 32.7 rev.37
  1647.4 32.8 rev.34
  1753.9 10.1 pad.523
  1811.7 24.0 fusion.99
  1835.8 10.4 add_add_fusion
  1846.2 15.7 fusion.96
  1861.9 13.9 multiply_add_fusion
  1920.0 16.7 slice.1435
  1936.7 17.2 slice.1433
  2073.3 10.1 slice.1394
  2135.0 16.7 slice.1470
  2185.8 10.4 pad.555
  2217.0 10.1 pad.539
  2234.7 24.2 all-gather.7
  2259.3 24.2 all-gather.8
  2284.3 32.5 rev.42
  2316.8 32.6 rev.39
  2363.7 23.4 fusion.97
  2392.9 25.3 convolution_bitcast_fusion
  2418.2 24.4 convolution_bitcast_fusion.1
  2452.4 108.7 %reduce-scatter.10.cloned.1.call-done = f32[64,10]{1,0:T(8,128)} async-done(((f32[2048,10]{1,0:T(8,128)}), f32[64,10]{1,0:T(8,128)}) %reduce-scatter.10.cloned.1.call-update) | async-done | bytes 2576
  2562.7 442.3 %reduce-scatter.8.cloned.1.call-done = f32[64,6144]{1,0:T(8,128)} async-done(((f32[2048,6144]{1,0:T(8,128)}), f32[64,6144]{1,0:T(8,128)}) %reduce-scatter.8.cloned.1.call-update) | async-done | bytes 1572880 | tf_op jit(solution)/shard_map/reduce_scatter | solution.py:635
  3005.0 437.9 %reduce-scatter.6.cloned.1.call-done = f32[64,6144]{1,0:T(8,128)} async-done(((f32[2048,6144]{1,0:T(8,128)}), f32[64,6144]{1,0:T(8,128)}) %reduce-scatter.6.cloned.1.call-update) | async-done | bytes 1572880 | tf_op jit(solution)/shard_map/reduce_scatter | solution.py:635
  (940 shorter events, 1111.1 us)
Async XLA Ops:
  7.2 616.4 %all-gather.12.cloned.1.call-start = ((), (), s32[]{:S(2)}) async-start(), calls=%async_computation.6 | async-start | bytes 25952256 | tf_op jit(solution)/shard_map/all_gather | solution.py:577
  10.0 1313.8 %all-gather.14.cloned.1.call-start = ((), (), s32[]{:S(2)}) async-start(), calls=%async_computation.7 | async-start | bytes 25952256 | tf_op jit(solution)/shard_map/all_gather | solution.py:595
  371.9 162.0 %copy-start.6 = (bf16[2,256,2048]{2,1,0:T(8,128)(2,1)S(1)}, bf16[2,256,2048]{2,1,0:T(8,128)(2,1)}, u32[]{:S(2)}) copy-start(bf16[2,256,2048]{2,1,0:T(8,128)(2,1)} %param.10) | copy-start | bytes 6291460
  371.9 234.9 %all-to-all-start = ((f32[4,2,256,512]{2,3,1,0:T(8,128)}), f32[4,2,256,512]{2,3,1,0:T(8,128)}, u32[]{:S(2)}, u32[]{:S(2)}) async-start(f32[4,2,256,512]{2,3,1,0:T(8,128)} %bitcast.121), calls=%async_computation | async-start | bytes 8388608 | tf_op jit(solution)/shard_map/all_to_all | solution.py:569
  377.9 2183.2 %reduce-scatter.10.cloned.1.call-start = ((), (), s32[]{:S(2)}) async-start(), calls=%async_computation.8 | async-start | bytes 1081344
  458.1 148.7 %copy-start.98 = (f32[2,2048]{1,0:T(2,128)}, f32[2,2048]{1,0:T(2,128)S(1)}, u32[]{:S(2)}) copy-start(f32[2,2048]{1,0:T(2,128)S(1)} %constant_dynamic-slice_fusion) | copy-start | bytes 49156
  534.2 72.5 %copy-start.65 = (f32[2,256]{1,0:T(2,128)}, f32[2,256]{1,0:T(2,128)S(1)}, u32[]{:S(2)}) copy-start(f32[2,256]{1,0:T(2,128)S(1)} %broadcast_multiply_fusion.2) | copy-start | bytes 6148
  606.7 42.6 %copy-start.113 = (f32[2048]{0:T(1024)}, f32[2048]{0:T(1024)S(1)}, u32[]{:S(2)}) copy-start(f32[2048]{0:T(1024)S(1)} %get-tuple-element.386) | copy-start | bytes 24580
  620.9 28.4 copy-start.68
  623.6 25.7 copy-start.72
  623.6 25.7 copy-start.3
  822.9 32.9 copy-start.104
  822.9 32.9 copy-start.105
  822.9 32.9 copy-start.106
  822.9 32.9 copy-start.107
  822.9 33.0 copy-start.82
  822.9 33.0 copy-start.83
  822.9 33.7 copy-start.92
  822.9 33.7 copy-start.93
  822.9 33.7 copy-start.147
  823.0 33.9 copy-start.145
  823.0 34.0 copy-start.76
  823.0 34.0 copy-start.77
  1241.7 26.9 copy-start.44
  1531.7 32.6 copy-start.137
  1531.7 81.7 %copy-start.64 = (f32[2,2048]{1,0:T(2,128)S(1)}, f32[2,2048]{1,0:T(2,128)}, u32[]{:S(2)}) copy-start(f32[2,2048]{1,0:T(2,128)} %custom-call.1) | copy-start | bytes 49156
  1647.3 32.9 copy-start.155
  1647.3 32.9 copy-start.156
  1647.3 32.9 copy-start.157
  1647.3 32.9 copy-start.158
  1647.3 33.1 copy-start.103
  1647.3 33.2 copy-start.102
  1647.3 33.4 copy-start.86
  1647.3 33.4 copy-start.87
  1647.3 33.4 copy-start.141
  1647.3 33.6 copy-start.140
  1647.4 33.7 copy-start.74
  1647.4 33.7 copy-start.75
  2063.4 24.7 copy-start.154
  2063.4 24.8 copy-start.101
  2063.4 24.9 copy-start.151
  2063.4 24.9 copy-start.152
  2063.4 25.0 copy-start.89
  2063.4 25.0 copy-start.91
  2063.4 25.1 copy-start.150
  2228.1 55.8 %copy-start.63 = (f32[2,2048]{1,0:T(2,128)S(1)}, f32[2,2048]{1,0:T(2,128)}, u32[]{:S(2)}) copy-start(f32[2,2048]{1,0:T(2,128)} %custom-call.2) | copy-start | bytes 49156
  2392.8 612.2 %reduce-scatter.8.cloned.1.call-start = ((), (), s32[]{:S(2)}) async-start(), calls=%async_computation.5 | async-start | bytes 51904512 | tf_op jit(solution)/shard_map/reduce_scatter | solution.py:635
  2418.2 1024.8 %reduce-scatter.6.cloned.1.call-start = ((), (), s32[]{:S(2)}) async-start(), calls=%async_computation.4 | async-start | bytes 51904512 | tf_op jit(solution)/shard_map/reduce_scatter | solution.py:635
  (129 other events, 1114.5 us)
Sparse Core Ops, SparseCore 0:
  11.5 263.3 all-gather.11
  277.8 195.3 all-gather.13
  2392.9 168.1 reduce-scatter.9
  2568.6 436.4 reduce-scatter.7
  3012.4 430.4 reduce-scatter.5

commit v2 on v0

--- a/solution.py
+++ b/solution.py
@@ -1,9 +1,1040 @@
+import functools
+import types
+
 import jax
 import jax.numpy as jnp
 from jax import lax
+from jax.experimental import pallas as pl
+from jax.experimental.pallas import tpu as pltpu
 from jax.sharding import PartitionSpec as P
 
+MESH = pl.DeviceIdType.MESH
+F32, BF16 = jnp.float32, jnp.bfloat16
+V, DMA = pltpu.VMEM, pltpu.SemaphoreType.DMA
 epsilon = 1e-05
+F = 128
+G3 = 3 * F
+HBM = pl.BlockSpec(memory_space=pl.ANY)
+INV = pl.BlockSpec(memory_space=pltpu.VMEM)
+
+
+class Dims:
+    def __init__(self, nb, ns, x_shape, w_shape):
+        self.nb, self.ns = nb, ns
+        self.inner = 2
+        self.outer = ns // 2
+        self.sb, self.steps, self.d = x_shape
+        self.local = self.sb * self.steps
+        self.nseq = self.sb * nb
+        self.tok = self.local * nb
+        self.q = self.d // nb
+        self.nf = self.q // F
+        self.cols = 3 * self.q
+        self.layers, self.rows = w_shape[0], w_shape[1]
+
+
+class Net:
+    def __init__(self, dm):
+        nb, ns, inner, outer = dm.nb, dm.ns, dm.inner, dm.outer
+        self.b, self.s = lax.axis_index("batch"), lax.axis_index("seq")
+        b, s = self.b, self.s
+        self.z, self.y = s // inner, lax.rem(s, inner)
+        self.across, self.sib, self.diag = b ^ 2, b ^ 1, b ^ 3
+        self.batch_peers = [lax.rem(b + j, nb) for j in range(1, nb)]
+        self.outer_peers = [lax.rem(self.z + j, outer) for j in range(1, outer)]
+        self.inner_peers = [lax.rem(self.y + j, inner) for j in range(1, inner)]
+        self.seq_peers = [lax.rem(s + j, ns) for j in range(1, ns)]
+        barrier = pltpu.get_barrier_semaphore()
+        for p in self.batch_peers:
+            pl.semaphore_signal(barrier, inc=1, device_id=(p, s), device_id_type=MESH)
+        for p in self.seq_peers:
+            pl.semaphore_signal(barrier, inc=1, device_id=(b, p), device_id_type=MESH)
+        pl.semaphore_wait(barrier, nb - 1 + ns - 1)
+
+
+def remote(src, dst, ssem, rsem, dev):
+    return pltpu.make_async_remote_copy(
+        src_ref=src, dst_ref=dst, send_sem=ssem, recv_sem=rsem, device_id=dev, device_id_type=MESH
+    )
+
+
+def arrived(dst, rsem, dev):
+    remote(dst, dst, rsem, rsem, dev).wait_recv()
+
+
+def sent(src, ssem, dev):
+    remote(src, src, ssem, ssem, dev).wait_send()
+
+
+def local_copy(src, dst, sem):
+    c = pltpu.make_async_copy(src, dst, sem)
+    c.start()
+    return c
+
+
+def at128(v):
+    return pl.multiple_of(v, F)
+
+
+def sigmoid(v):
+    return 1.0 / (1.0 + jnp.exp(jnp.minimum(-v, 80.0)))
+
+
+def launch(dm, name, cid, kernel, ins, outs, scratch):
+    names = list(ins) + list(outs) + list(scratch)
+
+    def run(*refs):
+        kernel(dm, types.SimpleNamespace(**dict(zip(names, refs))))
+
+    got = pl.pallas_call(
+        run,
+        out_shape=[jax.ShapeDtypeStruct(shape, dtype) for shape, dtype, _ in outs.values()],
+        in_specs=[spec for _, spec in ins.values()],
+        out_specs=[spec for _, _, spec in outs.values()],
+        scratch_shapes=list(scratch.values()),
+        compiler_params=pltpu.CompilerParams(collective_id=cid, has_side_effects=True, vmem_limit_bytes=63 * 2**20),
+        name=name,
+    )(*[array for array, _ in ins.values()])
+    return types.SimpleNamespace(**dict(zip(outs, got)))
+
+
+def norm_rows(x, gain):
+    mu = jnp.mean(x, axis=-1, keepdims=True)
+    xc = x - mu
+    rstd = lax.rsqrt(jnp.mean(xc * xc, axis=-1, keepdims=True) + epsilon)
+    return mu, rstd, (xc * rstd * gain).astype(BF16)
+
+
+def vrow(dm, r, n, k, fc):
+    return r.vec[k : k + 1, pl.ds(at128(n.b * dm.q + fc * F), F)]
+
+
+def products(dm, r, n, w, chunks, base):
+    lo, hi = chunks[0] * G3, (chunks[-1] + 1) * G3
+
+    def step(i, carry):
+        rows = pl.ds(pl.multiple_of(i * dm.steps, dm.steps), dm.steps)
+        m = jnp.dot(r.normed[rows, :], w[:, :, lo:hi].reshape(dm.d, hi - lo), preferred_element_type=F32)
+        for k, fc in enumerate(chunks):
+            o = k * G3
+            vf, bf, br = [vrow(dm, r, n, base + j, fc) for j in (1, 2, 4)]
+            r.fS[fc, rows, :] = sigmoid(m[:, o + F : o + 2 * F] + vf * r.xS[fc, rows, :] + bf)
+            r.cS[fc, rows, :] = m[:, o : o + F]
+            r.rS[fc, rows, :] = m[:, o + 2 * F : o + G3] + br
+        return carry
+
+    lax.fori_loop(0, dm.nseq, step, 0)
+
+
+def at_time(dm, t):
+    return pl.ds(t, dm.nseq, stride=dm.steps)
+
+
+def scan_totals(dm, r, n, fc):
+    def step(t, carry):
+        a, v = carry
+        at = at_time(dm, t)
+        f, cand = r.fS[fc, at, :], r.cS[fc, at, :]
+        return a * f, cand + f * (v - cand)
+
+    one, zero = jnp.ones((dm.nseq, F), F32), jnp.zeros((dm.nseq, F), F32)
+    a, v = lax.fori_loop(0, dm.steps, step, (one, zero), unroll=8)
+    r.totS[fc, 0] = a
+    r.totS[fc, 1] = v
+    r.tot[fc, n.s, 0] = a
+    r.tot[fc, n.s, 1] = v
+    for p in n.seq_peers:
+        remote(r.totS.at[fc], r.tot.at[fc, n.s], r.t_s.at[fc, p], r.t_r.at[fc, n.s], (n.b, p)).start()
+
+
+def scan_finish(dm, r, n, fc, base):
+    for p in n.seq_peers:
+        arrived(r.tot.at[fc, p], r.t_r.at[fc, p], (n.b, p))
+    vr = vrow(dm, r, n, base + 3, fc)
+
+    def fold(j, c):
+        return jnp.where(j < n.s, r.tot[fc, j, 0] * c + r.tot[fc, j, 1], c)
+
+    entering = lax.fori_loop(0, dm.ns, fold, jnp.zeros((dm.nseq, F), F32))
+    r.incS[fc] = entering
+
+    def step(t, prev):
+        at = at_time(dm, t)
+        f, cand, x = r.fS[fc, at, :], r.cS[fc, at, :], r.xS[fc, at, :]
+        reset = sigmoid(r.rS[fc, at, :] + vr * prev)
+        c = cand + f * (prev - cand)
+        r.cellS[fc, at, :] = c
+        r.rS[fc, at, :] = reset
+        r.hS[fc, at, :] = x + reset * (c - x)
+        return c
+
+    lax.fori_loop(0, dm.steps, step, entering, unroll=8)
+
+
+def totals_sent(dm, r, n):
+    for fc in range(dm.nf):
+        for p in n.seq_peers:
+            sent(r.totS.at[fc], r.t_s.at[fc, p], (n.b, p))
+
+
+def back_totals(dm, r, n, fc, base):
+    vr = vrow(dm, r, n, base + 3, fc)
+
+    def step(i, carry):
+        at = at_time(dm, dm.steps - 1 - i)
+        reset, dh = r.rS[fc, at, :], r.dhS[fc, at, :]
+        direct = dh * reset
+        dreset = (r.cellS[fc, at, :] - r.xS[fc, at, :]) * direct * (1.0 - reset)
+        r.rS[fc, at, :] = direct
+        r.drS[fc, at, :] = dreset
+        return r.fS[fc, at, :] * (direct + carry) + dreset * vr
+
+    v = lax.fori_loop(0, dm.steps, step, jnp.zeros((dm.nseq, F), F32), unroll=8)
+    r.bkS[fc] = v
+    r.bk[fc, n.s] = v
+    for p in n.seq_peers:
+        remote(r.bkS.at[fc], r.bk.at[fc, n.s], r.k_s.at[fc, p], r.k_r.at[fc, n.s], (n.b, p)).start()
+
+
+def back_finish(dm, r, n, fc, base):
+    for p in n.seq_peers:
+        arrived(r.bk.at[fc, p], r.k_r.at[fc, p], (n.b, p))
+    vf, vr = vrow(dm, r, n, base + 1, fc), vrow(dm, r, n, base + 3, fc)
+
+    def fold(i, c):
+        j = dm.ns - 1 - i
+        return jnp.where(j > n.s, r.tot[fc, j, 0] * c + r.bk[fc, j], c)
+
+    zero = jnp.zeros((dm.nseq, F), F32)
+    carry = lax.fori_loop(0, dm.ns, fold, zero)
+
+    def one(at, prev, state):
+        carry, s1, s2, s3, s4 = state
+        f, cand, x = r.fS[fc, at, :], r.cS[fc, at, :], r.xS[fc, at, :]
+        direct, dreset = r.rS[fc, at, :], r.drS[fc, at, :]
+        dcell = direct + carry
+        dcand = dcell * (1.0 - f)
+        dforget = dcand * f * (prev - cand)
+        r.cS[fc, at, :] = dcand
+        r.fS[fc, at, :] = dforget
+        r.rS[fc, at, :] = r.dhS[fc, at, :] - direct + dforget * vf
+        return (f * dcell + dreset * vr, s1 + dforget * x, s2 + dforget, s3 + dreset * prev, s4 + dreset)
+
+    def step(i, state):
+        t = dm.steps - 1 - i
+        return one(at_time(dm, t), r.cellS[fc, at_time(dm, t - 1), :], state)
+
+    state = lax.fori_loop(0, dm.steps - 1, step, (carry, zero, zero, zero, zero), unroll=5)
+    state = one(at_time(dm, 0), r.incS[fc], state)
+    for k in range(4):
+        r.vsum_out[fc, k] = state[k + 1]
+    r.dmixed[:, fc * G3 : fc * G3 + F] = r.cS[fc].astype(BF16)
+    r.dmixed[:, fc * G3 + F : fc * G3 + 2 * F] = r.fS[fc].astype(BF16)
+    r.dmixed[:, fc * G3 + 2 * F : fc * G3 + G3] = r.drS[fc].astype(BF16)
+
+
+def back_sent(dm, r, n):
+    for fc in range(dm.nf):
+        for p in n.seq_peers:
+            sent(r.bkS.at[fc], r.k_s.at[fc, p], (n.b, p))
+
+
+def back_outputs(dm, r, fc):
+    cols = pl.ds(fc * G3, G3)
+    return [
+        local_copy(r.dmixed.at[:, cols], r.dmixed_out.at[:, cols], r.out_sem.at[fc, 0]),
+        local_copy(r.rS.at[fc], r.dtail_out.at[fc], r.out_sem.at[fc, 1]),
+    ]
+
+
+class Gather:
+    def __init__(self, dm, n, r, l, w):
+        self.dm, self.n, self.r, self.l, self.w = dm, n, r, l, w
+
+    def strip(self, fc, pos):
+        R = self.dm.rows
+        return self.w.at[:, pl.ds(pl.multiple_of(pos * R, R), R), pl.ds(fc * G3, G3)]
+
+    def piece(self, fc, b):
+        n, R = self.n, self.dm.rows
+        return self.w.at[b, pl.ds(pl.multiple_of(n.s * R, R), R), pl.ds(fc * G3, G3)]
+
+    def pre(self, fc):
+        n, r, l = self.n, self.r, self.l
+        for p in n.batch_peers:
+            remote(r.w_in.at[l, p, fc], self.piece(fc, n.b), r.pre_s.at[l, fc, p], r.pre_r.at[l, fc, n.b], (p, n.s)).start()
+
+    def hop(self, fc, src, to):
+        n, r, l, dm = self.n, self.r, self.l, self.dm
+        at = self.strip(fc, src * dm.inner + n.y)
+        side = 1 if to > 0 else 0
+        return remote(at, at, r.z_s.at[l, fc, src, side], r.z_r.at[l, fc, src], (n.b, (n.z + to) * dm.inner + n.y))
+
+    def to_inner(self, fc, src):
+        n, r, l, dm = self.n, self.r, self.l, self.dm
+        at = self.strip(fc, src * dm.inner + n.y)
+        return [
+            remote(at, at, r.y_s.at[l, fc, src, p], r.y_r.at[l, fc, src, n.y], (n.b, n.z * dm.inner + p))
+            for p in n.inner_peers
+        ]
+
+    def start(self, fc):
+        n, r, l, dm = self.n, self.r, self.l, self.dm
+        for p in n.batch_peers:
+            arrived(self.piece(fc, p), r.pre_r.at[l, fc, p], (p, n.s))
+        pl.when(n.z < dm.outer - 1)(lambda: self.hop(fc, n.z, 1).start())
+        pl.when(n.z > 0)(lambda: self.hop(fc, n.z, -1).start())
+        for c in self.to_inner(fc, n.z):
+            c.start()
+
+    def forward(self, fc):
+        n, r, l, dm = self.n, self.r, self.l, self.dm
+        for h in range(1, dm.outer):
+            for way in (-1, 1):
+                src = n.z + way * h
+                has = (src >= 0) if way < 0 else (src < dm.outer)
+                on = (n.z < dm.outer - 1) if way < 0 else (n.z > 0)
+
+                def take(src=src, on=on, way=way):
+                    at = self.strip(fc, src * dm.inner + n.y)
+                    arrived(at, r.z_r.at[l, fc, src], (n.b, n.s))
+                    pl.when(on)(lambda: self.hop(fc, src, -way).start())
+                    for c in self.to_inner(fc, src):
+                        c.start()
+
+                pl.when(has)(take)
+
+    def complete(self, fc):
+        n, r, l, dm = self.n, self.r, self.l, self.dm
+        for o in range(dm.outer):
+            for p in n.inner_peers:
+                arrived(self.strip(fc, o * dm.inner + p), r.y_r.at[l, fc, o, p], (n.b, n.s))
+
+    def drain(self, fc):
+        n, r, l, dm = self.n, self.r, self.l, self.dm
+        for p in n.batch_peers:
+            sent(r.w_in.at[l, p, fc], r.pre_s.at[l, fc, p], (p, n.s))
+        for o in range(dm.outer):
+            for p in n.inner_peers:
+                sent(self.strip(fc, n.s), r.y_s.at[l, fc, o, p], (n.b, n.s))
+            right = jnp.logical_and(o <= n.z, n.z < dm.outer - 1)
+            left = jnp.logical_and(o >= n.z, n.z > 0)
+            for ok, side in ((right, 1), (left, 0)):
+                pl.when(ok)(lambda o=o, side=side: sent(self.strip(fc, n.s), r.z_s.at[l, fc, o, side], (n.b, n.s)))
+
+
+def kernel_one(dm, r):
+    n = Net(dm)
+    nb, ns, nf, inner, outer, R = dm.nb, dm.ns, dm.nf, dm.inner, dm.outer, dm.rows
+    b, s, z, y = n.b, n.s, n.z, n.y
+    w0, w1 = Gather(dm, n, r, 0, r.wq0), Gather(dm, n, r, 1, r.wq1_out)
+    NX = 4
+    XR = dm.local // NX
+
+    r.vecg[b, s] = r.vec_in[...]
+    for p in n.batch_peers:
+        remote(r.vec_in, r.vecg.at[b, s], r.vp_s.at[p], r.vp_r.at[b], (p, s)).start()
+    first = [local_copy(r.w_in.at[l, b, fc], g.piece(fc, b), r.loc.at[l * nf + fc]) for l, g in ((0, w0), (1, w1)) for fc in range(nf)]
+    own_x = local_copy(r.x_in, r.xg.at[b], r.loc.at[2 * nf])
+    for fc in range(nf):
+        w0.pre(fc)
+    remote(r.x_in, r.xg.at[b], r.xc_s, r.xc_r, (n.sib, s)).start()
+
+    def x_send(k):
+        rows = pl.ds(k * XR, XR)
+        return remote(r.x_in.at[rows], r.xg.at[b, rows], r.xx_s.at[k], r.xx_r.at[k], (n.across, s))
+
+    def x_relay(k):
+        at = r.xg.at[n.across, pl.ds(k * XR, XR)]
+        return remote(at, at, r.xl_s.at[k], r.xl_r.at[k], (n.sib, s))
+
+    def relay(k):
+        arrived(r.xg.at[n.across, pl.ds(k * XR, XR)], r.xx_r.at[k], (n.across, s))
+        x_relay(k).start()
+
+    for k in range(NX):
+        x_send(k).start()
+    for p in n.batch_peers:
+        arrived(r.vecg.at[p, s], r.vp_r.at[p], (p, s))
+    for p in n.outer_peers:
+        remote(r.vecg.at[:, s], r.vecg.at[:, s], r.vz_s.at[p], r.vz_r.at[z], (b, p * inner + y)).start()
+    for c in first:
+        c.wait()
+    w0.start(0)
+    for p in n.outer_peers:
+        arrived(r.vecg.at[:, p * inner + y], r.vz_r.at[p], (b, s))
+    for o in range(outer):
+        for p in n.inner_peers:
+            at = r.vecg.at[:, o * inner + y]
+            remote(at, at, r.vy_s.at[o, p], r.vy_r.at[o, y], (b, z * inner + p)).start()
+    for fc in range(1, nf):
+        w0.start(fc)
+    for o in range(outer):
+        for p in n.inner_peers:
+            arrived(r.vecg.at[:, o * inner + p], r.vy_r.at[o, p], (b, s))
+    per = F // R
+    for k in range(dm.d // F):
+        bb, s0 = (k * per) // ns, (k * per) % ns
+        total = r.vecg[bb, s0]
+        for j in range(1, per):
+            total = total + r.vecg[bb, s0 + j]
+        r.vec[:, k * F : (k + 1) * F] = total
+    own_x.wait()
+
+    TILE = 32
+
+    def norm_block(bb):
+        def step(i, carry):
+            rows = pl.ds(pl.multiple_of(i * TILE, TILE), TILE)
+            x = r.xg[bb, rows, :].astype(F32)
+            mu, rstd, normed = norm_rows(x, r.vec[0:1, :])
+            every = pl.ds(pl.multiple_of(bb * dm.local + i * TILE, TILE), TILE)
+            r.normed[every, :] = normed
+            r.mu_out[every, :] = jnp.broadcast_to(mu, (TILE, F))
+            r.rstd_out[every, :] = jnp.broadcast_to(rstd, (TILE, F))
+            for fc in range(nf):
+                r.xS[fc, every, :] = r.xg[bb, rows, pl.ds(at128(b * dm.q + fc * F), F)].astype(F32)
+            return carry
+
+        lax.fori_loop(0, dm.local // TILE, step, 0)
+
+    norm_block(b)
+    arrived(r.xg.at[n.sib], r.xc_r, (n.sib, s))
+    norm_block(n.sib)
+    w0.forward(0)
+    relay(0)
+    relay(1)
+    for fc in range(nf):
+        w1.pre(fc)
+    w0.forward(1)
+    relay(2)
+    w0.forward(2)
+    relay(3)
+    norm_block(n.across)
+    w0.forward(3)
+    for fc in range(nf):
+        w1.start(fc)
+    for k in range(NX):
+        arrived(r.xg.at[n.diag, pl.ds(k * XR, XR)], r.xl_r.at[k], (n.sib, s))
+    norm_block(n.diag)
+    normed_copy = local_copy(r.normed, r.normed_out, r.loc.at[0])
+
+    def p1(fc):
+        w0.complete(fc)
+        products(dm, r, n, r.wq0, (fc,), 0)
+        scan_totals(dm, r, n, fc)
+
+    pend = []
+
+    def p2(fc):
+        scan_finish(dm, r, n, fc, 0)
+        r.hb[fc] = r.hS[fc].astype(BF16)
+        remote(r.hb.at[fc], r.x1g_out.at[b, fc], r.h_s.at[fc], r.h_r.at[fc], (n.across, s)).start()
+        remote(r.hb.at[fc], r.x1g_out.at[b, fc], r.hc_s.at[fc], r.hc_r.at[fc], (n.sib, s)).start()
+        pend.append(local_copy(r.hb.at[fc], r.x1g_out.at[b, fc], r.out_sem.at[fc, 0]))
+        pairs = [(r.fS, r.f_out), (r.cS, r.c_out), (r.rS, r.r_out), (r.cellS, r.cell_out), (r.hS, r.x1_out), (r.xS, r.xo_out)]
+        for k, (src, dst) in enumerate(pairs):
+            pend.append(local_copy(src.at[fc], dst.at[fc], r.out_sem.at[fc, k + 1]))
+
+    def h_relay(fc):
+        at = r.x1g_out.at[n.across, fc]
+        arrived(at, r.h_r.at[fc], (n.across, s))
+        remote(at, at, r.hl_s.at[fc], r.hl_r.at[fc], (n.sib, s)).start()
+
+    p1(0)
+    p1(1)
+    p2(0)
+    for p in n.batch_peers:
+        cols = pl.ds(at128(p * dm.q), dm.q)
+        remote(r.cot_in.at[:, cols], r.cot_out.at[b], r.cot_s.at[p], r.cot_r.at[b], (p, s)).start()
+    pend.append(local_copy(r.cot_in.at[:, pl.ds(at128(b * dm.q), dm.q)], r.cot_out.at[b], r.loc.at[1]))
+    p1(2)
+    p2(1)
+    w1.forward(0)
+    p1(3)
+    p2(2)
+    p2(3)
+    wq_copy = local_copy(r.wq0, r.wq0_out, r.loc.at[2])
+    for fc in range(nf):
+        if fc:
+            w1.forward(fc)
+        h_relay(fc)
+    r.inc_out[...] = r.incS[...]
+    r.tot_out[...] = r.tot[...]
+    r.vec_out[...] = r.vec[...]
+    for fc in range(nf):
+        w1.complete(fc)
+        arrived(r.x1g_out.at[n.sib, fc], r.hc_r.at[fc], (n.sib, s))
+        arrived(r.x1g_out.at[n.diag, fc], r.hl_r.at[fc], (n.sib, s))
+    for p in n.batch_peers:
+        arrived(r.cot_out.at[p], r.cot_r.at[p], (p, s))
+    for c in pend:
+        c.wait()
+    normed_copy.wait()
+    wq_copy.wait()
+    for p in n.batch_peers:
+        sent(r.vec_in, r.vp_s.at[p], (p, s))
+        sent(r.cot_out.at[p], r.cot_s.at[p], (p, s))
+    for p in n.outer_peers:
+        sent(r.vecg.at[:, s], r.vz_s.at[p], (b, s))
+    for p in n.inner_peers:
+        for o in range(outer):
+            sent(r.vecg.at[:, s], r.vy_s.at[o, p], (b, s))
+    sent(r.x_in, r.xc_s, (n.sib, s))
+    for k in range(NX):
+        x_send(k).wait_send()
+        x_relay(k).wait_send()
+    totals_sent(dm, r, n)
+    for fc in range(nf):
+        w0.drain(fc)
+        w1.drain(fc)
+        for sem in (r.h_s, r.hc_s, r.hl_s):
+            sent(r.hb.at[fc], sem.at[fc], (b, s))
+
+
+def scan_scratch(dm):
+    nf, ns = dm.nf, dm.ns
+    return {
+        "totS": V((nf, 2, dm.nseq, F), F32),
+        "t_s": DMA((nf, ns)), "t_r": DMA((nf, ns)),
+    }
+
+
+def call_one(dm, x, w, vec, cot):
+    nb, ns, nf, inner, outer, R = dm.nb, dm.ns, dm.nf, dm.inner, dm.outer, dm.rows
+    D, q, tok, L = dm.d, dm.q, dm.tok, dm.layers
+    wshape = (nb, ns * R, dm.cols)
+    chunk, cV = ((nf, tok, F), F32, HBM), V((nf, tok, F), F32)
+    ins = {"x_in": (x, HBM), "w_in": (w, HBM), "vec_in": (vec, INV), "cot_in": (cot, HBM)}
+    outs = {
+        "normed_out": ((tok, D), BF16, HBM), "wq0_out": (wshape, BF16, HBM), "wq1_out": (wshape, BF16, HBM),
+        "cot_out": ((nb, dm.local, q), BF16, HBM), "x1g_out": ((nb, nf, tok, F), BF16, HBM),
+        "x1_out": chunk, "xo_out": chunk, "f_out": chunk, "c_out": chunk, "r_out": chunk, "cell_out": chunk,
+        "inc_out": ((nf, dm.nseq, F), F32, INV), "tot_out": ((nf, ns, 2, dm.nseq, F), F32, INV),
+        "vec_out": ((16, D), F32, INV), "mu_out": ((tok, F), F32, INV), "rstd_out": ((tok, F), F32, INV),
+    }
+    scratch = {
+        "xg": V((nb, dm.local, D), BF16), "normed": V((tok, D), BF16), "wq0": V(wshape, BF16),
+        "vecg": V((nb, ns, 16, F), F32), "vec": V((16, D), F32),
+        "xS": cV, "fS": cV, "cS": cV, "rS": cV, "cellS": cV, "hS": cV, "hb": V((nf, tok, F), BF16),
+        "incS": V((nf, dm.nseq, F), F32), "tot": V((nf, ns, 2, dm.nseq, F), F32),
+        "pre_s": DMA((L, nf, nb)), "pre_r": DMA((L, nf, nb)), "z_s": DMA((L, nf, outer, 2)), "z_r": DMA((L, nf, outer)),
+        "y_s": DMA((L, nf, outer, inner)), "y_r": DMA((L, nf, outer, inner)),
+        "vp_s": DMA((nb,)), "vp_r": DMA((nb,)), "vz_s": DMA((outer,)), "vz_r": DMA((outer,)),
+        "vy_s": DMA((outer, inner)), "vy_r": DMA((outer, inner)),
+        "xx_s": DMA((4,)), "xx_r": DMA((4,)), "xc_s": DMA, "xc_r": DMA, "xl_s": DMA((4,)), "xl_r": DMA((4,)),
+        "cot_s": DMA((nb,)), "cot_r": DMA((nb,)),
+        "h_s": DMA((nf,)), "h_r": DMA((nf,)), "hc_s": DMA((nf,)), "hc_r": DMA((nf,)), "hl_s": DMA((nf,)), "hl_r": DMA((nf,)),
+        "loc": DMA((2 * nf + 1,)), "out_sem": DMA((nf, 7)),
+        **scan_scratch(dm),
+    }
+    return launch(dm, "forward_one", 0, kernel_one, ins, outs, scratch)
+
+
+def kernel_two(dm, r):
+    n = Net(dm)
+    nb, nf = dm.nb, dm.nf
+    b, s = n.b, n.s
+    w_copy = local_copy(r.w_in, r.wq, r.loc.at[0])
+    x_copy = local_copy(r.x1_in, r.xS, r.loc.at[1])
+    cot_copy = [local_copy(r.cot_in.at[k], r.cot.at[pl.ds(k * dm.local, dm.local)], r.loc.at[2 + k]) for k in range(nb)]
+    TT, TILE = 256, 32
+
+    def fetch(k):
+        return pltpu.make_async_copy(r.x1g_in.at[:, :, pl.ds(k * TT, TT)], r.xt.at[k % 2], r.xt_sem.at[k % 2])
+
+    fetch(0).start()
+    for k in range(dm.tok // TT):
+        if (k + 1) * TT < dm.tok:
+            fetch(k + 1).start()
+        fetch(k).wait()
+
+        def step(i, carry, k=k):
+            rows = pl.ds(pl.multiple_of(i * TILE, TILE), TILE)
+            x = jnp.concatenate([r.xt[k % 2, q, fc, rows, :] for q in range(nb) for fc in range(nf)], axis=1).astype(F32)
+            mu, rstd, normed = norm_rows(x, r.vec[5:6, :])
+            every = pl.ds(pl.multiple_of(k * TT + i * TILE, TILE), TILE)
+            r.normed[every, :] = normed
+            r.mu_out[every, :] = jnp.broadcast_to(mu, (TILE, F))
+            r.rstd_out[every, :] = jnp.broadcast_to(rstd, (TILE, F))
+            return carry
+
+        lax.fori_loop(0, TT // TILE, step, 0)
+    normed_copy = local_copy(r.normed, r.normed_out, r.xt_sem.at[0])
+    for c in [w_copy, x_copy] + cot_copy:
+        c.wait()
+
+    def p1(fcs):
+        products(dm, r, n, r.wq, fcs, 5)
+        for fc in fcs:
+            scan_totals(dm, r, n, fc)
+
+    def block_send(fc, p):
+        cols = pl.ds(at128(b * dm.q + fc * F), F)
+        src = r.hb.at[fc, pl.ds(pl.multiple_of(p * dm.local, dm.local), dm.local)]
+        return remote(src, r.block_out.at[:, cols], r.o_s.at[fc, p], r.o_r.at[fc, b], (p, s))
+
+    pend = []
+
+    def p2(fc):
+        scan_finish(dm, r, n, fc, 5)
+        r.hb[fc] = r.hS[fc].astype(BF16)
+        for p in n.batch_peers:
+            block_send(fc, p).start()
+        cols = pl.ds(at128(b * dm.q + fc * F), F)
+        src = r.hb.at[fc, pl.ds(pl.multiple_of(b * dm.local, dm.local), dm.local)]
+        pend.append(local_copy(src, r.block_out.at[:, cols], r.out_sem.at[fc, 2]))
+        r.dhS[fc] = r.cot[:, fc * F : (fc + 1) * F].astype(F32)
+        back_totals(dm, r, n, fc, 5)
+
+    def p3(fc):
+        back_finish(dm, r, n, fc, 5)
+        pend.extend(back_outputs(dm, r, fc))
+
+    p1((0, 1))
+    p1((2, 3))
+    for fc in range(nf):
+        p2(fc)
+    for fc in range(nf):
+        p3(fc)
+    for fc in range(nf):
+        for p in n.batch_peers:
+            block_send(fc, p).wait_send()
+            arrived(r.block_out.at[:, pl.ds(at128(p * dm.q + fc * F), F)], r.o_r.at[fc, p], (p, s))
+    for c in pend:
+        c.wait()
+    normed_copy.wait()
+    totals_sent(dm, r, n)
+    back_sent(dm, r, n)
+
+
+def call_two(dm, one):
+    nb, ns, nf = dm.nb, dm.ns, dm.nf
+    tok = dm.tok
+    cV = V((nf, tok, F), F32)
+    ins = {
+        "w_in": (one.wq1_out, HBM), "x1_in": (one.x1_out, HBM), "cot_in": (one.cot_out, HBM),
+        "x1g_in": (one.x1g_out, HBM), "vec": (one.vec_out, INV),
+    }
+    outs = {
+        "normed_out": ((tok, dm.d), BF16, HBM), "block_out": ((dm.local, dm.d), BF16, HBM),
+        "dmixed_out": ((tok, dm.cols), BF16, HBM), "dtail_out": ((nf, tok, F), F32, HBM),
+        "vsum_out": ((nf, 4, dm.nseq, F), F32, INV), "mu_out": ((tok, F), F32, INV), "rstd_out": ((tok, F), F32, INV),
+    }
+    scratch = {
+        "wq": V((nb, ns * dm.rows, dm.cols), BF16), "cot": V((tok, dm.q), BF16), "xt": V((2, nb, nf, 256, F), BF16),
+        "normed": V((tok, dm.d), BF16), "dmixed": V((tok, dm.cols), BF16),
+        "xS": cV, "fS": cV, "cS": cV, "rS": cV, "cellS": cV, "drS": cV, "hS": cV, "hb": V((nf, tok, F), BF16),
+        "incS": V((nf, dm.nseq, F), F32), "tot": V((nf, ns, 2, dm.nseq, F), F32),
+        "bk": V((nf, ns, dm.nseq, F), F32), "bkS": V((nf, dm.nseq, F), F32),
+        "k_s": DMA((nf, ns)), "k_r": DMA((nf, ns)), "o_s": DMA((nf, nb)), "o_r": DMA((nf, nb)),
+        "loc": DMA((2 + nb,)), "xt_sem": DMA((2,)), "out_sem": DMA((nf, 3)),
+        **scan_scratch(dm),
+    }
+    alias = dict(scratch)
+
+    def kernel(dm, r):
+        r.dhS = r.hS
+        kernel_two(dm, r)
+
+    return launch(dm, "layer_two", 1, kernel, ins, outs, alias)
+
+
+def kernel_three(dm, r):
+    n = Net(dm)
+    nf = dm.nf
+    loads = []
+    for fc in range(nf):
+        pairs = [(r.f_in.at[fc], r.fS), (r.c_in.at[fc], r.cS), (r.r_in.at[fc], r.rS), (r.cell_in.at[fc], r.cellS),
+                 (r.xo_in.at[fc], r.xS), (r.dh_in.at[:, pl.ds(fc * F, F)], r.dhS)]
+        loads.append([local_copy(src, dst.at[fc], r.loc.at[fc, k]) for k, (src, dst) in enumerate(pairs)])
+    pend = []
+    for fc in range(nf):
+        for c in loads[fc]:
+            c.wait()
+        back_totals(dm, r, n, fc, 0)
+    for fc in range(nf):
+        back_finish(dm, r, n, fc, 0)
+        pend.extend(back_outputs(dm, r, fc))
+    for c in pend:
+        c.wait()
+    back_sent(dm, r, n)
+
+
+def call_three(dm, one, dh):
+    nb, ns, nf, tok = dm.nb, dm.ns, dm.nf, dm.tok
+    cV = V((nf, tok, F), F32)
+    ins = {
+        "f_in": (one.f_out, HBM), "c_in": (one.c_out, HBM), "r_in": (one.r_out, HBM), "cell_in": (one.cell_out, HBM),
+        "xo_in": (one.xo_out, HBM), "dh_in": (dh, HBM), "vec": (one.vec_out, INV), "incS": (one.inc_out, INV), "tot": (one.tot_out, INV),
+    }
+    outs = {
+        "dmixed_out": ((tok, dm.cols), BF16, HBM), "dtail_out": ((nf, tok, F), F32, HBM), "vsum_out": ((nf, 4, dm.nseq, F), F32, INV),
+    }
+    scratch = {
+        "dmixed": V((tok, dm.cols), BF16), "xS": cV, "fS": cV, "cS": cV, "rS": cV, "cellS": cV, "drS": cV, "dhS": cV,
+        "bk": V((nf, ns, dm.nseq, F), F32), "bkS": V((nf, dm.nseq, F), F32),
+        "k_s": DMA((nf, ns)), "k_r": DMA((nf, ns)), "loc": DMA((nf, 6)), "out_sem": DMA((nf, 3)),
+    }
+    return launch(dm, "layer_one_back", 2, kernel_three, ins, outs, scratch)
+
+
+def kernel_grads(first, dm, r):
+    n = Net(dm)
+    nb, ns, nf, inner, outer, R, q, tok = dm.nb, dm.ns, dm.nf, dm.inner, dm.outer, dm.rows, dm.q, dm.tok
+    b, s, z, y = n.b, n.s, n.z, n.y
+    base = 0 if first else 5
+    NT = nb
+    TR = tok // NT
+    H = 2
+    HC = dm.cols // H
+    loads = [local_copy(r.dm_in, r.dmS, r.loc.at[0]), local_copy(r.w_in, r.wS, r.loc.at[1])]
+    n_load = local_copy(r.normed_in, r.nS, r.loc.at[2])
+    for c in loads:
+        c.wait()
+
+    def part(quarter, k):
+        return lax.dot_general(
+            r.dmS[k * TR : (k + 1) * TR, :], r.wS[quarter], (((1,), (1,)), ((), ())), preferred_element_type=F32
+        )
+
+    def to_sib(buf, got, k, i):
+        return remote(buf.at[k], got.at[k], r.p_s.at[i, k], r.p_r.at[i, k], (n.sib, s))
+
+    def to_across(k):
+        return remote(r.pb.at[k], r.prb.at[k], r.p_s.at[1, k], r.p_r.at[1, k], (n.across, s))
+
+    def stage_a(k):
+        r.pa[k] = part(n.diag, k).astype(BF16)
+        to_sib(r.pa, r.pra, k, 0).start()
+
+    def stage_b(k):
+        v = part(n.across, k)
+        arrived(r.pra.at[k], r.p_r.at[0, k], (n.sib, s))
+        r.pb[k] = (v + r.pra[k].astype(F32)).astype(BF16)
+        to_across(k).start()
+
+    def stage_c(k):
+        to_sib(r.pa, r.pra, k, 0).wait_send()
+        r.pa[k] = part(n.sib, k).astype(BF16)
+        to_sib(r.pa, r.prc, k, 2).start()
+
+    def stage_d(k):
+        r.acc[k * TR : (k + 1) * TR, :] = part(b, k)
+
+    def stage_e(k):
+        arrived(r.prc.at[k], r.p_r.at[2, k], (n.sib, s))
+        arrived(r.prb.at[k], r.p_r.at[1, k], (n.across, s))
+        rows = slice(k * TR, (k + 1) * TR)
+        r.acc[rows, :] = r.acc[rows, :] + r.prc[k].astype(F32) + r.prb[k].astype(F32)
+
+    def strip(bb, h, pos):
+        return r.wg.at[bb, pl.ds(pl.multiple_of(pos * R, R), R), pl.ds(h * HC, HC)]
+
+    def wgrad(bb, h):
+        r.wg[bb, :, h * HC : (h + 1) * HC] = lax.dot_general(
+            r.nS[:, bb * q : (bb + 1) * q], r.dmS[:, h * HC : (h + 1) * HC], (((0,), (0,)), ((), ())), preferred_element_type=F32
+        ).astype(BF16)
+
+    def y_copy(ch, j, o):
+        bb, h = ch // H, ch % H
+        p = lax.rem(y + j, inner)
+        return remote(strip(bb, h, o * inner + p), r.yr.at[ch, inner - j - 1, o], r.y_s.at[ch, j - 1, o], r.y_r.at[ch, inner - j - 1, o], (b, z * inner + p))
+
+    def z_copy(ch, j):
+        p = lax.rem(z + j, outer)
+        return remote(r.zs.at[ch, p], r.zr.at[ch, outer - j - 1], r.z_s.at[ch, j - 1], r.z_r.at[ch, outer - j - 1], (b, p * inner + y))
+
+    def f_copy(ch):
+        bb, h = ch // H, ch % H
+        return remote(r.fs.at[ch], r.fr.at[b, h], r.f_s.at[ch], r.f_r.at[b, h], (bb, s))
+
+    def rs_start(ch):
+        wgrad(ch // H, ch % H)
+        for j in range(1, inner):
+            for o in range(outer):
+                y_copy(ch, j, o).start()
+
+    def rs_mid(ch):
+        bb, h = ch // H, ch % H
+        for j in range(1, inner):
+            for o in range(outer):
+                arrived(r.yr.at[ch, j - 1, o], r.y_r.at[ch, j - 1, o], (b, s))
+        for jz in range(outer):
+            o = lax.rem(z + jz, outer)
+            pos = pl.ds(pl.multiple_of((o * inner + y) * R, R), R)
+            total = r.wg[bb, pos, h * HC : (h + 1) * HC].astype(F32)
+            for j in range(1, inner):
+                total = total + r.yr[ch, j - 1, o].astype(F32)
+            r.zs[ch, o] = total.astype(BF16)
+            if jz:
+                z_copy(ch, jz).start()
+
+    def rs_last(ch):
+        bb, h = ch // H, ch % H
+        for j in range(1, outer):
+            arrived(r.zr.at[ch, j - 1], r.z_r.at[ch, j - 1], (b, s))
+        total = r.zs[ch, z].astype(F32)
+        for j in range(1, outer):
+            total = total + r.zr[ch, j - 1].astype(F32)
+        r.fs[ch] = total.astype(BF16)
+
+        @pl.when(b != bb)
+        def _():
+            f_copy(ch).start()
+
+        @pl.when(b == bb)
+        def _():
+            r.fr[b, h] = r.fs[ch]
+
+    NCH = nb * H
+    stage_a(0)
+    stage_a(1)
+    n_load.wait()
+    rs_start(0)
+    for k in range(NT):
+        if k + 2 < NT:
+            stage_a(k + 2)
+        stage_b(k)
+    rs_start(1)
+    rs_start(2)
+    for k in range(NT):
+        stage_c(k)
+        stage_d(k)
+    rs_start(3)
+    rs_mid(0)
+    rs_start(4)
+    rs_start(5)
+    rs_mid(1)
+    rs_start(6)
+    rs_start(7)
+    rs_last(0)
+    rs_mid(2)
+    rs_last(1)
+    for k in range(NT):
+        stage_e(k)
+    rs_mid(3)
+
+    NTILE = tok // F
+
+    def fetch(i, slot):
+        rows = pl.ds(pl.multiple_of(i * F, F), F)
+        return [
+            pltpu.make_async_copy(r.x_in.at[:, rows], r.xt.at[slot], r.tile_sem.at[slot, 0]),
+            pltpu.make_async_copy(r.dtail_in.at[:, rows], r.dt.at[slot], r.tile_sem.at[slot, 1]),
+            pltpu.make_async_copy(r.mu_in.at[rows], r.mt.at[slot], r.tile_sem.at[slot, 2]),
+            pltpu.make_async_copy(r.rstd_in.at[rows], r.rt.at[slot], r.tile_sem.at[slot, 3]),
+        ]
+
+    def tiles(body, init):
+        for c in fetch(0, 0):
+            c.start()
+
+        def step(i, carry):
+            slot = lax.rem(i, 2)
+
+            @pl.when(i + 1 < NTILE)
+            def _():
+                for c in fetch(i + 1, 1 - slot):
+                    c.start()
+
+            for c in fetch(i, slot):
+                c.wait()
+            return body(i, slot, carry)
+
+        return lax.fori_loop(0, NTILE, step, init)
+
+    gains = [vrow(dm, r, n, base, fc) for fc in range(nf)]
+
+    def stats(i, slot, sums):
+        rows = pl.ds(pl.multiple_of(i * F, F), F)
+        t1, t2 = jnp.zeros((F, F), F32), jnp.zeros((F, F), F32)
+        new = []
+        for fc in range(nf):
+            xhat = (r.xt[slot, fc] - r.mt[slot]) * r.rt[slot]
+            dn = r.acc[rows, fc * F : (fc + 1) * F]
+            dx = dn * gains[fc]
+            t1 = t1 + dx
+            t2 = t2 + dx * xhat
+            new.append(sums[fc] + jnp.sum((dn * xhat).reshape(F // 8, 8, F), axis=0))
+        r.st[b, 0, pl.ds(i, 1), :] = jnp.sum(t1.T, axis=0, keepdims=True)
+        r.st[b, 1, pl.ds(i, 1), :] = jnp.sum(t2.T, axis=0, keepdims=True)
+        return tuple(new)
+
+    sums = tiles(stats, tuple(jnp.zeros((8, F), F32) for _ in range(nf)))
+    for fc in range(nf):
+        r.gsum[fc] = sums[fc]
+    for p in n.batch_peers:
+        remote(r.st.at[b], r.st.at[b], r.st_s.at[p], r.st_r.at[b], (p, s)).start()
+    rs_mid(4)
+    rs_last(2)
+    for p in n.batch_peers:
+        arrived(r.st.at[p], r.st_r.at[p], (p, s))
+    for k in range(2):
+        total = r.st[0, k]
+        for j in range(1, nb):
+            total = total + r.st[j, k]
+        r.stt[k] = total * (1.0 / dm.d)
+
+    for k in range(NT):
+        to_across(k).wait_send()
+
+    def final(i, slot, carry):
+        rows = pl.ds(pl.multiple_of(i * F, F), F)
+        m1 = jnp.broadcast_to(r.stt[0, pl.ds(i, 1), :], (F, F)).T
+        m2 = jnp.broadcast_to(r.stt[1, pl.ds(i, 1), :], (F, F)).T
+        for fc in range(nf):
+            xhat = (r.xt[slot, fc] - r.mt[slot]) * r.rt[slot]
+            dx = r.acc[rows, fc * F : (fc + 1) * F] * gains[fc]
+            out = r.dt[slot, fc] + r.rt[slot] * (dx - m1 - xhat * m2)
+            if first:
+                per = TR // F
+                r.pb[i // per, pl.ds(pl.multiple_of(lax.rem(i, per) * F, F), F), fc * F : (fc + 1) * F] = out.astype(BF16)
+            else:
+                r.acc[rows, fc * F : (fc + 1) * F] = out
+        return carry
+
+    tiles(final, 0)
+    pend = []
+    if first:
+        for p in n.batch_peers:
+            remote(r.pb.at[p], r.fin.at[b], r.g_s.at[p], r.g_r.at[b], (p, s)).start()
+        r.fin[b] = r.pb[b]
+        vector_start(dm, r, n)
+    else:
+        pend.append(local_copy(r.acc, r.dx_out, r.loc.at[0]))
+        r.gsum_out[...] = r.gsum[...]
+    rs_mid(5)
+    rs_last(3)
+    rs_mid(6)
+    rs_last(4)
+    rs_mid(7)
+    rs_last(5)
+    if first:
+        for k in range(nb):
+            @pl.when(k != b)
+            def _(k=k):
+                arrived(r.fin.at[k], r.g_r.at[k], (b, s))
+
+            r.acc[k * TR : (k + 1) * TR, :] = r.fin[k].astype(F32)
+            pend.append(local_copy(r.acc.at[pl.ds(k * TR, TR)], r.dx_out.at[:, pl.ds(k * q, q)], r.loc.at[3 + k]))
+        vector_finish(dm, r, n)
+    rs_last(6)
+    rs_last(7)
+    for p in n.batch_peers:
+        for h in range(H):
+            arrived(r.fr.at[p, h], r.f_r.at[p, h], (p, s))
+    for k in range(nb):
+        for fc in range(nf):
+            h, o = (fc * G3) // HC, (fc * G3) % HC
+            for gate in range(3):
+                to = gate * dm.d + k * q + fc * F
+                r.wg_out[:, to : to + F] = r.fr[k, h, :, o + gate * F : o + (gate + 1) * F].astype(F32)
+    for c in pend:
+        c.wait()
+    for k in range(NT):
+        to_sib(r.pa, r.prc, k, 2).wait_send()
+    for p in n.batch_peers:
+        sent(r.st.at[b], r.st_s.at[p], (p, s))
+        if first:
+            sent(r.pb.at[p], r.g_s.at[p], (p, s))
+    for ch in range(NCH):
+        for j in range(1, inner):
+            for o in range(outer):
+                y_copy(ch, j, o).wait_send()
+        for j in range(1, outer):
+            z_copy(ch, j).wait_send()
+
+        @pl.when(b != ch // H)
+        def _(ch=ch):
+            f_copy(ch).wait_send()
+
+
+def vector_start(dm, r, n):
+    r.vg[n.s] = jnp.zeros((16, dm.q), F32)
+    for l, (vs, gs) in enumerate(((r.vsum0, r.gsum), (r.vsum1, r.gsum1))):
+        for fc in range(dm.nf):
+            cols = slice(fc * F, (fc + 1) * F)
+            r.vg[n.s, 5 * l : 5 * l + 1, cols] = jnp.sum(gs[fc], axis=0, keepdims=True)
+            for k in range(4):
+                r.vg[n.s, 5 * l + 1 + k : 5 * l + 2 + k, cols] = jnp.sum(vs[fc, k], axis=0, keepdims=True)
+    for p in n.seq_peers:
+        remote(r.vg.at[n.s], r.vg.at[n.s], r.v_s.at[p], r.v_r.at[n.s], (n.b, p)).start()
+
+
+def vector_finish(dm, r, n):
+    for p in n.seq_peers:
+        arrived(r.vg.at[p], r.v_r.at[p], (n.b, p))
+    total = r.vg[0]
+    for j in range(1, dm.ns):
+        total = total + r.vg[j]
+    r.vg_out[...] = total
+    for p in n.seq_peers:
+        sent(r.vg.at[n.s], r.v_s.at[p], (n.b, p))
+
+
+def call_grads(dm, first, w, normed, x, mu, rstd, vec, scans, more):
+    nb, ns, nf, inner, outer, R, q, tok = dm.nb, dm.ns, dm.nf, dm.inner, dm.outer, dm.rows, dm.q, dm.tok
+    TR, H = tok // nb, 2
+    HC, NCH = dm.cols // H, nb * H
+    ins = {
+        "dm_in": (scans.dmixed_out, HBM), "w_in": (w, HBM), "normed_in": (normed, HBM), "x_in": (x, HBM),
+        "dtail_in": (scans.dtail_out, HBM), "mu_in": (mu, HBM), "rstd_in": (rstd, HBM), "vec": (vec, INV),
+    }
+    outs = {"wg_out": ((R, 3 * dm.d), F32, INV)}
+    if first:
+        outs["dx_out"] = ((dm.local, dm.d), F32, HBM)
+        outs["vg_out"] = ((16, q), F32, INV)
+        ins.update({k: (v, INV) for k, v in more.items()})
+    else:
+        outs["dx_out"] = ((tok, q), F32, HBM)
+        outs["gsum_out"] = ((nf, 8, F), F32, INV)
+    bV = V((nb, TR, q), BF16)
+    scratch = {
+        "dmS": V((tok, dm.cols), BF16), "wS": V((nb, ns * R, dm.cols), BF16), "nS": V((tok, dm.d), BF16),
+        "acc": V((tok, q), F32), "pa": bV, "pra": bV, "pb": bV, "prb": bV, "prc": bV,
+        "wg": V((nb, ns * R, dm.cols), BF16), "yr": V((NCH, inner - 1, outer, R, HC), BF16),
+        "zs": V((NCH, outer, R, HC), BF16), "zr": V((NCH, outer - 1, R, HC), BF16),
+        "fs": V((NCH, R, HC), BF16), "fr": V((nb, H, R, HC), BF16),
+        "xt": V((2, nf, F, F), F32), "dt": V((2, nf, F, F), F32), "mt": V((2, F, F), F32), "rt": V((2, F, F), F32),
+        "st": V((nb, 2, tok // F, F), F32), "stt": V((2, tok // F, F), F32), "gsum": V((nf, 8, F), F32),
+        "loc": DMA((3 + nb,)), "tile_sem": DMA((2, 4)), "p_s": DMA((3, nb)), "p_r": DMA((3, nb)),
+        "y_s": DMA((NCH, inner - 1, outer)), "y_r": DMA((NCH, inner - 1, outer)),
+        "z_s": DMA((NCH, outer - 1)), "z_r": DMA((NCH, outer - 1)),
+        "f_s": DMA((NCH,)), "f_r": DMA((nb, H)), "st_s": DMA((nb,)), "st_r": DMA((nb,)),
+    }
+    if first:
+        scratch.update({"fin": bV, "g_s": DMA((nb,)), "g_r": DMA((nb,)), "vg": V((ns, 16, q), F32), "v_s": DMA((ns,)), "v_r": DMA((ns,))})
+    return launch(dm, "grads_one" if first else "grads_two", 3 if first else 4, functools.partial(kernel_grads, first), ins, outs, scratch)
+
+
+def prepare(dm, block_input, weight, vectors, cotangent):
+    D, nf, nb, R = dm.d, dm.nf, dm.nb, dm.rows
+    x = block_input.reshape(dm.local, D)
+    cot = cotangent.reshape(dm.local, D)
+    w = weight.reshape(dm.layers, R, 3, nb, nf, F).transpose(0, 3, 4, 1, 2, 5).reshape(dm.layers, nb, nf, R, G3)
+    s = lax.axis_index("seq")
+    v = jnp.pad(vectors.reshape(dm.layers * 5, R), ((0, 16 - dm.layers * 5), (0, 0)))
+    lane = lax.broadcasted_iota(jnp.int32, (16, F), 1) // R
+    v = jnp.where(lane == lax.rem(s, F // R), jnp.tile(v, (1, F // R)), 0.0)
+    return x, w, v, cot
+
+
+def tuned_body(nb, ns, block_input, weight, vectors, cotangent):
+    dm = Dims(nb, ns, block_input.shape, weight.shape)
+    one = call_one(dm, *prepare(dm, block_input, weight, vectors, cotangent))
+    two = call_two(dm, one)
+    g1 = call_grads(dm, False, one.wq1_out, two.normed_out, one.x1_out, two.mu_out, two.rstd_out, one.vec_out, two, {})
+    three = call_three(dm, one, g1.dx_out)
+    more = {"vsum0": three.vsum_out, "vsum1": two.vsum_out, "gsum1": g1.gsum_out}
+    g0 = call_grads(dm, True, one.wq0_out, one.normed_out, one.xo_out, one.mu_out, one.rstd_out, one.vec_out, three, more)
+    weight_grad = jnp.stack([g0.wg_out, g1.wg_out], axis=0)
+    s = lax.axis_index("seq")
+    mine = lax.dynamic_slice_in_dim(g0.vg_out, s * dm.rows, dm.rows, axis=1)[: dm.layers * 5]
+    vector_grad = mine.reshape(dm.layers, 5, dm.rows)
+    return (
+        two.block_out.reshape(block_input.shape), g0.dx_out.reshape(block_input.shape), weight_grad, vector_grad,
+    )
 
 
 def prefix(value, axis, join, neutral, backward):
@@ -72,7 +1103,7 @@
     return (cells, previous, reset)
 
 
-def body(block_input, weight, vectors, cotangent):
+def general_body(block_input, weight, vectors, cotangent):
     sequence_batch, time_steps, hidden_width = block_input.shape
     layers = weight.shape[0]
     params = lax.all_gather(vectors, ("batch", "seq"), axis=2, tiled=True)
@@ -175,6 +1206,8 @@
 
 
 def solution(mesh):
+    nb, ns = mesh.shape["batch"], mesh.shape["seq"]
+    body = functools.partial(tuned_body, nb, ns) if (nb, ns) == (4, 8) else general_body
     placed = (
         P("batch", "seq", None),
         P(None, ("batch", "seq"), None),

time: 2960 us -> 662 us (0.22); the launches traced: 2920 us -> 654 us
  local copies, waits for them, and re-layouts: 1120 us -> 16.1 us
  waiting for transfers between devices: 1000 us -> 0 us
  Pallas kernels: 0 us -> 632 us
  other arithmetic: 351 us -> 4.62 us
  blocking collectives: 283 us -> 0 us
  matrix products: 142 us -> 0 us
    reduce_scatter x2 -> x0, waiting for transfers between devices: 880 us -> none  [body(): lax.psum_scatter(weight_term(jnp.int32(0), rows * lax.axis_size(('batch',...]
    pallas_call x0 -> x5, Pallas kernels: none -> 632 us  [launch(): pl.pallas_call(run, out_shape=[jax.ShapeDtypeStruct(shape, dtype) for sha...]
    slice x216 -> x1, local copies, waits for them, and re-layouts: 604 us -> 0.77 us  [tuned_body(): lax.dynamic_slice_in_dim(g0.vg_out, s * dm.rows, dm.rows, axis=1)]
    all_gather x9 -> x0, blocking collectives: 283 us -> none  [the longest x8 192 us: prefix(): pieces = jax.tree.map(lambda part: lax.all_gather(part, axis), value)]
    pad x112 -> x1, local copies, waits for them, and re-layouts: 273 us -> 0.01 us  [prepare(): jnp.pad(vectors.reshape(dm.layers * 5, R), ((0, 16 - dm.layers * 5), (0,...]
    add x101 -> x0, other arithmetic: 182 us -> none  [the longest x36 61.6 us: body(): lax.associative_scan(compose, (jnp.flip(forget_gate, 1), jnp.flip(inject,...]
    dot_general x6 -> x0, matrix products: 142 us -> none  [the longest x2 49.6 us: weight_term(): lax.dot_general(normed_input, dmixed, (((0,), (0,)), ((), ())), preferred...]
    rev x8 -> x0, local copies, waits for them, and re-layouts: 131 us -> none  [the longest x2 65.3 us: body(): back_gates = jnp.flip(back_gates, 1)]
  transfers between devices with their start and end apart: 5 -> 0, of which waited for: 4 -> 0; matrix products, arithmetic and copies ran while one was open for 17% -> 0% of each run, Pallas kernels for 0% -> 0%
where the time goes in v2:
time: 662 us; the launch traced here: 654 us
  Pallas kernels  632 us (95%)
  local copies, waits for them, and re-layouts  16.1 us (2%)
    pallas_call x5, Pallas kernels, launch(): pl.pallas_call(run, out_shape=[jax.ShapeDtypeStruct(shape, dtype) for sha...  632 us

profile of v2, /device:TPU:11, one launch (start us, length us, event | category | flops | bytes accessed | tf_op | source)
XLA Modules:
  0.0 654.1 jit_solution(3476252214307043524)
XLA Ops:
  0.7 0.7 copy.11
  1.4 0.1 tile.10
  1.5 0.6 fusion.refs_2_
  2.1 4.5 reshape.37
  6.6 2.5 copy.14
  9.2 2.5 reshape.38.refs_1_
  11.7 183.5 %forward_one.1 = (bf16[2048,2048]{1,0:T(8,128)(2,1)}, bf16[4,512,1536]{2,1,0:T(8,128)(2,1)}, bf16[4,512,1536]{2,1,0:T(8,128)(2,1)}, bf16[4,512,512]{2,1,0:T(8,12...) custom-call(bf16[512,2048]{1,0:T(8,128)(2,1)} %bitcast.11, ...), custom_call_target="tpu_custom_call" | custom-call | tf_op jit(solution)/shard_map/forward_one/pallas_call | solution.py:89
  195.2 134.4 %layer_two.1 = (bf16[2048,2048]{1,0:T(8,128)(2,1)}, bf16[512,2048]{1,0:T(8,128)(2,1)}, bf16[2048,1536]{1,0:T(8,128)(2,1)}, f32[4,2048,128]{2,1,0:T(8,128)}, f32[...) custom-call(bf16[4,512,1536]{2,1,0:T(8,128)(2,1)} %get-tuple-element.36.refs_0_.refs_1_, ...), custom_call_target="tpu_custom_call" | custom-call | tf_op jit(solution)/shard_map/layer_two/pallas_call | solution.py:89
  329.6 121.5 %grads_two.1 = (f32[64,6144]{1,0:T(8,128)}, f32[2048,512]{1,0:T(8,128)}, f32[4,8,128]{2,1,0:T(8,128)}) custom-call(bf16[2048,1536]{1,0:T(8,128)(2,1)} %get-tuple-element.47.refs_0_, bf16[4,512,1536]{2,1,0:T(8,128)(2,1)} %get-tuple-element.36.refs_0_.refs_1_, bf16[2048,2048]{1,0:T(8,128)(2,1)} %get-tuple-element.48.refs_2_, ...), custom_call_target="tpu_custom_call" | custom-call | tf_op jit(solution)/shard_map/grads_two/pallas_call | solution.py:89
  451.0 69.7 %layer_one_back.1 = (bf16[2048,1536]{1,0:T(8,128)(2,1)}, f32[4,2048,128]{2,1,0:T(8,128)}, f32[4,4,8,128]{3,2,1,0:T(8,128)}) custom-call(f32[4,2048,128]{2,1,0:T(8,128)} %get-tuple-element.42.refs_0_, f32[4,2048,128]{2,1,0:T(8,128)} %get-tuple-element.43.refs_1_, f32[4,2048,128]{2,1,0:T(8,128)} %get-tuple-element.44.refs_2_, ...), custom_call_target="tpu_custom_call" | custom-call | tf_op jit(solution)/shard_map/layer_one_back/pallas_call | solution.py:89
  520.8 123.4 %grads_one.1 = (f32[64,6144]{1,0:T(8,128)}, f32[512,2048]{1,0:T(8,128)}, f32[16,512]{1,0:T(8,128)}) custom-call(bf16[2048,1536]{1,0:T(8,128)(2,1)} %get-tuple-element.55.refs_0_, bf16[4,512,1536]{2,1,0:T(8,128)(2,1)} %get-tuple-element.56.refs_1_, bf16[2048,2048]{1,0:T(8,128)(2,1)} %get-tuple-element.57.refs_2_, ...), custom_call_target="tpu_custom_call" | custom-call | tf_op jit(solution)/shard_map/grads_one/pallas_call | solution.py:89
  644.1 0.0 copy-start.1
  644.2 4.0 pad_maximum_fusion
  648.2 0.8 constant_dynamic-slice_fusion
  648.9 0.0 copy-start
  648.9 0.6 copy.12
  649.5 0.0 copy-done.1
  649.5 1.3 copy.17
  650.9 1.0 copy-done
  651.9 2.0 copy.18
  (6 shorter events, 0.0 us)
Async XLA Ops:
  644.1 5.4 copy-start.1
  648.9 3.0 copy-start

commit v3 on v0

--- a/solution.py
+++ b/solution.py
@@ -1,9 +1,1385 @@
+import functools
+import types
+
 import jax
 import jax.numpy as jnp
 from jax import lax
+from jax.experimental import pallas as pl
+from jax.experimental.pallas import tpu as pltpu
 from jax.sharding import PartitionSpec as P
 
+MESH = pl.DeviceIdType.MESH
+F32, BF16 = jnp.float32, jnp.bfloat16
+V, DMA = pltpu.VMEM, pltpu.SemaphoreType.DMA
 epsilon = 1e-05
+F = 128
+HBM = pl.BlockSpec(memory_space=pl.ANY)
+INV = None
+
+
+class Dims:
+    def __init__(self, nb, ns, x_shape, w_shape):
+        self.nb, self.ns = nb, ns
+        self.inner = 2
+        self.outer = ns // 2
+        self.sb, self.steps, self.d = x_shape
+        self.local = self.sb * self.steps
+        self.runs = 8
+        self.stretch = self.runs // self.sb
+        self.length = self.local // self.runs
+        self.tok = self.local * nb
+        self.q = self.d // nb
+        self.nf = self.q // F
+        self.on_time = 10
+        self.early = 2
+        self.layers, self.rows = w_shape[0], w_shape[1]
+
+
+class Net:
+    def __init__(self, dm):
+        nb, ns, inner, outer = dm.nb, dm.ns, dm.inner, dm.outer
+        self.b, self.s = lax.axis_index("batch"), lax.axis_index("seq")
+        b, s = self.b, self.s
+        self.z, self.y = s // inner, lax.rem(s, inner)
+        self.across, self.sib, self.diag = b ^ 2, b ^ 1, b ^ 3
+        self.batch_peers = [lax.rem(b + j, nb) for j in range(1, nb)]
+        self.outer_peers = [lax.rem(self.z + j, outer) for j in range(1, outer)]
+        self.inner_peers = [lax.rem(self.y + j, inner) for j in range(1, inner)]
+        self.seq_peers = [lax.rem(s + j, ns) for j in range(1, ns)]
+        barrier = pltpu.get_barrier_semaphore()
+        for p in self.batch_peers:
+            pl.semaphore_signal(barrier, inc=1, device_id=(p, s), device_id_type=MESH)
+        for p in self.seq_peers:
+            pl.semaphore_signal(barrier, inc=1, device_id=(b, p), device_id_type=MESH)
+        self.count = nb - 1 + ns - 1
+
+    def ready(self):
+        pl.semaphore_wait(pltpu.get_barrier_semaphore(), self.count)
+
+
+def remote(src, dst, ssem, rsem, dev):
+    return pltpu.make_async_remote_copy(
+        src_ref=src, dst_ref=dst, send_sem=ssem, recv_sem=rsem, device_id=dev, device_id_type=MESH
+    )
+
+
+def arrived(dst, rsem, dev):
+    remote(dst, dst, rsem, rsem, dev).wait_recv()
+
+
+def sent(src, ssem, dev):
+    remote(src, src, ssem, ssem, dev).wait_send()
+
+
+def local_copy(src, dst, sem):
+    c = pltpu.make_async_copy(src, dst, sem)
+    c.start()
+    return c
+
+
+def at128(v):
+    return pl.multiple_of(v, F)
+
+
+def sigmoid(v):
+    return 1.0 / (1.0 + jnp.exp(jnp.minimum(-v, 80.0)))
+
+
+def launch(dm, name, cid, kernel, ins, outs, scratch):
+    keep_in = [k for k, (_, kind) in ins.items() if kind is INV]
+    keep_out = [k for k, (_, _, kind) in outs.items() if kind is INV]
+    names = [k + ("_far" if k in keep_in else "") for k in ins] + [k + ("_far" if k in keep_out else "") for k in outs]
+    scratch = dict(scratch)
+    for k in keep_in:
+        scratch[k] = V(ins[k][0].shape, ins[k][0].dtype)
+    for k in keep_out:
+        scratch[k] = V(outs[k][0], outs[k][1])
+    scratch["keep_sem"] = DMA((len(keep_in) + len(keep_out) + 1,))
+    names += list(scratch)
+
+    def run(*refs):
+        r = types.SimpleNamespace(**dict(zip(names, refs)))
+        far = vars(r)
+        loads = {k: local_copy(far[k + "_far"], far[k], r.keep_sem.at[i]) for i, k in enumerate(keep_in)}
+        stores = []
+
+        def need(*which):
+            for k in which:
+                loads.pop(k).wait()
+
+        def store(k):
+            stores.append(local_copy(far[k], far[k + "_far"], r.keep_sem.at[len(keep_in) + keep_out.index(k)]))
+
+        r.need, r.store = need, store
+        kernel(dm, r)
+        for c in stores:
+            c.wait()
+
+    got = pl.pallas_call(
+        run,
+        out_shape=[jax.ShapeDtypeStruct(shape, dtype) for shape, dtype, _ in outs.values()],
+        in_specs=[HBM for _ in ins],
+        out_specs=[HBM for _ in outs],
+        scratch_shapes=list(scratch.values()),
+        compiler_params=pltpu.CompilerParams(collective_id=cid, has_side_effects=True, vmem_limit_bytes=63 * 2**20),
+        name=name,
+    )(*[array for array, _ in ins.values()])
+    return types.SimpleNamespace(**dict(zip(outs, got)))
+
+
+def norm_rows(x, gain):
+    mu = jnp.mean(x, axis=-1, keepdims=True)
+    xc = x - mu
+    rstd = lax.rsqrt(jnp.mean(xc * xc, axis=-1, keepdims=True) + epsilon)
+    return mu, rstd, (xc * rstd * gain).astype(BF16)
+
+
+def vrow(dm, r, n, k, fc):
+    return r.vec[k : k + 1, pl.ds(at128(n.b * dm.q + fc * F), F)]
+
+
+def products(dm, r, n, w, chunks, base, pieces):
+    TM = 256
+
+    def step(first, i, carry):
+        rows = pl.ds(pl.multiple_of(first + i * TM, TM), TM)
+        right = jnp.concatenate(
+            [w[fc, g].reshape(dm.d, F) for fc in chunks for g in range(3)], axis=1
+        )
+        m = jnp.dot(r.normed[rows, :], right, preferred_element_type=F32)
+        for k, fc in enumerate(chunks):
+            o = 3 * k * F
+            vf, bf, br = [vrow(dm, r, n, base + j, fc) for j in (1, 2, 4)]
+            r.fS[fc, rows, :] = sigmoid(m[:, o + F : o + 2 * F] + vf * r.xS[fc, rows, :] + bf)
+            r.cS[fc, rows, :] = m[:, o : o + F]
+            r.rS[fc, rows, :] = m[:, o + 2 * F : o + 3 * F] + br
+        return carry
+
+    if pieces is None:
+        lax.fori_loop(0, dm.tok // TM, functools.partial(step, 0), 0)
+    else:
+        for g, part in pieces:
+            step(g * dm.local, part, 0)
+
+
+def at_time(dm, g, t):
+    return pl.ds(pl.multiple_of(g * dm.local + t * dm.runs, dm.runs), dm.runs)
+
+
+def run_index(dm):
+    return lax.rem(lax.broadcasted_iota(jnp.int32, (dm.runs, F), 0), dm.stretch)
+
+
+def turn(v, by):
+    return pltpu.roll(v, by % v.shape[0], 0)
+
+
+def pack(dm, parts, end):
+    row = lax.broadcasted_iota(jnp.int32, (dm.runs, F), 0)
+    out = jnp.zeros((dm.runs, F), F32)
+    for g in range(dm.nb):
+        for j in range(dm.sb):
+            to = g * dm.sb + j
+            out = jnp.where(row == to, turn(parts[g], to - (j * dm.stretch + end)), out)
+    return out
+
+
+def unpack(dm, packed, g, end):
+    row = lax.broadcasted_iota(jnp.int32, (dm.runs, F), 0)
+    out = jnp.zeros((dm.runs, F), F32)
+    for j in range(dm.sb):
+        to = j * dm.stretch + end
+        out = jnp.where(row == to, turn(packed, to - (g * dm.sb + j)), out)
+    return out
+
+
+def enter(dm, a, v, first, back):
+    start = dm.stretch - 1 if back else 0
+    index = run_index(dm)
+    state = first
+    for _ in range(dm.stretch - 1):
+        state = jnp.where(index == start, first, turn(a * state + v, -1 if back else 1))
+    return state
+
+
+def scan_totals(dm, r, n, fc):
+    groups = range(dm.nb)
+
+    def step(t, carry):
+        new = []
+        for g in groups:
+            a, v = carry[g]
+            at = at_time(dm, g, t)
+            f, cand = r.fS[fc, at, :], r.cS[fc, at, :]
+            new.append((a * f, cand + f * (v - cand)))
+        return tuple(new)
+
+    one, zero = jnp.ones((dm.runs, F), F32), jnp.zeros((dm.runs, F), F32)
+    got = lax.fori_loop(0, dm.length, step, tuple((one, zero) for _ in groups), unroll=4)
+    index = run_index(dm)
+    for_a, for_v = [], []
+    for g in groups:
+        a, v = got[g]
+        r.runA[fc, g] = a
+        r.runV[fc, g] = v
+        product = a
+        for _ in range(dm.stretch - 1):
+            product = jnp.where(index == 0, a, a * turn(product, 1))
+        for_a.append(product)
+        for_v.append(a * enter(dm, a, v, zero, False) + v)
+    a, v = pack(dm, for_a, dm.stretch - 1), pack(dm, for_v, dm.stretch - 1)
+    r.totS[fc, 0] = a
+    r.totS[fc, 1] = v
+    r.tot[fc, n.s, 0] = a
+    r.tot[fc, n.s, 1] = v
+    for p in n.seq_peers:
+        remote(r.totS.at[fc], r.tot.at[fc, n.s], r.t_s.at[fc, p], r.t_r.at[fc, n.s], (n.b, p)).start()
+
+
+def scan_finish(dm, r, n, fc, base):
+    for p in n.seq_peers:
+        arrived(r.tot.at[fc, p], r.t_r.at[fc, p], (n.b, p))
+    vr = vrow(dm, r, n, base + 3, fc)
+
+    def fold(j, c):
+        return jnp.where(j < n.s, r.tot[fc, j, 0] * c + r.tot[fc, j, 1], c)
+
+    packed = lax.fori_loop(0, dm.ns, fold, jnp.zeros((dm.runs, F), F32))
+    entering = []
+    for g in range(dm.nb):
+        e = enter(dm, r.runA[fc, g], r.runV[fc, g], unpack(dm, packed, g, 0), False)
+        r.incS[fc, g] = e
+        entering.append(e)
+
+    def step(t, carry):
+        new = []
+        for g in range(dm.nb):
+            prev = carry[g]
+            at = at_time(dm, g, t)
+            f, cand, x = r.fS[fc, at, :], r.cS[fc, at, :], r.xS[fc, at, :]
+            reset = sigmoid(r.rS[fc, at, :] + vr * prev)
+            c = cand + f * (prev - cand)
+            r.cellS[fc, at, :] = c
+            r.rS[fc, at, :] = reset
+            r.hS[fc, at, :] = x + reset * (c - x)
+            new.append(c)
+        return tuple(new)
+
+    lax.fori_loop(0, dm.length, step, tuple(entering), unroll=2)
+
+
+def totals_sent(dm, r, n):
+    for fc in range(dm.nf):
+        for p in n.seq_peers:
+            sent(r.totS.at[fc], r.t_s.at[fc, p], (n.b, p))
+
+
+def back_totals(dm, r, n, fc, base):
+    vr = vrow(dm, r, n, base + 3, fc)
+    zero = jnp.zeros((dm.runs, F), F32)
+
+    def step(i, carry):
+        new = []
+        for g in range(dm.nb):
+            at = at_time(dm, g, dm.length - 1 - i)
+            reset, dh = r.rS[fc, at, :], r.dhS[fc, at, :]
+            direct = dh * reset
+            dreset = (r.cellS[fc, at, :] - r.xS[fc, at, :]) * direct * (1.0 - reset)
+            r.rS[fc, at, :] = direct
+            r.drS[fc, at, :] = dreset
+            new.append(r.fS[fc, at, :] * (direct + carry[g]) + dreset * vr)
+        return tuple(new)
+
+    got = lax.fori_loop(0, dm.length, step, tuple(zero for _ in range(dm.nb)), unroll=2)
+    parts = []
+    for g in range(dm.nb):
+        a, v = r.runA[fc, g], got[g]
+        r.backV[fc, g] = v
+        parts.append(a * enter(dm, a, v, zero, True) + v)
+    v = pack(dm, parts, 0)
+    r.bkS[fc] = v
+    r.bk[fc, n.s] = v
+    for p in n.seq_peers:
+        remote(r.bkS.at[fc], r.bk.at[fc, n.s], r.k_s.at[fc, p], r.k_r.at[fc, n.s], (n.b, p)).start()
+
+
+def back_finish(dm, r, n, fc, base):
+    for p in n.seq_peers:
+        arrived(r.bk.at[fc, p], r.k_r.at[fc, p], (n.b, p))
+    vf, vr = vrow(dm, r, n, base + 1, fc), vrow(dm, r, n, base + 3, fc)
+
+    def fold(i, c):
+        j = dm.ns - 1 - i
+        return jnp.where(j > n.s, r.tot[fc, j, 0] * c + r.bk[fc, j], c)
+
+    zero = jnp.zeros((dm.runs, F), F32)
+    packed = lax.fori_loop(0, dm.ns, fold, zero)
+    carries = [
+        enter(dm, r.runA[fc, g], r.backV[fc, g], unpack(dm, packed, g, dm.stretch - 1), True) for g in range(dm.nb)
+    ]
+
+    def one(at, prev, carry, sums):
+        s1, s2, s3, s4 = sums
+        f, cand, x = r.fS[fc, at, :], r.cS[fc, at, :], r.xS[fc, at, :]
+        direct, dreset = r.rS[fc, at, :], r.drS[fc, at, :]
+        dcell = direct + carry
+        dcand = dcell * (1.0 - f)
+        dforget = dcand * f * (prev - cand)
+        r.cS[fc, at, :] = dcand
+        r.fS[fc, at, :] = dforget
+        r.rS[fc, at, :] = r.dhS[fc, at, :] - direct + dforget * vf
+        return f * dcell + dreset * vr, (s1 + dforget * x, s2 + dforget, s3 + dreset * prev, s4 + dreset)
+
+    def step(i, state):
+        t = dm.length - 1 - i
+        carry, sums = state
+        new = []
+        for g in range(dm.nb):
+            c, sums = one(at_time(dm, g, t), r.cellS[fc, at_time(dm, g, t - 1), :], carry[g], sums)
+            new.append(c)
+        return tuple(new), sums
+
+    carry, sums = lax.fori_loop(0, dm.length - 1, step, (tuple(carries), (zero, zero, zero, zero)), unroll=3)
+    for g in range(dm.nb):
+        _, sums = one(at_time(dm, g, 0), r.incS[fc, g], carry[g], sums)
+    for k in range(4):
+        r.vsum_out[fc, k] = sums[k]
+    for g, part in enumerate((r.cS, r.fS, r.drS)):
+        r.dmixed[fc, g] = part[fc].astype(BF16)
+
+
+def back_sent(dm, r, n):
+    for fc in range(dm.nf):
+        for p in n.seq_peers:
+            sent(r.bkS.at[fc], r.k_s.at[fc, p], (n.b, p))
+
+
+def back_outputs(dm, r, fc):
+    return [
+        local_copy(r.dmixed.at[fc], r.dmixed_out.at[fc], r.out_sem.at[fc, 0]),
+        local_copy(r.rS.at[fc], r.dtail_out.at[fc], r.out_sem.at[fc, 1]),
+    ]
+
+
+class Gather:
+    def __init__(self, dm, n, r, l, w):
+        self.dm, self.n, self.r, self.l, self.w = dm, n, r, l, w
+
+    def strip(self, fc, pos):
+        R = self.dm.rows
+        return self.w.at[fc, :, :, pl.ds(pl.multiple_of(pos * R, R), R)]
+
+    def piece(self, fc, b, gates=slice(0, 3)):
+        n, R = self.n, self.dm.rows
+        return self.w.at[fc, gates, b, pl.ds(pl.multiple_of(n.s * R, R), R)]
+
+    def source(self, fc, p, gate):
+        dm = self.dm
+        return self.r.w_in.at[self.l, :, pl.ds(at128(gate * dm.d + p * dm.q + fc * F), F)]
+
+    def own(self, fc):
+        r, l, b = self.r, self.l, self.n.b
+        return [local_copy(self.source(fc, b, g), self.piece(fc, b, g), r.own_sem.at[l, fc, g]) for g in range(3)]
+
+    def pre(self, fc):
+        n, r, l = self.n, self.r, self.l
+        for p in n.batch_peers:
+            for g in range(3):
+                remote(
+                    self.source(fc, p, g), self.piece(fc, n.b, g), r.pre_s.at[l, fc, p], r.pre_r.at[l, fc, n.b], (p, n.s)
+                ).start()
+
+    def hop(self, fc, src, to):
+        n, r, l, dm = self.n, self.r, self.l, self.dm
+        at = self.strip(fc, src * dm.inner + n.y)
+        side = 1 if to > 0 else 0
+        return remote(at, at, r.z_s.at[l, fc, src, side], r.z_r.at[l, fc, src], (n.b, (n.z + to) * dm.inner + n.y))
+
+    def to_inner(self, fc, src):
+        n, r, l, dm = self.n, self.r, self.l, self.dm
+        at = self.strip(fc, src * dm.inner + n.y)
+        return [
+            remote(at, at, r.y_s.at[l, fc, src, p], r.y_r.at[l, fc, src, n.y], (n.b, n.z * dm.inner + p))
+            for p in n.inner_peers
+        ]
+
+    def start(self, fc, inner=True):
+        n, r, l, dm = self.n, self.r, self.l, self.dm
+        for p in n.batch_peers:
+            arrived(self.piece(fc, p), r.pre_r.at[l, fc, p], (p, n.s))
+        pl.when(n.z < dm.outer - 1)(lambda: self.hop(fc, n.z, 1).start())
+        pl.when(n.z > 0)(lambda: self.hop(fc, n.z, -1).start())
+        if inner:
+            for c in self.to_inner(fc, n.z):
+                c.start()
+
+    def step(self, fc, h, inner=True):
+        n, r, l, dm = self.n, self.r, self.l, self.dm
+        for way in (-1, 1):
+            src = n.z + way * h
+            has = (src >= 0) if way < 0 else (src < dm.outer)
+            on = (n.z < dm.outer - 1) if way < 0 else (n.z > 0)
+
+            def take(src=src, on=on, way=way):
+                at = self.strip(fc, src * dm.inner + n.y)
+                arrived(at, r.z_r.at[l, fc, src], (n.b, n.s))
+                pl.when(on)(lambda: self.hop(fc, src, -way).start())
+                if inner:
+                    for c in self.to_inner(fc, src):
+                        c.start()
+
+            pl.when(has)(take)
+
+    def complete(self, fc):
+        n, r, l, dm = self.n, self.r, self.l, self.dm
+        for o in range(dm.outer):
+            for p in n.inner_peers:
+                arrived(self.strip(fc, o * dm.inner + p), r.y_r.at[l, fc, o, p], (n.b, n.s))
+
+    def drain_inner(self, fc):
+        for o in range(self.dm.outer):
+            for p in self.n.inner_peers:
+                sent(self.strip(fc, self.n.s), self.r.y_s.at[self.l, fc, o, p], (self.n.b, self.n.s))
+
+    def drain(self, fc, inner=True):
+        n, r, l, dm = self.n, self.r, self.l, self.dm
+        if inner:
+            self.drain_inner(fc)
+        for p in n.batch_peers:
+            sent(self.piece(fc, p), r.pre_s.at[l, fc, p], (p, n.s))
+        for o in range(dm.outer):
+            right = jnp.logical_and(o <= n.z, n.z < dm.outer - 1)
+            left = jnp.logical_and(o >= n.z, n.z > 0)
+            for ok, side in ((right, 1), (left, 0)):
+                pl.when(ok)(lambda o=o, side=side: sent(self.strip(fc, n.s), r.z_s.at[l, fc, o, side], (n.b, n.s)))
+
+
+def kernel_one(dm, r):
+    n = Net(dm)
+    nb, ns, nf, inner, outer, R = dm.nb, dm.ns, dm.nf, dm.inner, dm.outer, dm.rows
+    b, s, z, y = n.b, n.s, n.z, n.y
+    w0, w1 = Gather(dm, n, r, 0, r.wq0), Gather(dm, n, r, 1, r.wq1_out)
+    NX, NA = 4, dm.early
+    XR = dm.local // NX
+
+    own_w = [w0.own(fc) for fc in range(nf)]
+    own_x = local_copy(r.x_in, r.xg.at[b], r.loc.at[2 * nf])
+    r.need("vec_in")
+    n.ready()
+    for fc in range(nf):
+        w0.pre(fc)
+        if fc == 0:
+            r.vecg[b, s] = r.vec_in[...]
+            for p in n.batch_peers:
+                remote(r.vec_in, r.vecg.at[b, s], r.vp_s.at[p], r.vp_r.at[b], (p, s)).start()
+    remote(r.x_in, r.xg.at[b], r.xc_s, r.xc_r, (n.sib, s)).start()
+
+    def x_send(k):
+        rows = pl.ds(k * XR, XR)
+        return remote(r.x_in.at[rows], r.xg.at[b, rows], r.xx_s.at[k], r.xx_r.at[k], (n.across, s))
+
+    def x_relay(k):
+        at = r.xg.at[n.across, pl.ds(k * XR, XR)]
+        return remote(at, at, r.xl_s.at[k], r.xl_r.at[k], (n.sib, s))
+
+    def relay(k):
+        arrived(r.xg.at[n.across, pl.ds(k * XR, XR)], r.xx_r.at[k], (n.across, s))
+        x_relay(k).start()
+
+    def w0_start(fc):
+        for c in own_w[fc]:
+            c.wait()
+        w0.start(fc)
+
+    w0_start(0)
+    for k in range(NX):
+        x_send(k).start()
+    for p in n.batch_peers:
+        arrived(r.vecg.at[p, s], r.vp_r.at[p], (p, s))
+    for p in n.outer_peers:
+        remote(r.vecg.at[:, s], r.vecg.at[:, s], r.vz_s.at[p], r.vz_r.at[z], (b, p * inner + y)).start()
+    w0.step(0, 1)
+    for p in n.outer_peers:
+        arrived(r.vecg.at[:, p * inner + y], r.vz_r.at[p], (b, s))
+    for o in range(outer):
+        for p in n.inner_peers:
+            at = r.vecg.at[:, o * inner + y]
+            remote(at, at, r.vy_s.at[o, p], r.vy_r.at[o, y], (b, z * inner + p)).start()
+    w0.step(0, 2)
+    w0_start(1)
+    w0.step(0, 3)
+    for o in range(outer):
+        for p in n.inner_peers:
+            arrived(r.vecg.at[:, o * inner + p], r.vy_r.at[o, p], (b, s))
+    per = F // R
+    for k in range(dm.d // F):
+        bb, s0 = (k * per) // ns, (k * per) % ns
+        total = r.vecg[bb, s0]
+        for j in range(1, per):
+            total = total + r.vecg[bb, s0 + j]
+        r.vec[:, k * F : (k + 1) * F] = total
+    own_x.wait()
+
+    TILE = 32
+
+    def norm_block(bb, lo=0, count=dm.local):
+        def step(i, carry):
+            rows = pl.ds(pl.multiple_of(lo + i * TILE, TILE), TILE)
+            x = r.xg[bb, rows, :].astype(F32)
+            mu, rstd, normed = norm_rows(x, r.vec[0:1, :])
+            every = pl.ds(pl.multiple_of(bb * dm.local + lo + i * TILE, TILE), TILE)
+            r.normed[every, :] = normed
+            r.mu_out[every, :] = jnp.broadcast_to(mu, (TILE, F))
+            r.rstd_out[every, :] = jnp.broadcast_to(rstd, (TILE, F))
+            for fc in range(nf):
+                r.xS[fc, every, :] = r.xg[bb, rows, pl.ds(at128(b * dm.q + fc * F), F)].astype(F32)
+            return carry
+
+        lax.fori_loop(0, count // TILE, step, 0)
+
+    def diag_norm(k):
+        arrived(r.xg.at[n.diag, pl.ds(k * XR, XR)], r.xl_r.at[k], (n.sib, s))
+        norm_block(n.diag, k * XR, XR)
+
+    def across_norm(k):
+        norm_block(n.across, k * XR, XR)
+
+    def prod(fc, *pieces):
+        products(dm, r, n, r.wq0, (fc,), 0, pieces)
+
+    near = [(g, part) for g in (b, n.sib) for part in range(2)]
+    w0.step(1, 1)
+    norm_block(b)
+    w0.step(1, 2)
+    w0_start(2)
+    arrived(r.xg.at[n.sib], r.xc_r, (n.sib, s))
+    norm_block(n.sib)
+    w0.step(1, 3)
+    w0.step(2, 1)
+    relay(0)
+    w0.complete(0)
+    prod(0, *near)
+    w0.step(2, 2)
+    w0_start(3)
+    across_norm(0)
+    relay(1)
+    across_norm(1)
+    w0.step(2, 3)
+    w0.step(3, 1)
+    prod(0, (n.across, 0))
+    diag_norm(0)
+    w0.step(3, 2)
+    diag_norm(1)
+    w0.complete(1)
+    prod(1, *near)
+    w0.step(3, 3)
+    relay(2)
+    across_norm(2)
+    prod(0, (n.diag, 0))
+    prod(1, (n.across, 0), (n.diag, 0))
+    diag_norm(2)
+    second = [c for fc in range(nf) for c in w1.own(fc)]
+    relay(3)
+    for fc in range(nf):
+        w1.pre(fc)
+    across_norm(3)
+    prod(0, (n.across, 1))
+    diag_norm(3)
+    prod(0, (n.diag, 1))
+    scan_totals(dm, r, n, 0)
+    prod(1, (n.across, 1), (n.diag, 1))
+    scan_totals(dm, r, n, 1)
+    normed_copy = local_copy(r.normed, r.normed_out, r.loc.at[0])
+    r.store("mu_out")
+    r.store("rstd_out")
+
+    pend = []
+
+    def p2(fc):
+        scan_finish(dm, r, n, fc, 0)
+        r.hb[fc] = r.hS[fc].astype(BF16)
+        remote(r.hb.at[fc], r.x1g_out.at[b, fc], r.h_s.at[fc], r.h_r.at[fc], (n.across, s)).start()
+        remote(r.hb.at[fc], r.x1g_out.at[b, fc], r.hc_s.at[fc], r.hc_r.at[fc], (n.sib, s)).start()
+        pend.append(local_copy(r.hb.at[fc], r.x1g_out.at[b, fc], r.out_sem.at[fc, 0]))
+        pairs = [(r.fS, r.f_out), (r.cS, r.c_out), (r.rS, r.r_out), (r.cellS, r.cell_out), (r.hS, r.x1_out), (r.xS, r.xo_out)]
+        for k, (src, dst) in enumerate(pairs):
+            pend.append(local_copy(src.at[fc], dst.at[fc], r.out_sem.at[fc, k + 1]))
+
+    def h_relay(fc):
+        at = r.x1g_out.at[n.across, fc]
+        arrived(at, r.h_r.at[fc], (n.across, s))
+        remote(at, at, r.hl_s.at[fc], r.hl_r.at[fc], (n.sib, s)).start()
+
+    for c in second:
+        c.wait()
+    w1.start(0, 0 < NA)
+    w0.complete(2)
+    products(dm, r, n, r.wq0, (2,), 0, None)
+    scan_totals(dm, r, n, 2)
+    w1.step(0, 1, 0 < NA)
+    p2(0)
+    w1.step(0, 2, 0 < NA)
+    w1.start(1, 1 < NA)
+    p2(1)
+    w0.complete(3)
+    products(dm, r, n, r.wq0, (3,), 0, None)
+    wq_copy = local_copy(r.wq0, r.wq0_out, r.loc.at[2])
+    scan_totals(dm, r, n, 3)
+    w1.step(0, 3, 0 < NA)
+    p2(2)
+    w1.step(1, 1, 1 < NA)
+    h_relay(0)
+    p2(3)
+    r.inc_out[...] = r.incS[...]
+    r.runA_out[...] = r.runA[...]
+    r.tot_out[...] = r.tot[...]
+    r.vec_out[...] = r.vec[...]
+    for k in ("inc_out", "runA_out", "tot_out", "vec_out"):
+        r.store(k)
+    w1.step(1, 2, 1 < NA)
+    w1.start(2, 2 < NA)
+    w1.step(1, 3, 1 < NA)
+    h_relay(1)
+    w1.step(2, 1, 2 < NA)
+    w1.step(2, 2, 2 < NA)
+    w1.start(3, 3 < NA)
+    w1.step(2, 3, 2 < NA)
+    h_relay(2)
+    for h in range(1, outer):
+        w1.step(3, h, 3 < NA)
+    h_relay(3)
+    for fc in range(nf):
+        if fc < NA:
+            w1.complete(fc)
+        arrived(r.x1g_out.at[n.sib, fc], r.hc_r.at[fc], (n.sib, s))
+        arrived(r.x1g_out.at[n.diag, fc], r.hl_r.at[fc], (n.sib, s))
+    for c in pend:
+        c.wait()
+    normed_copy.wait()
+    wq_copy.wait()
+    for p in n.batch_peers:
+        sent(r.vec_in, r.vp_s.at[p], (p, s))
+    for p in n.outer_peers:
+        sent(r.vecg.at[:, s], r.vz_s.at[p], (b, s))
+    for p in n.inner_peers:
+        for o in range(outer):
+            sent(r.vecg.at[:, s], r.vy_s.at[o, p], (b, s))
+    sent(r.x_in, r.xc_s, (n.sib, s))
+    for k in range(NX):
+        x_send(k).wait_send()
+        x_relay(k).wait_send()
+    totals_sent(dm, r, n)
+    for fc in range(nf):
+        w0.drain(fc)
+        w1.drain(fc, fc < NA)
+        for sem in (r.h_s, r.hc_s, r.hl_s):
+            sent(r.hb.at[fc], sem.at[fc], (b, s))
+
+
+def scan_scratch(dm):
+    nf, ns = dm.nf, dm.ns
+    return dict(
+        totS=V((nf, 2, dm.runs, F), F32),
+        t_s=DMA((nf, ns)), t_r=DMA((nf, ns)),
+    )
+
+
+def call_one(dm, x, w, vec):
+    nb, ns, nf, inner, outer, R = dm.nb, dm.ns, dm.nf, dm.inner, dm.outer, dm.rows
+    D, q, tok, L = dm.d, dm.q, dm.tok, dm.layers
+    wshape = (nf, 3, nb, ns * R, F)
+    chunk, cV = ((nf, tok, F), F32, HBM), V((nf, tok, F), F32)
+    ins = dict(x_in=(x, HBM), w_in=(w, HBM), vec_in=(vec, INV))
+    outs = dict(
+        normed_out=((tok, D), BF16, HBM), wq0_out=(wshape, BF16, HBM), wq1_out=(wshape, BF16, HBM),
+        x1g_out=((nb, nf, tok, F), BF16, HBM),
+        x1_out=chunk, xo_out=chunk, f_out=chunk, c_out=chunk, r_out=chunk, cell_out=chunk,
+        inc_out=((nf, nb, dm.runs, F), F32, INV), runA_out=((nf, nb, dm.runs, F), F32, INV), tot_out=((nf, ns, 2, dm.runs, F), F32, INV),
+        vec_out=((16, D), F32, INV), mu_out=((tok, F), F32, INV), rstd_out=((tok, F), F32, INV),
+    )
+    scratch = dict(
+        xg=V((nb, dm.local, D), BF16), normed=V((tok, D), BF16), wq0=V(wshape, BF16),
+        vecg=V((nb, ns, 16, F), F32), vec=V((16, D), F32),
+        xS=cV, fS=cV, cS=cV, rS=cV, cellS=cV, hS=cV, hb=V((nf, tok, F), BF16),
+        incS=V((nf, nb, dm.runs, F), F32), tot=V((nf, ns, 2, dm.runs, F), F32),
+        pre_s=DMA((L, nf, nb)), pre_r=DMA((L, nf, nb)), z_s=DMA((L, nf, outer, 2)), z_r=DMA((L, nf, outer)),
+        y_s=DMA((L, nf, outer, inner)), y_r=DMA((L, nf, outer, inner)),
+        vp_s=DMA((nb,)), vp_r=DMA((nb,)), vz_s=DMA((outer,)), vz_r=DMA((outer,)),
+        vy_s=DMA((outer, inner)), vy_r=DMA((outer, inner)),
+        xx_s=DMA((4,)), xx_r=DMA((4,)), xc_s=DMA, xc_r=DMA, xl_s=DMA((4,)), xl_r=DMA((4,)),
+        h_s=DMA((nf,)), h_r=DMA((nf,)), hc_s=DMA((nf,)), hc_r=DMA((nf,)), hl_s=DMA((nf,)), hl_r=DMA((nf,)),
+        loc=DMA((2 * nf + 1,)), own_sem=DMA((L, nf, 3)), out_sem=DMA((nf, 7)),
+        runA=V((nf, nb, dm.runs, F), F32), runV=V((nf, nb, dm.runs, F), F32),
+        **scan_scratch(dm),
+    )
+    return launch(dm, "forward_one", 0, kernel_one, ins, outs, scratch)
+
+
+def kernel_two(dm, r):
+    n = Net(dm)
+    nb, nf = dm.nb, dm.nf
+    b, s = n.b, n.s
+    w1 = Gather(dm, n, r, 1, r.wq)
+    NA = dm.early
+    x_copy = local_copy(r.x1_in, r.xS, r.loc.at[0])
+    w_copy = []
+    for fc in range(NA):
+        w_copy.append(local_copy(r.w_in.at[fc], r.wq.at[fc], r.w_sem.at[fc, 0]))
+    w_late, y_sends = [], {fc: [] for fc in range(NA, nf)}
+    for fc in range(NA, nf):
+        for o in range(dm.outer):
+            rows = pl.ds(pl.multiple_of((o * dm.inner + n.y) * dm.rows, dm.rows), dm.rows)
+            at = (fc, slice(None), slice(None), rows)
+            for p in n.inner_peers:
+                y_sends[fc].append(
+                    remote(r.w_in.at[at], r.wq.at[at], r.y_s.at[1, fc, o, p], r.y_r.at[1, fc, o, n.y], (b, n.z * dm.inner + p))
+                )
+            w_late.append(local_copy(r.w_in.at[at], r.wq.at[at], r.w_sem.at[fc, o]))
+
+    def cot_send(p):
+        cols = pl.ds(at128(p * dm.q), dm.q)
+        at = r.cot.at[pl.ds(pl.multiple_of(b * dm.local, dm.local), dm.local)]
+        return remote(r.cot_in.at[:, cols], at, r.c_s.at[p], r.c_r.at[b], (p, s))
+
+    cot_copy = local_copy(
+        r.cot_in.at[:, pl.ds(at128(b * dm.q), dm.q)], r.cot.at[pl.ds(pl.multiple_of(b * dm.local, dm.local), dm.local)], r.loc.at[1]
+    )
+    TT, TILE = 256, 32
+
+    def fetch(k):
+        return pltpu.make_async_copy(r.x1g_in.at[:, :, pl.ds(k * TT, TT)], r.xt.at[k % 2], r.xt_sem.at[k % 2])
+
+    fetch(0).start()
+    r.need("vec")
+    n.ready()
+    for c in y_sends[NA]:
+        c.start()
+    for p in n.batch_peers:
+        cot_send(p).start()
+    for k in range(dm.tok // TT):
+        if (k + 1) * TT < dm.tok:
+            fetch(k + 1).start()
+        fetch(k).wait()
+
+        def step(i, carry, k=k):
+            rows = pl.ds(pl.multiple_of(i * TILE, TILE), TILE)
+            x = jnp.concatenate([r.xt[k % 2, q, fc, rows, :] for q in range(nb) for fc in range(nf)], axis=1).astype(F32)
+            mu, rstd, normed = norm_rows(x, r.vec[5:6, :])
+            every = pl.ds(pl.multiple_of(k * TT + i * TILE, TILE), TILE)
+            r.normed[every, :] = normed
+            r.mu_out[every, :] = jnp.broadcast_to(mu, (TILE, F))
+            r.rstd_out[every, :] = jnp.broadcast_to(rstd, (TILE, F))
+            return carry
+
+        lax.fori_loop(0, TT // TILE, step, 0)
+    normed_copy = local_copy(r.normed, r.normed_out, r.xt_sem.at[0])
+    r.store("mu_out")
+    r.store("rstd_out")
+    for c in [x_copy, cot_copy] + w_copy:
+        c.wait()
+
+    def p1(fcs):
+        products(dm, r, n, r.wq, fcs, 5, None)
+        for fc in fcs:
+            scan_totals(dm, r, n, fc)
+
+    pend = []
+
+    def p2(fc):
+        scan_finish(dm, r, n, fc, 5)
+        r.hb[fc] = r.hS[fc].astype(BF16)
+        pend.append(local_copy(r.hb.at[fc], r.h_out.at[fc], r.out_sem.at[fc, 2]))
+        r.dhS[fc] = r.cot[:, fc * F : (fc + 1) * F].astype(F32)
+        back_totals(dm, r, n, fc, 5)
+
+    def p3(fc):
+        back_finish(dm, r, n, fc, 5)
+        pend.extend(back_outputs(dm, r, fc))
+
+    p1((0, 1))
+    for fc in range(NA + 1, nf):
+        for c in y_sends[fc]:
+            c.start()
+    for p in n.batch_peers:
+        arrived(r.cot.at[pl.ds(pl.multiple_of(p * dm.local, dm.local), dm.local)], r.c_r.at[p], (p, s))
+    p2(0)
+    p2(1)
+    for c in w_late:
+        c.wait()
+    for fc in range(NA, nf):
+        w1.complete(fc)
+        p1((fc,))
+    pend.append(local_copy(r.wq, r.wq_out, r.loc.at[0]))
+    for fc in range(NA, nf):
+        p2(fc)
+    for fc in range(nf):
+        p3(fc)
+    r.store("vsum_out")
+    for c in pend:
+        c.wait()
+    normed_copy.wait()
+    for p in n.batch_peers:
+        cot_send(p).wait_send()
+    for fc in range(NA, nf):
+        w1.drain_inner(fc)
+    totals_sent(dm, r, n)
+    back_sent(dm, r, n)
+
+
+def call_two(dm, one, cot):
+    nb, ns, nf = dm.nb, dm.ns, dm.nf
+    tok = dm.tok
+    cV = V((nf, tok, F), F32)
+    ins = dict(
+        w_in=(one.wq1_out, HBM), x1_in=(one.x1_out, HBM), cot_in=(cot, HBM),
+        x1g_in=(one.x1g_out, HBM), vec=(one.vec_out, INV),
+    )
+    outs = dict(
+        wq_out=((nf, 3, nb, ns * dm.rows, F), BF16, HBM),
+        normed_out=((tok, dm.d), BF16, HBM), h_out=((nf, tok, F), BF16, HBM),
+        dmixed_out=((nf, 3, tok, F), BF16, HBM), dtail_out=((nf, tok, F), F32, HBM),
+        vsum_out=((nf, 4, dm.runs, F), F32, INV), mu_out=((tok, F), F32, INV), rstd_out=((tok, F), F32, INV),
+    )
+    scratch = dict(
+        wq=V((nf, 3, nb, ns * dm.rows, F), BF16), cot=V((tok, dm.q), BF16), xt=V((2, nb, nf, 256, F), BF16),
+        normed=V((tok, dm.d), BF16), dmixed=V((nf, 3, tok, F), BF16),
+        xS=cV, fS=cV, cS=cV, rS=cV, cellS=cV, drS=cV, hS=cV, hb=V((nf, tok, F), BF16),
+        incS=V((nf, nb, dm.runs, F), F32), tot=V((nf, ns, 2, dm.runs, F), F32),
+        bk=V((nf, ns, dm.runs, F), F32), bkS=V((nf, dm.runs, F), F32), backV=V((nf, nb, dm.runs, F), F32),
+        runA=V((nf, nb, dm.runs, F), F32), runV=V((nf, nb, dm.runs, F), F32),
+        k_s=DMA((nf, ns)), k_r=DMA((nf, ns)),
+        c_s=DMA((nb,)), c_r=DMA((nb,)), w_sem=DMA((nf, dm.outer)),
+        y_s=DMA((2, nf, dm.outer, dm.inner)), y_r=DMA((2, nf, dm.outer, dm.inner)),
+        loc=DMA((2,)), xt_sem=DMA((2,)), out_sem=DMA((nf, 3)),
+        **scan_scratch(dm),
+    )
+    alias = dict(scratch)
+
+    def kernel(dm, r):
+        r.dhS = r.hS
+        kernel_two(dm, r)
+
+    return launch(dm, "layer_two", 1, kernel, ins, outs, alias)
+
+
+def kernel_three(dm, r):
+    n = Net(dm)
+    nf = dm.nf
+    loads = []
+    for fc in range(nf):
+        pairs = [(r.f_in.at[fc], r.fS), (r.c_in.at[fc], r.cS), (r.r_in.at[fc], r.rS), (r.cell_in.at[fc], r.cellS),
+                 (r.xo_in.at[fc], r.xS), (r.dh_in.at[:, pl.ds(fc * F, F)], r.dhS)]
+        loads.append([local_copy(src, dst.at[fc], r.loc.at[fc, k]) for k, (src, dst) in enumerate(pairs)])
+    rs = Scatter(dm, n, r, dm.on_time)
+    late = range(dm.on_time, rs.count)
+    b, s = n.b, n.s
+
+    def block_send(fc, p):
+        cols = pl.ds(at128(b * dm.q + fc * F), F)
+        src = r.h_in.at[fc, pl.ds(pl.multiple_of(p * dm.local, dm.local), dm.local)]
+        return remote(src, r.block_out.at[:, cols], r.o_s.at[fc, p], r.o_r.at[fc, b], (p, s))
+
+    pend = []
+    for fc in range(nf):
+        cols = pl.ds(at128(b * dm.q + fc * F), F)
+        src = r.h_in.at[fc, pl.ds(pl.multiple_of(b * dm.local, dm.local), dm.local)]
+        pend.append(local_copy(src, r.block_out.at[:, cols], r.out_sem.at[fc, 2]))
+    r.need("wg")
+    n.ready()
+    rs.start(late[0])
+    for fc in range(nf):
+        for p in n.batch_peers:
+            block_send(fc, p).start()
+    r.need("vec", "incS", "runA", "tot")
+    for fc in range(nf):
+        for c in loads[fc]:
+            c.wait()
+        back_totals(dm, r, n, fc, 0)
+    for ch in late[1:]:
+        rs.start(ch)
+    rs.mid(late[0])
+    for fc in range(nf):
+        back_finish(dm, r, n, fc, 0)
+        pend.extend(back_outputs(dm, r, fc))
+        if 0 < fc < len(late):
+            rs.mid(late[fc])
+            rs.last(late[fc - 1])
+    rs.last(late[-1])
+    r.store("vsum_out")
+    r.need("fr_early")
+    rs.assemble(r.fr_early)
+    r.store("wg_out")
+    for c in pend:
+        c.wait()
+    back_sent(dm, r, n)
+    for fc in range(nf):
+        for p in n.batch_peers:
+            block_send(fc, p).wait_send()
+            arrived(r.block_out.at[:, pl.ds(at128(p * dm.q + fc * F), F)], r.o_r.at[fc, p], (p, s))
+    rs.drain(late)
+
+
+def call_three(dm, one, two, g1):
+    nb, ns, nf, tok = dm.nb, dm.ns, dm.nf, dm.tok
+    cV = V((nf, tok, F), F32)
+    ins = dict(
+        f_in=(one.f_out, HBM), c_in=(one.c_out, HBM), r_in=(one.r_out, HBM), cell_in=(one.cell_out, HBM),
+        xo_in=(one.xo_out, HBM), dh_in=(g1.dx_out, HBM), vec=(one.vec_out, INV), incS=(one.inc_out, INV),
+        runA=(one.runA_out, INV), tot=(one.tot_out, INV), wg=(g1.late_out, INV), fr_early=(g1.fr_out, INV),
+        h_in=(two.h_out, HBM),
+    )
+    outs = dict(
+        block_out=((dm.local, dm.d), BF16, HBM),
+        dmixed_out=((nf, 3, tok, F), BF16, HBM), dtail_out=((nf, tok, F), F32, HBM), vsum_out=((nf, 4, dm.runs, F), F32, INV),
+        wg_out=((dm.rows, 3 * dm.d), F32, INV),
+    )
+    scratch = dict(
+        dmixed=V((nf, 3, tok, F), BF16), xS=cV, fS=cV, cS=cV, rS=cV, cellS=cV, drS=cV, dhS=cV,
+        bk=V((nf, ns, dm.runs, F), F32), bkS=V((nf, dm.runs, F), F32), backV=V((nf, nb, dm.runs, F), F32),
+        k_s=DMA((nf, ns)), k_r=DMA((nf, ns)), loc=DMA((nf, 6)), out_sem=DMA((nf, 3)), o_s=DMA((nf, nb)), o_r=DMA((nf, nb)),
+        fr=V((nb, 3, dm.rows, dm.q), BF16), **scatter_scratch(dm, 3 * nb - dm.on_time),
+    )
+    return launch(dm, "layer_one_back", 2, kernel_three, ins, outs, scratch)
+
+
+class Scatter:
+    def __init__(self, dm, n, r, lo):
+        self.dm, self.n, self.r, self.lo = dm, n, r, lo
+        self.H = 3
+        self.count = dm.nb * self.H
+
+    def strip(self, ch, pos):
+        R = self.dm.rows
+        return self.r.wg.at[ch - self.lo, pl.ds(pl.multiple_of(pos * R, R), R)]
+
+    def y_copy(self, ch, j, o):
+        n, r, I, k = self.n, self.r, self.dm.inner, ch - self.lo
+        p = lax.rem(n.y + j, I)
+        return remote(
+            self.strip(ch, o * I + p), r.yr.at[k, I - j - 1, o], r.ry_s.at[k, j - 1, o], r.ry_r.at[k, I - j - 1, o], (n.b, n.z * I + p)
+        )
+
+    def z_copy(self, ch, j):
+        n, r, O, k = self.n, self.r, self.dm.outer, ch - self.lo
+        p = lax.rem(n.z + j, O)
+        return remote(
+            r.zs.at[k, p], r.zr.at[k, O - j - 1], r.rz_s.at[k, j - 1], r.rz_r.at[k, O - j - 1], (n.b, p * self.dm.inner + n.y)
+        )
+
+    def f_copy(self, ch):
+        n, r, k = self.n, self.r, ch - self.lo
+        return remote(r.fs.at[k], r.fr.at[n.b, ch % self.H], r.rf_s.at[k], r.rf_r.at[n.b, ch % self.H], (ch // self.H, n.s))
+
+    def start(self, ch):
+        for j in range(1, self.dm.inner):
+            for o in range(self.dm.outer):
+                self.y_copy(ch, j, o).start()
+
+    def mid(self, ch):
+        n, r, dm, k = self.n, self.r, self.dm, ch - self.lo
+        for j in range(1, dm.inner):
+            for o in range(dm.outer):
+                arrived(r.yr.at[k, j - 1, o], r.ry_r.at[k, j - 1, o], (n.b, n.s))
+        for jz in range(dm.outer):
+            o = lax.rem(n.z + jz + 1, dm.outer)
+            pos = pl.ds(pl.multiple_of((o * dm.inner + n.y) * dm.rows, dm.rows), dm.rows)
+            total = r.wg[k, pos, :].astype(F32)
+            for j in range(1, dm.inner):
+                total = total + r.yr[k, j - 1, o].astype(F32)
+            r.zs[k, o] = total.astype(BF16)
+            if jz + 1 < dm.outer:
+                self.z_copy(ch, jz + 1).start()
+
+    def last(self, ch):
+        n, r, dm, k = self.n, self.r, self.dm, ch - self.lo
+        for j in range(1, dm.outer):
+            arrived(r.zr.at[k, j - 1], r.rz_r.at[k, j - 1], (n.b, n.s))
+        total = r.zs[k, n.z].astype(F32)
+        for j in range(1, dm.outer):
+            total = total + r.zr[k, j - 1].astype(F32)
+        r.fs[k] = total.astype(BF16)
+        pl.when(n.b != ch // self.H)(lambda: self.f_copy(ch).start())
+
+        @pl.when(n.b == ch // self.H)
+        def _():
+            r.fr[n.b, ch % self.H] = r.fs[k]
+
+    def receive(self, chunks):
+        n, r = self.n, self.r
+        for ch in chunks:
+
+            @pl.when(n.b == ch // self.H)
+            def _(ch=ch):
+                for p in n.batch_peers:
+                    arrived(r.fr.at[p, ch % self.H], r.rf_r.at[p, ch % self.H], (p, n.s))
+
+    def assemble(self, early=None):
+        n, r, dm = self.n, self.r, self.dm
+        self.receive(range(self.lo, self.count))
+        for h in range(self.H):
+            here = n.b * self.H + h >= self.lo
+            for k in range(dm.nb):
+                to = h * dm.d + k * dm.q
+
+                @pl.when(here)
+                def _(h=h, k=k, to=to):
+                    r.wg_out[:, to : to + dm.q] = r.fr[k, h].astype(F32)
+
+                if early is not None:
+
+                    @pl.when(jnp.logical_not(here))
+                    def _(h=h, k=k, to=to):
+                        r.wg_out[:, to : to + dm.q] = early[k, h].astype(F32)
+
+    def drain(self, chunks):
+        for ch in chunks:
+            for j in range(1, self.dm.inner):
+                for o in range(self.dm.outer):
+                    self.y_copy(ch, j, o).wait_send()
+            for j in range(1, self.dm.outer):
+                self.z_copy(ch, j).wait_send()
+            pl.when(self.n.b != ch // self.H)(lambda ch=ch: self.f_copy(ch).wait_send())
+
+
+def scatter_scratch(dm, count):
+    inner, outer, R, q = dm.inner, dm.outer, dm.rows, dm.q
+    return dict(
+        yr=V((count, inner - 1, outer, R, q), BF16), zs=V((count, outer, R, q), BF16), zr=V((count, outer - 1, R, q), BF16),
+        fs=V((count, R, q), BF16),
+        ry_s=DMA((count, inner - 1, outer)), ry_r=DMA((count, inner - 1, outer)),
+        rz_s=DMA((count, outer - 1)), rz_r=DMA((count, outer - 1)), rf_s=DMA((count,)), rf_r=DMA((dm.nb, 3)),
+    )
+
+
+def kernel_grads(first, dm, r):
+    n = Net(dm)
+    nb, nf, q, tok = dm.nb, dm.nf, dm.q, dm.tok
+    b, s = n.b, n.s
+    base = 0 if first else 5
+    NT = nb
+    TR = tok // NT
+    PER = TR // F
+    rs = Scatter(dm, n, r, 0)
+    H, NCH = rs.H, rs.count
+    mine = range(NCH if first else dm.on_time)
+    dm_load = local_copy(r.dm_in, r.dmS, r.loc.at[0])
+    n_load = [local_copy(r.normed_in.at[:, pl.ds(k * q, q)], r.nS.at[:, pl.ds(k * q, q)], r.n_sem.at[k]) for k in range(nb)]
+    w_load = local_copy(r.w_in, r.wS, r.loc.at[1])
+    half = nb // 2
+    order = [j + half * k for j in range(half) for k in range(2)]
+
+    def fetch(k):
+        rows, slot = pl.ds(order[k] * TR, TR), k % 2
+        return [
+            pltpu.make_async_copy(r.x_in.at[:, rows], r.xt.at[slot], r.tile_sem.at[slot, 0]),
+            pltpu.make_async_copy(r.dtail_in.at[:, rows], r.dt.at[slot], r.tile_sem.at[slot, 1]),
+            pltpu.make_async_copy(r.mu_in.at[rows], r.mt.at[slot], r.tile_sem.at[slot, 2]),
+            pltpu.make_async_copy(r.rstd_in.at[rows], r.rt.at[slot], r.tile_sem.at[slot, 3]),
+        ]
+
+    def part(quarter, c):
+        left = jnp.concatenate([r.dmS[fc, g, c * TR : (c + 1) * TR, :] for fc in range(nf) for g in range(3)], axis=1)
+        right = jnp.concatenate([r.wS[fc, g, quarter] for fc in range(nf) for g in range(3)], axis=1)
+        return lax.dot_general(left, right, (((1,), (1,)), ((), ())), preferred_element_type=F32)
+
+    def to_sib(buf, got, c, i):
+        return remote(buf.at[c], got.at[c], r.p_s.at[i, c], r.p_r.at[i, c], (n.sib, s))
+
+    def to_across(c):
+        return remote(r.pb.at[c], r.prb.at[c], r.p_s.at[1, c], r.p_r.at[1, c], (n.across, s))
+
+    def sums_of(k, v, quarter, fresh=False):
+        c = order[k]
+        cols = pl.ds(at128(quarter * q), q)
+        t1 = v * r.vec[base : base + 1, cols]
+        t2 = v * r.nS[c * TR : (c + 1) * TR, cols].astype(F32)
+        for j, t in enumerate((t1, t2)):
+            total = t[:, :F]
+            for fc in range(1, nf):
+                total = total + t[:, fc * F : (fc + 1) * F]
+            r.rows[j] = total if fresh else r.rows[j] + total
+
+    def stage(k, between=None):
+        c = order[k]
+        v = part(n.diag, c)
+        r.pa[c] = v.astype(BF16)
+        to_sib(r.pa, r.pra, c, 0).start()
+        sums_of(k, v, n.diag, True)
+        v = part(b, c)
+        r.acc[c * TR : (c + 1) * TR, :] = v
+        sums_of(k, v, b)
+        if between is not None:
+            between()
+        to_sib(r.pa, r.pra, c, 0).wait_send()
+        v = part(n.sib, c)
+        r.pa[c] = v.astype(BF16)
+        to_sib(r.pa, r.prc, c, 2).start()
+        sums_of(k, v, n.sib)
+        v = part(n.across, c)
+        sums_of(k, v, n.across)
+        for i in range(PER):
+            for j in range(2):
+                r.st[b, k, j, i : i + 1, :] = jnp.sum(r.rows[j, i * F : (i + 1) * F, :].T, axis=0, keepdims=True)
+        for p in n.batch_peers:
+            stats_copy(k, p).start()
+        arrived(r.pra.at[c], r.p_r.at[0, c], (n.sib, s))
+        r.pb[c] = (v + r.pra[c].astype(F32)).astype(BF16)
+        to_across(c).start()
+
+    def wgrad(ch, begin=None):
+        bb, h = ch // H, ch % H
+        right = jnp.concatenate([r.dmS[fc, h] for fc in range(nf)], axis=1)
+        r.wg[ch] = lax.dot_general(
+            r.nS[:, bb * q : (bb + 1) * q], right, (((0,), (0,)), ((), ())), preferred_element_type=F32
+        ).astype(BF16)
+        if begin is not None:
+            begin()
+        if ch in mine:
+            rs.start(ch)
+
+    def mid(ch):
+        if ch in mine:
+            rs.mid(ch)
+
+    def last(ch):
+        if ch in mine:
+            rs.last(ch)
+
+    def gain(fc):
+        return vrow(dm, r, n, base, fc)
+
+    def stats_copy(k, p):
+        return remote(r.st.at[b, k], r.st.at[b, k], r.st_s.at[k, p], r.st_r.at[k, b], (p, s))
+
+    pend = []
+
+    def final(k):
+        c, slot = order[k], k % 2
+        for p in n.batch_peers:
+            arrived(r.st.at[p, k], r.st_r.at[k, p], (p, s))
+        arrived(r.prc.at[c], r.p_r.at[2, c], (n.sib, s))
+        arrived(r.prb.at[c], r.p_r.at[1, c], (n.across, s))
+        for copy in fetch(k):
+            copy.wait()
+        if first:
+            to_across(c).wait_send()
+
+        def step(i, sums):
+            near = pl.ds(pl.multiple_of(i * F, F), F)
+            rows = pl.ds(pl.multiple_of(c * TR + i * F, F), F)
+            mu, rstd = r.mt[slot, near, :], r.rt[slot, near, :]
+            means = []
+            for j in range(2):
+                total = r.st[0, k, j, pl.ds(i, 1), :]
+                for m in range(1, nb):
+                    total = total + r.st[m, k, j, pl.ds(i, 1), :]
+                means.append(jnp.broadcast_to(total * (1.0 / dm.d), (F, F)).T)
+            new = []
+            for fc in range(nf):
+                cols = slice(fc * F, (fc + 1) * F)
+                dn = r.acc[rows, cols] + r.prc[c, near, cols].astype(F32) + r.prb[c, near, cols].astype(F32)
+                xhat = (r.xt[slot, fc, near, :] - mu) * rstd
+                new.append(sums[fc] + jnp.sum((dn * xhat).reshape(F // 8, 8, F), axis=0))
+                out = r.dt[slot, fc, near, :] + rstd * (dn * gain(fc) - means[0] - xhat * means[1])
+                if first:
+                    r.pb[c, near, cols] = out.astype(BF16)
+                else:
+                    r.acc[rows, cols] = out
+            return tuple(new)
+
+        sums = lax.fori_loop(0, PER, step, tuple(jnp.zeros((8, F), F32) for _ in range(nf)))
+        for fc in range(nf):
+            r.gsum[fc] = sums[fc] if k == 0 else r.gsum[fc] + sums[fc]
+        if k + 2 < NT:
+            for copy in fetch(k + 2):
+                copy.start()
+        if first:
+            pl.when(b != c)(lambda: to_owner(c).start())
+        else:
+            rows = pl.ds(c * TR, TR)
+            pend.append(local_copy(r.acc.at[rows], r.dx_out.at[rows], r.loc.at[3 + c]))
+
+    def to_owner(c):
+        return remote(r.pb.at[c], r.fin.at[b], r.g_s.at[c], r.g_r.at[b], (c, s))
+
+    dm_load.wait()
+    n_load[0].wait()
+    wgrad(0, n.ready)
+    wgrad(1)
+    wgrad(2)
+    r.need("vec")
+    for c in n_load[1:] + [w_load]:
+        c.wait()
+    stage(0, lambda: mid(0))
+    for k in range(2):
+        for copy in fetch(k):
+            copy.start()
+    wgrad(3)
+    stage(1, lambda: mid(1))
+    wgrad(4)
+    mid(2)
+    stage(2)
+    wgrad(5)
+    stage(3, lambda: mid(3))
+    wgrad(6)
+    mid(4)
+    for ch in range(3):
+        last(ch)
+    final(0)
+    wgrad(7)
+    mid(5)
+    last(3)
+    final(1)
+    wgrad(8)
+    last(4)
+    mid(6)
+    wgrad(9)
+    last(5)
+    mid(7)
+    final(2)
+    wgrad(10)
+    last(6)
+    mid(8)
+    wgrad(11)
+    last(7)
+    final(3)
+    mid(9)
+    if not first:
+        r.late[...] = r.wg[dm.on_time :]
+        pend.append(local_copy(r.late, r.late_out, r.loc.at[0]))
+    if first:
+        vector_start(dm, r, n)
+    else:
+        r.store("gsum")
+    last(8)
+    mid(10)
+    last(9)
+    mid(11)
+    last(10)
+    if first:
+
+        r.fin[b] = r.pb[b]
+        for k in range(nb):
+
+            @pl.when(k != b)
+            def _(k=k):
+                arrived(r.fin.at[k], r.g_r.at[k], (b, s))
+
+            r.acc[k * TR : (k + 1) * TR, :] = r.fin[k].astype(F32)
+            pend.append(local_copy(r.acc.at[pl.ds(k * TR, TR)], r.dx_out.at[:, pl.ds(k * q, q)], r.loc.at[3 + k]))
+    if first:
+        vector_finish(dm, r, n)
+    last(11)
+    if first:
+        rs.assemble()
+        r.store("wg_out")
+    else:
+        rs.receive(mine)
+        pend.append(local_copy(r.fr, r.fr_out, r.loc.at[1]))
+    for c in pend:
+        c.wait()
+    for k in range(NT):
+        c = order[k]
+        to_sib(r.pa, r.prc, c, 2).wait_send()
+        if first:
+            pl.when(b != c)(lambda c=c: to_owner(c).wait_send())
+        else:
+            to_across(c).wait_send()
+        for p in n.batch_peers:
+            stats_copy(k, p).wait_send()
+    rs.drain(mine)
+
+
+def vector_start(dm, r, n):
+    r.need("vsum0", "vsum1", "gsum1")
+    r.vg[n.s] = jnp.zeros((16, dm.q), F32)
+    for l, (vs, gs) in enumerate(((r.vsum0, r.gsum), (r.vsum1, r.gsum1))):
+        for fc in range(dm.nf):
+            cols = slice(fc * F, (fc + 1) * F)
+            r.vg[n.s, 5 * l : 5 * l + 1, cols] = jnp.sum(gs[fc], axis=0, keepdims=True)
+            for k in range(4):
+                r.vg[n.s, 5 * l + 1 + k : 5 * l + 2 + k, cols] = jnp.sum(vs[fc, k], axis=0, keepdims=True)
+    for p in n.seq_peers:
+        remote(r.vg.at[n.s], r.vg.at[n.s], r.v_s.at[p], r.v_r.at[n.s], (n.b, p)).start()
+
+
+def vector_finish(dm, r, n):
+    for p in n.seq_peers:
+        arrived(r.vg.at[p], r.v_r.at[p], (n.b, p))
+    total = r.vg[0]
+    for j in range(1, dm.ns):
+        total = total + r.vg[j]
+    r.vg_out[...] = total
+    r.store("vg_out")
+    for p in n.seq_peers:
+        sent(r.vg.at[n.s], r.v_s.at[p], (n.b, p))
+
+
+def call_grads(dm, first, w, normed, x, mu, rstd, vec, scans, more):
+    nb, ns, nf, R, q, tok = dm.nb, dm.ns, dm.nf, dm.rows, dm.q, dm.tok
+    TR, H = tok // nb, 3
+    NCH = nb * H
+    late = NCH - dm.on_time
+    ins = dict(
+        dm_in=(scans.dmixed_out, HBM), w_in=(w, HBM), normed_in=(normed, HBM), x_in=(x, HBM),
+        dtail_in=(scans.dtail_out, HBM), mu_in=(mu, HBM), rstd_in=(rstd, HBM), vec=(vec, INV),
+    )
+    bV = V((nb, TR, q), BF16)
+    scratch = dict(
+        dmS=V((nf, 3, tok, F), BF16), wS=V((nf, 3, nb, ns * R, F), BF16), nS=V((tok, dm.d), BF16),
+        acc=V((tok, q), F32), pa=bV, pra=bV, pb=bV, prb=bV, prc=bV,
+        wg=V((NCH, ns * R, q), BF16), fr=V((nb, H, R, q), BF16), **scatter_scratch(dm, NCH if first else dm.on_time),
+        xt=V((2, nf, TR, F), F32), dt=V((2, nf, TR, F), F32), mt=V((2, TR, F), F32), rt=V((2, TR, F), F32),
+        st=V((nb, nb, 2, TR // F, F), F32), rows=V((2, TR, F), F32),
+        loc=DMA((3 + nb,)), n_sem=DMA((nb,)), tile_sem=DMA((2, 4)), p_s=DMA((3, nb)), p_r=DMA((3, nb)),
+        st_s=DMA((nb, nb)), st_r=DMA((nb, nb)),
+    )
+    if first:
+        outs = dict(wg_out=((R, 3 * dm.d), F32, INV), dx_out=((dm.local, dm.d), F32, HBM), vg_out=((16, q), F32, INV))
+        ins.update({k: (v, INV) for k, v in more.items()})
+        scratch.update(
+            dict(fin=bV, g_s=DMA((nb,)), g_r=DMA((nb,)), vg=V((ns, 16, q), F32), v_s=DMA((ns,)), v_r=DMA((ns,)),
+             gsum=V((nf, 8, F), F32))
+        )
+    else:
+        outs = dict(
+            dx_out=((tok, q), F32, HBM), gsum=((nf, 8, F), F32, INV), fr_out=((nb, H, R, q), BF16, HBM),
+            late_out=((late, ns * R, q), BF16, HBM),
+        )
+        scratch["late"] = V((late, ns * R, q), BF16)
+    return launch(dm, "grads_one" if first else "grads_two", 3 if first else 4, functools.partial(kernel_grads, first), ins, outs, scratch)
+
+
+def prepare(dm, block_input, weight, vectors, cotangent):
+    D, nf, nb, R = dm.d, dm.nf, dm.nb, dm.rows
+    x, cot = [v.reshape(dm.runs, dm.length, D).swapaxes(0, 1).reshape(dm.local, D) for v in (block_input, cotangent)]
+    s = lax.axis_index("seq")
+    v = jnp.pad(vectors.reshape(dm.layers * 5, R), ((0, 16 - dm.layers * 5), (0, 0)))
+    lane = lax.broadcasted_iota(jnp.int32, (16, F), 1) // R
+    v = jnp.where(lane == lax.rem(s, F // R), jnp.tile(v, (1, F // R)), 0.0)
+    return x, weight, v, cot
+
+
+def natural(dm, v, shape):
+    return v.reshape(dm.length, dm.runs, dm.d).swapaxes(0, 1).reshape(shape)
+
+
+def tuned_body(nb, ns, block_input, weight, vectors, cotangent):
+    dm = Dims(nb, ns, block_input.shape, weight.shape)
+    x, w, vec, cot = prepare(dm, block_input, weight, vectors, cotangent)
+    one = call_one(dm, x, w, vec)
+    two = call_two(dm, one, cot)
+    g1 = call_grads(dm, False, two.wq_out, two.normed_out, one.x1_out, two.mu_out, two.rstd_out, one.vec_out, two, {})
+    three = call_three(dm, one, two, g1)
+    more = dict(vsum0=three.vsum_out, vsum1=two.vsum_out, gsum1=g1.gsum)
+    g0 = call_grads(dm, True, one.wq0_out, one.normed_out, one.xo_out, one.mu_out, one.rstd_out, one.vec_out, three, more)
+    weight_grad = jnp.stack([g0.wg_out, three.wg_out], axis=0)
+    s = lax.axis_index("seq")
+    mine = lax.dynamic_slice_in_dim(g0.vg_out, s * dm.rows, dm.rows, axis=1)[: dm.layers * 5]
+    vector_grad = mine.reshape(dm.layers, 5, dm.rows)
+    return (
+        natural(dm, three.block_out, block_input.shape), natural(dm, g0.dx_out, block_input.shape), weight_grad, vector_grad,
+    )
 
 
 def prefix(value, axis, join, neutral, backward):
@@ -72,7 +1448,7 @@
     return (cells, previous, reset)
 
 
-def body(block_input, weight, vectors, cotangent):
+def general_body(block_input, weight, vectors, cotangent):
     sequence_batch, time_steps, hidden_width = block_input.shape
     layers = weight.shape[0]
     params = lax.all_gather(vectors, ("batch", "seq"), axis=2, tiled=True)
@@ -175,6 +1551,8 @@
 
 
 def solution(mesh):
+    nb, ns = mesh.shape["batch"], mesh.shape["seq"]
+    body = functools.partial(tuned_body, nb, ns) if (nb, ns) == (4, 8) else general_body
     placed = (
         P("batch", "seq", None),
         P(None, ("batch", "seq"), None),

time: 2960 us -> 461 us (0.16); the launches traced: 2920 us -> 454 us
  local copies, waits for them, and re-layouts: 1120 us -> 17.5 us
  waiting for transfers between devices: 1000 us -> 0 us
  Pallas kernels: 0 us -> 433 us
  other arithmetic: 351 us -> 2.5 us
  blocking collectives: 283 us -> 0 us
  matrix products: 142 us -> 0 us
    reduce_scatter x2 -> x0, waiting for transfers between devices: 880 us -> none  [body(): lax.psum_scatter(weight_term(jnp.int32(0), rows * lax.axis_size(('batch',...]
    slice x216 -> x1, local copies, waits for them, and re-layouts: 604 us -> 0.77 us  [tuned_body(): lax.dynamic_slice_in_dim(g0.vg_out, s * dm.rows, dm.rows, axis=1)]
    pallas_call x0 -> x5, Pallas kernels: none -> 433 us  [launch(): pl.pallas_call(run, out_shape=[jax.ShapeDtypeStruct(shape, dtype) for sha...]
    all_gather x9 -> x0, blocking collectives: 283 us -> none  [the longest x8 192 us: prefix(): pieces = jax.tree.map(lambda part: lax.all_gather(part, axis), value)]
    pad x112 -> x1, local copies, waits for them, and re-layouts: 273 us -> 0.01 us  [prepare(): jnp.pad(vectors.reshape(dm.layers * 5, R), ((0, 16 - dm.layers * 5), (0,...]
    add x101 -> x0, other arithmetic: 182 us -> none  [the longest x36 61.6 us: body(): lax.associative_scan(compose, (jnp.flip(forget_gate, 1), jnp.flip(inject,...]
    dot_general x6 -> x0, matrix products: 142 us -> none  [the longest x2 49.6 us: weight_term(): lax.dot_general(normed_input, dmixed, (((0,), (0,)), ((), ())), preferred...]
    rev x8 -> x0, local copies, waits for them, and re-layouts: 131 us -> none  [the longest x2 65.3 us: body(): back_gates = jnp.flip(back_gates, 1)]
  transfers between devices with their start and end apart: 5 -> 0, of which waited for: 4 -> 0; matrix products, arithmetic and copies ran while one was open for 17% -> 0% of each run, Pallas kernels for 0% -> 0%
where the time goes in v3:
time: 461 us; the launch traced here: 454 us
  Pallas kernels  433 us (94%)
  local copies, waits for them, and re-layouts  17.5 us (4%)
    pallas_call x5, Pallas kernels, launch(): pl.pallas_call(run, out_shape=[jax.ShapeDtypeStruct(shape, dtype) for sha...  433 us

profile of v3, /device:TPU:11, one launch (start us, length us, event | category | flops | bytes accessed | tf_op | source)
XLA Modules:
  0.0 453.7 jit_solution(16498693078288417901)
XLA Ops:
  0.6 0.0 copy-start.1
  0.7 0.8 copy.14
  1.5 0.1 tile.10
  1.6 0.6 fusion.refs_2_
  2.2 4.1 copy.22
  6.3 0.0 copy-done.1
  6.3 2.5 copy.21
  8.8 141.1 %forward_one.1 = (bf16[2048,2048]{1,0:T(8,128)(2,1)}, bf16[4,3,4,512,128]{4,3,2,1,0:T(8,128)(2,1)}, bf16[4,3,4,512,128]{4,3,2,1,0:T(8,128)(2,1)}, bf16[4,4,2048,...) custom-call(bf16[512,2048]{1,0:T(8,128)(2,1)} %bitcast.23, ...), custom_call_target="tpu_custom_call" | custom-call | tf_op jit(solution)/shard_map/forward_one/pallas_call | solution.py:118
  149.8 82.6 %layer_two.1 = (bf16[4,3,4,512,128]{4,3,2,1,0:T(8,128)(2,1)}, bf16[2048,2048]{1,0:T(8,128)(2,1)}, bf16[4,2048,128]{2,1,0:T(8,128)(2,1)}, bf16[4,3,2048,128]{3,2,...) custom-call(bf16[4,3,4,512,128]{4,3,2,1,0:T(8,128)(2,1)} %get-tuple-, ...), custom_call_target="tpu_custom_call" | custom-call | tf_op jit(solution)/shard_map/layer_two/pallas_call | solution.py:118
  232.5 81.7 %grads_two.1 = (f32[2048,512]{1,0:T(8,128)}, f32[4,8,128]{2,1,0:T(8,128)}, bf16[4,3,64,512]{3,2,1,0:T(8,128)(2,1)}, bf16[2,512,512]{2,1,0:T(8,128)(2,1)}) custom-call(bf16[4,3,2048,128]{3,2,1,0:T(8,128)(2,1)} %get-tuple-element.49.refs_0_, bf16[4,3,4,512,128]{4,3,2,1,0:T(8,128)(2,1)} %get-tuple-element.50.refs_1_, ...), custom_call_target="tpu_custom_call" | custom-call | tf_op jit(solution)/shard_map/grads_two/pallas_call | solution.py:118
  314.1 31.1 %layer_one_back.1 = (bf16[512,2048]{1,0:T(8,128)(2,1)}, bf16[4,3,2048,128]{3,2,1,0:T(8,128)(2,1)}, f32[4,2048,128]{2,1,0:T(8,128)}, f32[4,4,8,128]{3,2,1,0:T(8,128)}, f32[64,6144]{1,0:T(8,128)}) custom-call(f32[4,2048,128]{2,1,0:T(8,128)} %get-tuple-element.40.refs_0_, f32[4,2048,128]{2,1,0:T(8,128)} %get-tuple-element.41.refs_1_, ...), custom_call_target="tpu_custom_call" | custom-call | tf_op jit(solution)/shard_map/layer_one_back/pallas_call | solution.py:118
  345.3 96.1 %grads_one.1 = (f32[64,6144]{1,0:T(8,128)}, f32[512,2048]{1,0:T(8,128)}, f32[16,512]{1,0:T(8,128)}) custom-call(bf16[4,3,2048,128]{3,2,1,0:T(8,128)(2,1)} %get-tuple-element.63.refs_0_, bf16[4,3,4,512,128]{4,3,2,1,0:T(8,128)(2,1)} %get-tuple-element.64.refs_1_, bf16[2048,2048]{1,0:T(8,128)(2,1)} %get-tuple-element.65.refs_2_, ...), custom_call_target="tpu_custom_call" | custom-call | tf_op jit(solution)/shard_map/grads_one/pallas_call | solution.py:118
  441.3 0.0 copy-start
  441.3 4.2 copy.16
  445.6 0.0 copy-done
  445.6 0.0 copy-start.2
  445.6 0.0 copy-start.3
  445.6 4.4 copy.17
  450.0 0.0 copy-done.2
  450.0 0.0 copy-done.3
  450.0 1.9 pad_maximum_fusion
  451.9 0.8 constant_dynamic-slice_fusion
  452.7 0.6 copy.18
  (6 shorter events, 0.0 us)
Async XLA Ops:
  0.6 5.7 %copy-start.1 = (bf16[2,256,2048]{2,1,0:T(8,128)(2,1)S(1)}, bf16[2,256,2048]{2,1,0:T(8,128)(2,1)}, u32[]{:S(2)}) copy-start(bf16[2,256,2048]{2,1,0:T(8,128)(2,1)} %param.7) | copy-start | bytes 6291460
  441.3 4.2 copy-start
  445.6 4.4 copy-start.2
  445.6 4.5 copy-start.3

commit v4 on v3

--- a/solution.py
+++ b/solution.py
@@ -403,10 +403,12 @@
             for p in n.inner_peers
         ]
 
+    def begun(self, fc):
+        for p in self.n.batch_peers:
+            arrived(self.piece(fc, p), self.r.pre_r.at[self.l, fc, p], (p, self.n.s))
+
     def start(self, fc, inner=True):
-        n, r, l, dm = self.n, self.r, self.l, self.dm
-        for p in n.batch_peers:
-            arrived(self.piece(fc, p), r.pre_r.at[l, fc, p], (p, n.s))
+        n, dm = self.n, self.dm
         pl.when(n.z < dm.outer - 1)(lambda: self.hop(fc, n.z, 1).start())
         pl.when(n.z > 0)(lambda: self.hop(fc, n.z, -1).start())
         if inner:
@@ -441,12 +443,12 @@
             for p in self.n.inner_peers:
                 sent(self.strip(fc, self.n.s), self.r.y_s.at[self.l, fc, o, p], (self.n.b, self.n.s))
 
-    def drain(self, fc, inner=True):
+    def drain_pre(self, fc):
+        for p in self.n.batch_peers:
+            sent(self.piece(fc, p), self.r.pre_s.at[self.l, fc, p], (p, self.n.s))
+
+    def drain_outer(self, fc):
         n, r, l, dm = self.n, self.r, self.l, self.dm
-        if inner:
-            self.drain_inner(fc)
-        for p in n.batch_peers:
-            sent(self.piece(fc, p), r.pre_s.at[l, fc, p], (p, n.s))
         for o in range(dm.outer):
             right = jnp.logical_and(o <= n.z, n.z < dm.outer - 1)
             left = jnp.logical_and(o >= n.z, n.z > 0)
@@ -489,6 +491,7 @@
     def w0_start(fc):
         for c in own_w[fc]:
             c.wait()
+        w0.begun(fc)
         w0.start(fc)
 
     w0_start(0)
@@ -535,7 +538,7 @@
                 r.xS[fc, every, :] = r.xg[bb, rows, pl.ds(at128(b * dm.q + fc * F), F)].astype(F32)
             return carry
 
-        lax.fori_loop(0, count // TILE, step, 0)
+        lax.fori_loop(0, count // TILE, step, 0, unroll=2)
 
     def diag_norm(k):
         arrived(r.xg.at[n.diag, pl.ds(k * XR, XR)], r.xl_r.at[k], (n.sib, s))
@@ -612,6 +615,7 @@
 
     for c in second:
         c.wait()
+    w1.begun(0)
     w1.start(0, 0 < NA)
     w0.complete(2)
     products(dm, r, n, r.wq0, (2,), 0, None)
@@ -619,6 +623,7 @@
     w1.step(0, 1, 0 < NA)
     p2(0)
     w1.step(0, 2, 0 < NA)
+    w1.begun(1)
     w1.start(1, 1 < NA)
     p2(1)
     w0.complete(3)
@@ -637,16 +642,15 @@
     for k in ("inc_out", "runA_out", "tot_out", "vec_out"):
         r.store(k)
     w1.step(1, 2, 1 < NA)
+    w1.begun(2)
     w1.start(2, 2 < NA)
     w1.step(1, 3, 1 < NA)
     h_relay(1)
     w1.step(2, 1, 2 < NA)
     w1.step(2, 2, 2 < NA)
-    w1.start(3, 3 < NA)
     w1.step(2, 3, 2 < NA)
     h_relay(2)
-    for h in range(1, outer):
-        w1.step(3, h, 3 < NA)
+    w1.begun(3)
     h_relay(3)
     for fc in range(nf):
         if fc < NA:
@@ -670,8 +674,14 @@
         x_relay(k).wait_send()
     totals_sent(dm, r, n)
     for fc in range(nf):
-        w0.drain(fc)
-        w1.drain(fc, fc < NA)
+        w0.drain_pre(fc)
+        w1.drain_pre(fc)
+        w0.drain_outer(fc)
+        w0.drain_inner(fc)
+        if fc < NA:
+            w1.drain_inner(fc)
+        if fc < nf - 1:
+            w1.drain_outer(fc)
         for sem in (r.h_s, r.hc_s, r.hl_s):
             sent(r.hb.at[fc], sem.at[fc], (b, s))
 
@@ -726,7 +736,8 @@
     for fc in range(NA):
         w_copy.append(local_copy(r.w_in.at[fc], r.wq.at[fc], r.w_sem.at[fc, 0]))
     w_late, y_sends = [], {fc: [] for fc in range(NA, nf)}
-    for fc in range(NA, nf):
+    last = nf - 1
+    for fc in range(NA, last):
         for o in range(dm.outer):
             rows = pl.ds(pl.multiple_of((o * dm.inner + n.y) * dm.rows, dm.rows), dm.rows)
             at = (fc, slice(None), slice(None), rows)
@@ -736,6 +747,9 @@
                 )
             w_late.append(local_copy(r.w_in.at[at], r.wq.at[at], r.w_sem.at[fc, o]))
 
+    rows = pl.ds(pl.multiple_of(s * dm.rows, dm.rows), dm.rows)
+    own = local_copy(r.w_in.at[last, :, :, rows], r.wq.at[last, :, :, rows], r.w_sem.at[last, 0])
+
     def cot_send(p):
         cols = pl.ds(at128(p * dm.q), dm.q)
         at = r.cot.at[pl.ds(pl.multiple_of(b * dm.local, dm.local), dm.local)]
@@ -754,6 +768,8 @@
     n.ready()
     for c in y_sends[NA]:
         c.start()
+    own.wait()
+    w1.start(last, False)
     for p in n.batch_peers:
         cot_send(p).start()
     for k in range(dm.tok // TT):
@@ -771,7 +787,9 @@
             r.rstd_out[every, :] = jnp.broadcast_to(rstd, (TILE, F))
             return carry
 
-        lax.fori_loop(0, TT // TILE, step, 0)
+        lax.fori_loop(0, TT // TILE, step, 0, unroll=2)
+        if k in (2, 4, 6):
+            w1.step(last, k // 2, False)
     normed_copy = local_copy(r.normed, r.normed_out, r.xt_sem.at[0])
     r.store("mu_out")
     r.store("rstd_out")
@@ -797,8 +815,8 @@
         pend.extend(back_outputs(dm, r, fc))
 
     p1((0, 1))
-    for fc in range(NA + 1, nf):
-        for c in y_sends[fc]:
+    for o in range(dm.outer):
+        for c in w1.to_inner(last, o):
             c.start()
     for p in n.batch_peers:
         arrived(r.cot.at[pl.ds(pl.multiple_of(p * dm.local, dm.local), dm.local)], r.c_r.at[p], (p, s))
@@ -822,6 +840,7 @@
         cot_send(p).wait_send()
     for fc in range(NA, nf):
         w1.drain_inner(fc)
+    w1.drain_outer(last)
     totals_sent(dm, r, n)
     back_sent(dm, r, n)
 
@@ -850,6 +869,7 @@
         k_s=DMA((nf, ns)), k_r=DMA((nf, ns)),
         c_s=DMA((nb,)), c_r=DMA((nb,)), w_sem=DMA((nf, dm.outer)),
         y_s=DMA((2, nf, dm.outer, dm.inner)), y_r=DMA((2, nf, dm.outer, dm.inner)),
+        z_s=DMA((2, nf, dm.outer, 2)), z_r=DMA((2, nf, dm.outer)),
         loc=DMA((2,)), xt_sem=DMA((2,)), out_sem=DMA((nf, 3)),
         **scan_scratch(dm),
     )

time: 461 us -> 457 us (level)
  Pallas kernels: 433 us -> 428 us
where the time goes in v4:
time: 457 us; the launch traced here: 449 us
  Pallas kernels  428 us (94%)
  local copies, waits for them, and re-layouts  17.5 us (4%)
    pallas_call x5, Pallas kernels, launch(): pl.pallas_call(run, out_shape=[jax.ShapeDtypeStruct(shape, dtype) for sha...  428 us

profile of v4, /device:TPU:11, one launch (start us, length us, event | category | flops | bytes accessed | tf_op | source)
XLA Modules:
  0.0 449.4 jit_solution(6293347660922549439)
XLA Ops:
  0.6 0.0 copy-start.1
  0.7 0.8 copy.14
  1.5 0.1 tile.10
  1.6 0.6 fusion.refs_2_
  2.2 4.1 copy.22
  6.3 0.0 copy-done.1
  6.3 2.5 copy.21
  8.8 139.0 %forward_one.1 = (bf16[2048,2048]{1,0:T(8,128)(2,1)}, bf16[4,3,4,512,128]{4,3,2,1,0:T(8,128)(2,1)}, bf16[4,3,4,512,128]{4,3,2,1,0:T(8,128)(2,1)}, bf16[4,4,2048,...) custom-call(bf16[512,2048]{1,0:T(8,128)(2,1)} %bitcast.23, ...), custom_call_target="tpu_custom_call" | custom-call | tf_op jit(solution)/shard_map/forward_one/pallas_call | solution.py:118
  147.7 79.4 %layer_two.1 = (bf16[4,3,4,512,128]{4,3,2,1,0:T(8,128)(2,1)}, bf16[2048,2048]{1,0:T(8,128)(2,1)}, bf16[4,2048,128]{2,1,0:T(8,128)(2,1)}, bf16[4,3,2048,128]{3,2,...) custom-call(bf16[4,3,4,512,128]{4,3,2,1,0:T(8,128)(2,1)} %get-tuple-, ...), custom_call_target="tpu_custom_call" | custom-call | tf_op jit(solution)/shard_map/layer_two/pallas_call | solution.py:118
  227.2 82.6 %grads_two.1 = (f32[2048,512]{1,0:T(8,128)}, f32[4,8,128]{2,1,0:T(8,128)}, bf16[4,3,64,512]{3,2,1,0:T(8,128)(2,1)}, bf16[2,512,512]{2,1,0:T(8,128)(2,1)}) custom-call(bf16[4,3,2048,128]{3,2,1,0:T(8,128)(2,1)} %get-tuple-element.49.refs_0_, bf16[4,3,4,512,128]{4,3,2,1,0:T(8,128)(2,1)} %get-tuple-element.50.refs_1_, ...), custom_call_target="tpu_custom_call" | custom-call | tf_op jit(solution)/shard_map/grads_two/pallas_call | solution.py:118
  309.8 31.1 %layer_one_back.1 = (bf16[512,2048]{1,0:T(8,128)(2,1)}, bf16[4,3,2048,128]{3,2,1,0:T(8,128)(2,1)}, f32[4,2048,128]{2,1,0:T(8,128)}, f32[4,4,8,128]{3,2,1,0:T(8,128)}, f32[64,6144]{1,0:T(8,128)}) custom-call(f32[4,2048,128]{2,1,0:T(8,128)} %get-tuple-element.40.refs_0_, f32[4,2048,128]{2,1,0:T(8,128)} %get-tuple-element.41.refs_1_, ...), custom_call_target="tpu_custom_call" | custom-call | tf_op jit(solution)/shard_map/layer_one_back/pallas_call | solution.py:118
  340.9 96.1 %grads_one.1 = (f32[64,6144]{1,0:T(8,128)}, f32[512,2048]{1,0:T(8,128)}, f32[16,512]{1,0:T(8,128)}) custom-call(bf16[4,3,2048,128]{3,2,1,0:T(8,128)(2,1)} %get-tuple-element.63.refs_0_, bf16[4,3,4,512,128]{4,3,2,1,0:T(8,128)(2,1)} %get-tuple-element.64.refs_1_, bf16[2048,2048]{1,0:T(8,128)(2,1)} %get-tuple-element.65.refs_2_, ...), custom_call_target="tpu_custom_call" | custom-call | tf_op jit(solution)/shard_map/grads_one/pallas_call | solution.py:118
  437.0 0.0 copy-start
  437.0 4.2 copy.16
  441.2 0.0 copy-done
  441.2 0.0 copy-start.2
  441.2 0.0 copy-start.3
  441.2 4.4 copy.17
  445.7 0.0 copy-done.2
  445.7 0.0 copy-done.3
  445.7 1.9 pad_maximum_fusion
  447.5 0.8 constant_dynamic-slice_fusion
  448.3 0.6 copy.18
  (6 shorter events, 0.0 us)
Async XLA Ops:
  0.6 5.7 %copy-start.1 = (bf16[2,256,2048]{2,1,0:T(8,128)(2,1)S(1)}, bf16[2,256,2048]{2,1,0:T(8,128)(2,1)}, u32[]{:S(2)}) copy-start(bf16[2,256,2048]{2,1,0:T(8,128)(2,1)} %param.7) | copy-start | bytes 6291460
  437.0 4.2 copy-start
  441.2 4.4 copy-start.2
  441.2 4.5 copy-start.3
